TPU v7x, 32 devices: a whole 2x2x4 slice. The times are simulated.
32 devices in a mesh: grp: 2 (over x), ch: 16 (over z, y, core).
Axes of the slice: x: 2, y: 2, z: 4, core: 2. Of those that a mesh axis runs over, the one named last changes fastest.
Arguments:
- features: bfloat16 [2048, 2048], P('ch', 'grp'), parts along dimension 1, may hold values from -50 to 50
- dw_weight: float32 [2048, 49], P('ch'), may hold values from -0.875 to 0.875
- norm_gain: float32 [2048], replicated, may hold values from 0.25 to 1.75
- layer_scale: float32 [2048], replicated, may hold values from 0.2 to 1
- w_in: bfloat16 [8192, 2048], P('ch'), may hold values from -0.125 to 0.125
- w_out: bfloat16 [8192, 2048], P('ch'), may hold values from -0.0625 to 0.0625
- w_head: bfloat16 [2048, 150], replicated, may hold values from -3 to 3
- labels: int32 [2048], P('grp'), parts along dimension 0, may hold values from 0 to 149
Outputs:
- d_features: float32 [2048, 2048], P('ch', 'grp'), parts along dimension 1
- d_dw: float32 [2048, 98], P('ch', 'grp'), parts along dimension 1
- d_scale: float32 [4096], P(('grp', 'ch')), parts along dimension 0
- d_w_in: float32 [16384, 2048], P(('grp', 'ch')), parts along dimension 0
- d_w_out: float32 [16384, 2048], P(('grp', 'ch')), parts along dimension 0
- d_head: float32 [2048, 300], P('ch', 'grp'), parts along dimension 1
- mean_loss: float32 [2], P('grp'), parts along dimension 0
There are 2 independent parts, one for each index of `grp`. A program takes and returns all parts, laid end to end along the dimension named above; an argument that names none is the same for every part. Nothing has to cross between parts.
All inputs are finite; a program needn't handle non-finite values.
Results may differ from a plain program's by a relative error of at most 0.012.
Values may be sent and summed in bfloat16 or wider, within the bound.
No kernel may reach another device: no remote copies, remote signals or barrier semaphores. Data moves between devices by JAX's collectives and lax.ppermute only.
A program may use at most 128 MiB of HBM per device.

v0:
```python
import jax
import jax.numpy as jnp
from jax import lax
from jax.sharding import PartitionSpec as P

KS = 7
WIN_H = 32
WIN_W = 32


norm_eps = 1e-06


def conv_apply(in_grid, kernel):
    half = KS // 2
    padded = jnp.pad(in_grid, ((0, 0), (half, half), (half, half)))
    running = jnp.zeros(in_grid.shape, in_grid.dtype)
    for row_shift in range(KS):
        for col_shift in range(KS):
            tap = kernel[:, row_shift * KS + col_shift]
            running = (
                running
                + tap[:, None, None]
                * padded[:, row_shift : row_shift + WIN_H, col_shift : col_shift + WIN_W]
            )
    return running


def gelu_parts(values):
    cum_prob = 0.5 * (1.0 + lax.erf(values * 0.7071067811865476))
    density = jnp.exp(-0.5 * values * values) * 0.3989422804014327
    return (values * cum_prob, cum_prob + values * density)


def per_device(features, dw_weight, norm_gain, layer_scale, w_in, w_out, w_head, labels):
    highest = lax.Precision.HIGHEST
    my_rows = features.shape[0]
    tok_count = features.shape[1]
    class_count = w_head.shape[1]
    row_offset = lax.axis_index("ch") * my_rows
    inputs_wide = features.astype(jnp.float32)
    in_grid = inputs_wide.reshape(my_rows, WIN_H, WIN_W)
    conv_out = conv_apply(in_grid, dw_weight).reshape(my_rows, tok_count).astype(jnp.bfloat16)
    conv_all = lax.all_gather(conv_out, "ch", axis=0, tiled=True)
    conv_wide = conv_all.astype(jnp.float32)
    tok_mean = jnp.mean(conv_wide, axis=0)
    centered = conv_wide - tok_mean[None, :]
    tok_var = jnp.mean(centered * centered, axis=0)
    inv_std = 1.0 / jnp.sqrt(tok_var + norm_eps)
    normed = centered * inv_std[None, :]
    norm_out = (norm_gain[:, None] * normed).astype(jnp.bfloat16)
    pre_act = jnp.dot(w_in, norm_out, preferred_element_type=jnp.float32)
    gelu_out, gelu_slope = gelu_parts(pre_act)
    hidden = gelu_out.astype(jnp.bfloat16)
    my_scale = lax.dynamic_slice_in_dim(layer_scale, row_offset, my_rows, 0)
    head_wide = w_head.astype(jnp.float32)
    my_head = lax.dynamic_slice_in_dim(head_wide, row_offset, my_rows, 0)
    w_cols = w_out
    branch_sum = lax.psum_scatter(
        lax.dot_general(
            w_cols, hidden, (((0,), (0,)), ((), ())), preferred_element_type=jnp.float32
        ),
        "ch",
        scatter_dimension=0,
        tiled=True,
    )
    block_out = inputs_wide + my_scale[:, None] * branch_sum
    part_logits = lax.dot_general(block_out, my_head, (((0,), (0,)), ((), ())), precision=highest)
    logits = lax.psum(part_logits, "ch")
    row_max = jnp.max(logits, axis=1, keepdims=True)
    exp_terms = jnp.exp(logits - row_max)
    exp_total = jnp.sum(exp_terms, axis=1, keepdims=True)
    log_total = jnp.log(exp_total) + row_max
    onehot = (labels[:, None] == jnp.arange(class_count, dtype=jnp.int32)[None, :]).astype(
        jnp.float32
    )
    picked = jnp.sum(logits * onehot, axis=1)
    mean_loss = jnp.mean(log_total[:, 0] - picked).reshape(1)
    logit_grad = exp_terms / exp_total - onehot
    out_grad = lax.dot_general(my_head, logit_grad, (((1,), (1,)), ((), ())), precision=highest)
    d_head = jnp.dot(block_out, logit_grad, precision=highest)
    d_scale = jnp.sum(out_grad * branch_sum, axis=1)
    branch_grad = (my_scale[:, None] * out_grad).astype(jnp.bfloat16)
    incoming = lax.all_gather(branch_grad, "ch", axis=0, tiled=True)
    w_cols = w_out
    hidden_acc = jnp.dot(w_cols, incoming, preferred_element_type=jnp.float32)
    tile_grad = lax.dot_general(
        hidden, incoming, (((1,), (1,)), ((), ())), preferred_element_type=jnp.float32
    )
    pre_grad = (hidden_acc * gelu_slope).astype(jnp.bfloat16)
    d_w_in = lax.dot_general(
        pre_grad, norm_out, (((1,), (1,)), ((), ())), preferred_element_type=jnp.float32
    )
    norm_grad = lax.dot_general(
        w_in, pre_grad, (((0,), (0,)), ((), ())), preferred_element_type=jnp.float32
    )
    gained = norm_gain[:, None] * norm_grad
    conv_term = (
        gained
        - jnp.mean(gained, axis=0)[None, :]
        - normed * jnp.mean(gained * normed, axis=0)[None, :]
    ) * inv_std[None, :]
    conv_grad = lax.psum_scatter(conv_term, "ch", scatter_dimension=0, tiled=True)
    unused, pullback = jax.vjp(conv_apply, in_grid, dw_weight)
    grid_grad, d_dw = pullback(conv_grad.reshape(my_rows, WIN_H, WIN_W))
    d_features = out_grad + grid_grad.reshape(my_rows, tok_count)
    return (d_features, d_dw, d_scale, d_w_in, tile_grad, d_head, mean_loss)


def solution(mesh):
    placed = (P("ch", "grp"), P("ch", None), P(), P(), P("ch", None), P("ch", None), P(), P("grp"))
    return jax.shard_map(
        per_device,
        mesh=mesh,
        in_specs=placed,
        out_specs=(
            P("ch", "grp"),
            P("ch", "grp"),
            P(("grp", "ch")),
            P(("grp", "ch"), None),
            P(("grp", "ch"), None),
            P("ch", "grp"),
            P("grp"),
        ),
        check_vma=False,
    )
```

profile of v0, /device:TPU:0, one launch (start us, length us, event | category | flops | bytes accessed | tf_op | source)
XLA Modules:
  0.0 497.7 jit_solution(14007070145774544614)
XLA Ops:
  10.4 1.1 copy.19
  11.6 4.8 add_convert_fusion
  16.5 56.0 %all-gather.3.cloned.1.call-done = bf16[2048,1024]{0,1:T(8,128)(2,1)} async-done(((bf16[128,1024]{0,1:T(8,128)(2,1)}), bf16[2048,1024]{0,1:T(8,128)(2,1)}) %all-gather.3.cloned.1.call-update) | async-done | bytes 4194320 | tf_op jit(solution)/shard_map/all_gather | solution.py:44
  72.5 3.0 convert_reduce_fusion
  75.9 1.2 fusion.9
  77.3 1.6 fusion.5
  79.0 2.4 fusion.31
  81.4 1.3 copy-done.7
  82.7 5.6 %convolution_bitcast_fusion = f32[2048,1024]{0,1:T(8,128)} fusion(bf16[512,2048]{1,0:T(8,128)(2,1)S(1)} %copy-done.45, f32[1024,512]{1,0:T(8,128)S(1)} %fusion.31), kind=kOutput, calls=%fused_computation.62 | convolution fusion | flops 2150105088 | bytes 12582912 | tf_op jit(solution)/shard_map/dot_general | solution.py:60
  89.2 102.4 %reduce-scatter.3.cloned.1.call-done = f32[128,1024]{0,1:T(8,128)} async-done(((f32[2048,1024]{0,1:T(8,128)}), f32[128,1024]{0,1:T(8,128)}) %reduce-scatter.3.cloned.1.call-update) | async-done | bytes 524304 | tf_op jit(solution)/shard_map/reduce_scatter | solution.py:59
  191.5 2.6 fusion.22
  194.2 91.7 %all-reduce.101.cloned.1.call-done = f32[1024,150]{0,1:T(8,128)} async-done(((f32[1024,150]{0,1:T(8,128)}), f32[1024,150]{0,1:T(8,128)}) %all-reduce.101.cloned.1.call-update) | async-done | bytes 614416 | tf_op jit(solution)/shard_map/psum | solution.py:69
  285.9 1.1 reduce_max.9
  287.0 1.2 select_reduce_fusion
  288.2 1.7 fusion.23
  290.9 2.5 multiply_reduce_fusion.1
  293.7 53.5 %all-gather.5.cloned.1.call-done = bf16[2048,1024]{0,1:T(8,128)(2,1)} async-done(((bf16[128,1024]{0,1:T(8,128)(2,1)}), bf16[2048,1024]{0,1:T(8,128)(2,1)}) %all-gather.5.cloned.1.call-update) | async-done | bytes 4194320 | tf_op jit(solution)/shard_map/all_gather | solution.py:84
  347.2 6.5 %fusion.15 = bf16[512,1024]{0,1:T(8,128)(2,1)S(1)} fusion(f32[1024,512]{1,0:T(8,128)} %copy-done.7, bf16[2048,1024]{0,1:T(8,128)(2,1)} %all-gather.5.cloned.1.call-done, bf16[512,2048]{1,0:T(8,128)(2,1)} %param.13), kind=kOutput, calls=%fused_computation.69 | convolution fusion | flops 2152726528 | bytes 9437184 | tf_op jit(solution)/shard_map/dot_general | solution.py:86
  353.7 3.0 fusion.6
  357.3 5.4 %fusion.8 = f32[2048,1024]{0,1:T(8,128)} fusion(bf16[2048,1024]{0,1:T(8,128)(2,1)S(1)} %copy-done.3, f32[1024,2048]{1,0:T(8,128)S(1)} %get-tuple-element.158, f32[1024]{0:T(1024)S(1)} %get-tuple-element.159, f32[1024]{0:T(1024)S(1)} %get-tuple-element.160, f32[2048]{0:T(1024)S(1)} %copy-done.13, f32[1024]{0:T(1024)S(1)} %add_rsqrt_fusion, ...), kind=kLoop, calls=%fused_computation.10 | loop fusion | flops 16777216 | bytes 20996096 | tf_op jit(solution)/shard_map/mul | solution.py:98
  364.1 1.5 fusion.21
  365.6 7.4 %fusion.32 = f32[512,2048]{1,0:T(8,128)} fusion(bf16[512,1024]{0,1:T(8,128)(2,1)} %copy-done.10, bf16[2048,1024]{0,1:T(8,128)(2,1)} %copy-done.4), kind=kOutput, calls=%fused_computation.255 | convolution fusion | flops 2147483648 | bytes 9437184 | tf_op jit(solution)/shard_map/dot_general | solution.py:91
  372.9 4.5 fusion.28
  377.5 88.5 %reduce-scatter.5.cloned.1.call-done = f32[128,1024]{0,1:T(8,128)} async-done(((f32[2048,1024]{0,1:T(8,128)}), f32[128,1024]{0,1:T(8,128)}) %reduce-scatter.5.cloned.1.call-update) | async-done | bytes 524304 | tf_op jit(solution)/shard_map/reduce_scatter | solution.py:103
  465.9 2.9 broadcast_multiply_fusion.2
  470.0 2.4 broadcast_multiply_fusion
  472.4 6.0 %pad_add_fusion = f32[128,38,38]{0,2,1:T(8,128)S(1)} fusion(f32[128,32,32]{0,2,1:T(8,128)S(1)} %get-tuple-element.66, f32[128,32,32]{0,2,1:T(8,128)S(1)} %get-tuple-element.67, f32[128,32,32]{0,2,1:T(8,128)S(1)} %get-tuple-element.68, f32[128,32,32]{0,2,1:T(8,128)S(1)} %get-tuple-element.69, f32[128,32,32]{0,2,1:T(8,128)S(1)} %get-tuple-element.70, ...), kind=kLoop, calls=%fused_computation.76 | loop fusion | flops 7762944 | bytes 23283712 | tf_op jit(solution)/shard_map/transpose(jvp())/add_any | solution.py:24
  478.4 3.1 pad_add_fusion.1
  481.5 2.1 copy.21
  483.5 2.1 add.438
  486.4 1.4 multiply_reduce_fusion.49
  487.8 1.4 multiply_reduce_fusion.50
  (116 shorter events, 9.8 us)
Async XLA Ops:
  7.2 71.8 %copy-start = (bf16[512,2048]{1,0:T(8,128)(2,1)S(1)}, bf16[512,2048]{1,0:T(8,128)(2,1)}, u32[]{:S(2)}) copy-start(bf16[512,2048]{1,0:T(8,128)(2,1)} %param.12) | copy-start | bytes 6291460
  7.2 65.3 %all-gather.3.cloned.1.call-start = ((), (), s32[]{:S(2)}) async-start(), calls=%async_computation.2 | async-start | bytes 4456448 | tf_op jit(solution)/shard_map/all_gather | solution.py:44
  9.2 67.9 %copy-start.29 = (f32[128]{0:T(128)}, f32[128]{0:T(128)S(1)}, u32[]{:S(2)}) copy-start(f32[128]{0:T(128)S(1)} %get-tuple-element.110) | copy-start | bytes 1540
  9.2 67.9 %copy-start.30 = (f32[128]{0:T(128)}, f32[128]{0:T(128)S(1)}, u32[]{:S(2)}) copy-start(f32[128]{0:T(128)S(1)} %get-tuple-element.111) | copy-start | bytes 1540
  9.2 67.9 %copy-start.31 = (f32[128]{0:T(128)}, f32[128]{0:T(128)S(1)}, u32[]{:S(2)}) copy-start(f32[128]{0:T(128)S(1)} %get-tuple-element.112) | copy-start | bytes 1540
  9.2 67.9 %copy-start.32 = (f32[128]{0:T(128)}, f32[128]{0:T(128)S(1)}, u32[]{:S(2)}) copy-start(f32[128]{0:T(128)S(1)} %get-tuple-element.113) | copy-start | bytes 1540
  9.3 67.9 %copy-start.33 = (f32[128]{0:T(128)}, f32[128]{0:T(128)S(1)}, u32[]{:S(2)}) copy-start(f32[128]{0:T(128)S(1)} %get-tuple-element.114) | copy-start | bytes 1540
  9.3 67.9 %copy-start.34 = (f32[128]{0:T(128)}, f32[128]{0:T(128)S(1)}, u32[]{:S(2)}) copy-start(f32[128]{0:T(128)S(1)} %get-tuple-element.115) | copy-start | bytes 1540
  9.3 67.9 %copy-start.35 = (f32[128]{0:T(128)}, f32[128]{0:T(128)S(1)}, u32[]{:S(2)}) copy-start(f32[128]{0:T(128)S(1)} %get-tuple-element.116) | copy-start | bytes 1540
  9.3 67.9 %copy-start.36 = (f32[128]{0:T(128)}, f32[128]{0:T(128)S(1)}, u32[]{:S(2)}) copy-start(f32[128]{0:T(128)S(1)} %get-tuple-element.117) | copy-start | bytes 1540
  9.3 67.9 %copy-start.37 = (f32[128]{0:T(128)}, f32[128]{0:T(128)S(1)}, u32[]{:S(2)}) copy-start(f32[128]{0:T(128)S(1)} %get-tuple-element.118) | copy-start | bytes 1540
  9.3 67.9 %copy-start.38 = (f32[128]{0:T(128)}, f32[128]{0:T(128)S(1)}, u32[]{:S(2)}) copy-start(f32[128]{0:T(128)S(1)} %get-tuple-element.119) | copy-start | bytes 1540
  9.3 67.9 %copy-start.39 = (f32[128]{0:T(128)}, f32[128]{0:T(128)S(1)}, u32[]{:S(2)}) copy-start(f32[128]{0:T(128)S(1)} %get-tuple-element.120) | copy-start | bytes 1540
  9.3 67.9 %copy-start.40 = (f32[128]{0:T(128)}, f32[128]{0:T(128)S(1)}, u32[]{:S(2)}) copy-start(f32[128]{0:T(128)S(1)} %get-tuple-element.121) | copy-start | bytes 1540
  10.4 65.1 %copy-start.20 = (f32[128]{0:T(128)}, f32[128]{0:T(128)S(1)}, u32[]{:S(2)}) copy-start(f32[128]{0:T(128)S(1)} %get-tuple-element.136) | copy-start | bytes 1540
  10.4 65.1 %copy-start.22 = (f32[128]{0:T(128)}, f32[128]{0:T(128)S(1)}, u32[]{:S(2)}) copy-start(f32[128]{0:T(128)S(1)} %get-tuple-element.137) | copy-start | bytes 1540
  10.4 66.9 %copy-start.24 = (f32[128]{0:T(128)}, f32[128]{0:T(128)S(1)}, u32[]{:S(2)}) copy-start(f32[128]{0:T(128)S(1)} %get-tuple-element.138) | copy-start | bytes 1540
  10.4 66.9 %copy-start.26 = (f32[128]{0:T(128)}, f32[128]{0:T(128)S(1)}, u32[]{:S(2)}) copy-start(f32[128]{0:T(128)S(1)} %get-tuple-element.139) | copy-start | bytes 1540
  16.4 175.1 %reduce-scatter.3.cloned.1.call-start = ((), (), s32[]{:S(2)}) async-start(), calls=%async_computation.3 | async-start | bytes 8912896 | tf_op jit(solution)/shard_map/reduce_scatter | solution.py:59
  88.3 198.7 %copy-start.41 = (s32[1024]{0:T(1024)S(1)}, s32[1024]{0:T(1024)}, u32[]{:S(2)}) copy-start(s32[1024]{0:T(1024)} %param.15) | copy-start | bytes 12292
  88.4 197.5 %all-reduce.101.cloned.1.call-start = ((), (), s32[]{:S(2)}) async-start(), calls=%async_computation.4 | async-start | bytes 1245184 | tf_op jit(solution)/shard_map/psum | solution.py:69
  89.2 105.0 %copy-start.43 = (f32[128]{0:T(128)}, f32[128]{0:T(128)S(1)}, u32[]{:S(2)}) copy-start(f32[128]{0:T(128)S(1)} %dynamic_slice.7) | copy-start | bytes 1540
  194.1 153.1 %all-gather.5.cloned.1.call-start = ((), (), s32[]{:S(2)}) async-start(), calls=%async_computation.5 | async-start | bytes 4456448 | tf_op jit(solution)/shard_map/all_gather | solution.py:84
  289.9 63.7 %copy-start.11 = (f32[128,1024]{1,0:T(8,128)}, f32[128,1024]{1,0:T(8,128)S(1)}, u32[]{:S(2)}) copy-start(f32[128,1024]{1,0:T(8,128)S(1)} %fusion.23) | copy-start | bytes 1572868
  293.4 172.5 %reduce-scatter.5.cloned.1.call-start = ((), (), s32[]{:S(2)}) async-start(), calls=%async_computation.6 | async-start | bytes 8912896 | tf_op jit(solution)/shard_map/reduce_scatter | solution.py:103
  377.4 91.4 %copy-start.15 = (f32[128]{0:T(128)S(1)}, f32[128]{0:T(128)}, u32[]{:S(2)}) copy-start(f32[128]{0:T(128)} %copy-done.14) | copy-start | bytes 1540
  377.4 91.4 %copy-start.17 = (f32[128]{0:T(128)S(1)}, f32[128]{0:T(128)}, u32[]{:S(2)}) copy-start(f32[128]{0:T(128)} %copy-done.16) | copy-start | bytes 1540
  377.4 91.4 %copy-start.19 = (f32[128]{0:T(128)S(1)}, f32[128]{0:T(128)}, u32[]{:S(2)}) copy-start(f32[128]{0:T(128)} %copy-done.18) | copy-start | bytes 1540
  377.5 91.4 %copy-start.21 = (f32[128]{0:T(128)S(1)}, f32[128]{0:T(128)}, u32[]{:S(2)}) copy-start(f32[128]{0:T(128)} %copy-done.20) | copy-start | bytes 1540
  377.5 91.4 %copy-start.23 = (f32[128]{0:T(128)S(1)}, f32[128]{0:T(128)}, u32[]{:S(2)}) copy-start(f32[128]{0:T(128)} %copy-done.22) | copy-start | bytes 1540
  377.5 91.4 %copy-start.25 = (f32[128]{0:T(128)S(1)}, f32[128]{0:T(128)}, u32[]{:S(2)}) copy-start(f32[128]{0:T(128)} %copy-done.24) | copy-start | bytes 1540
  377.5 91.4 %copy-start.27 = (f32[128]{0:T(128)S(1)}, f32[128]{0:T(128)}, u32[]{:S(2)}) copy-start(f32[128]{0:T(128)} %copy-done.26) | copy-start | bytes 1540
  (19 other events, 197.3 us)
Sparse Core Ops, SparseCore 0:
  16.5 55.9 all-gather.2
  88.5 103.0 reduce-scatter.2
  195.5 90.2 all-reduce.100
  293.5 53.5 all-gather.4
  362.9 102.9 reduce-scatter.4
where the time goes:
time: 498 us
  waiting for transfers between devices  392 us (79%)
  other arithmetic  44 us (9%)
  matrix products  35 us (7%)
  between operations  16.2 us (3%)
  local copies, waits for them, and re-layouts  9.9 us (2%)
    reduce_scatter x1, waiting for transfers between devices, per_device(): lax.psum_scatter(lax.dot_general(w_cols, hidden, (((0,), (0,)), ((), ()))...  102 us
    psum x1, waiting for transfers between devices, per_device(): logits = lax.psum(part_logits, 'ch')  91.7 us
    reduce_scatter x1, waiting for transfers between devices, per_device(): lax.psum_scatter(conv_term, 'ch', scatter_dimension=0, tiled=True)  88.5 us
    all_gather x1, waiting for transfers between devices, per_device(): conv_all = lax.all_gather(conv_out, 'ch', axis=0, tiled=True)  56 us
    all_gather x1, waiting for transfers between devices, per_device(): incoming = lax.all_gather(branch_grad, 'ch', axis=0, tiled=True)  53.5 us
  transfers between devices with their start and end apart: 5, of which 5 were waited for; matrix products, arithmetic and copies ran while one was open for 3% of the time, Pallas kernels for 0%

commit v1 on v0

--- a/solution.py
+++ b/solution.py
@@ -1,14 +1,421 @@
+import functools
+
 import jax
 import jax.numpy as jnp
+import numpy as np
 from jax import lax
+from jax.experimental import pallas as pl
+from jax.experimental.pallas import tpu as pltpu
 from jax.sharding import PartitionSpec as P
 
 KS = 7
+HALF = KS // 2
 WIN_H = 32
 WIN_W = 32
-
-
 norm_eps = 1e-06
+BF = jnp.bfloat16
+F32 = jnp.float32
+
+WALK = (0, 2, 4, 6, 7, 5, 3, 1)
+CHIPS = len(WALK)
+REL = np.array([[WALK[(WALK.index(chip) + d) % CHIPS] for d in range(CHIPS)] for chip in range(CHIPS)], np.int32)
+CLASS_ROWS = 160
+EXTRA = 24
+LANE = 128
+
+
+def walk_perm(step):
+    return [
+        (WALK[p] * 2 + c, WALK[(p + step) % CHIPS] * 2 + c) for p in range(CHIPS) for c in range(2)
+    ]
+
+
+def flip_perm(bit):
+    return [(i, i ^ bit) for i in range(2 * CHIPS)]
+
+
+def send(value, perm):
+    return lax.ppermute(value, "ch", perm)
+
+
+FORTH, BACK, SIBLING = walk_perm(1), walk_perm(-1), flip_perm(1)
+VMEM = pl.BlockSpec(memory_space=pltpu.VMEM)
+SMEM = pl.BlockSpec(memory_space=pltpu.SMEM)
+
+
+def call(kernel, outs, ins, scratch=(), flops=0, moved=0, limit=40, name=None):
+    result = pl.pallas_call(
+        kernel,
+        out_shape=[jax.ShapeDtypeStruct(s, d) for s, d in outs],
+        in_specs=[s for _, s in ins],
+        out_specs=[VMEM] * len(outs),
+        scratch_shapes=list(scratch),
+        compiler_params=pltpu.CompilerParams(vmem_limit_bytes=limit << 20),
+        cost_estimate=pl.CostEstimate(flops=int(flops), bytes_accessed=int(moved), transcendentals=0),
+        name=name,
+    )(*[a for a, _ in ins])
+    return result
+
+
+def dot(a, b, dims):
+    return lax.dot_general(a, b, (dims, ((), ())), preferred_element_type=F32)
+
+
+def shifted_copies(grid_pad, copies):
+    for j in range(KS):
+        copies[j] = grid_pad[:, pl.ds(8 + j - HALF, WIN_W), :]
+
+
+def clear_border(grid_pad):
+    grid_pad[...] = jnp.zeros_like(grid_pad)
+
+
+def put_rows(grid_pad, row, tile):
+    grid_pad[pl.ds(row + HALF, 4), pl.ds(8, WIN_W), :] = tile.T.reshape(4, WIN_W, tile.shape[0])
+
+
+def put_taps(weight, taps):
+    square = jnp.concatenate([weight, jnp.zeros((weight.shape[0], LANE - KS * KS), F32)], axis=1)
+    taps[...] = square.T
+
+
+def conv_rows(copies, taps, row, flip):
+    acc = None
+    for j in range(KS):
+        for i in range(KS):
+            index = (KS - 1 - i) * KS + KS - 1 - j if flip else i * KS + j
+            term = taps[index : index + 1, :][None] * copies[j, pl.ds(row + i, 4)]
+            acc = term if acc is None else acc + term
+    return acc
+
+
+def conv_kernel(x_ref, w_ref, out_ref, grid_pad, copies, taps):
+    clear_border(grid_pad)
+    put_taps(w_ref[...], taps)
+    for g in range(8):
+        put_rows(grid_pad, 4 * g, x_ref[:, g * LANE : (g + 1) * LANE].astype(F32))
+    shifted_copies(grid_pad, copies)
+
+    for g in range(8):
+        acc = conv_rows(copies, taps, 4 * g, False)
+        out_ref[:, g * LANE : (g + 1) * LANE] = acc.reshape(LANE, LANE).T.astype(BF)
+
+
+def weights_kernel(w_in_ref, gain_ref, w_out_ref, scale_ref, head_ref, w_gain_ref, w_gain_t_ref, gain_sum_ref, mix_ref):
+    w_gain = (w_in_ref[...].astype(F32) * gain_ref[...]).astype(BF)
+    w_gain_ref[...] = w_gain
+    w_gain_t_ref[...] = w_gain.T
+    gain_sum_ref[...] = jnp.sum(w_gain.astype(F32), axis=1, keepdims=True)
+    scaled = (head_ref[...].astype(F32) * scale_ref[...]).astype(BF)
+    mix_ref[...] = dot(w_out_ref[...], scaled, ((1,), (0,))).astype(BF)
+
+
+def add_blocks(offs_ref, w_gain_ref, blocks, ids, shift, acc, sums):
+    for n, (own, sib) in enumerate(blocks):
+        left = w_gain_ref[:, pl.ds(pl.multiple_of(offs_ref[2 * ids[n]], LANE), LANE)]
+        right = w_gain_ref[:, pl.ds(pl.multiple_of(offs_ref[2 * ids[n] + 1], LANE), LANE)]
+        pair = jnp.concatenate([own[...], sib[...]], axis=0)
+        term = dot(jnp.concatenate([left, right], axis=1), pair, ((1,), (0,)))
+        acc = term if acc is None else acc + term
+        away = pair.astype(F32) - shift
+        first = jnp.sum(away, axis=0, keepdims=True)
+        second = jnp.sum(away * away, axis=0, keepdims=True)
+        sums = (first, second) if sums is None else (sums[0] + first, sums[1] + second)
+    return acc, sums
+
+
+def early_kernel(ids, offs_ref, w_gain_ref, *refs):
+    blocks, (acc_ref, sums_ref) = refs[:-2], refs[-2:]
+    blocks = [(blocks[2 * n], blocks[2 * n + 1]) for n in range(len(ids))]
+    shift = jnp.mean(blocks[0][0][...].astype(F32), axis=0, keepdims=True)
+    acc, (first, second) = add_blocks(offs_ref, w_gain_ref, blocks, ids, shift, None, None)
+    acc_ref[...] = acc
+    sums_ref[...] = jnp.concatenate([shift, first, second, jnp.zeros((5, shift.shape[1]), F32)], axis=0)
+
+
+def forward_kernel(ids, classes, offs_ref, w_gain_ref, acc_ref, sums_ref, gain_sum_ref, mix_ref, head_ref, x_ref, *refs):
+    blocks, (pre_ref, hidden_ref, stats_ref, logits_ref) = refs[:-4], refs[-4:]
+    blocks = [(blocks[2 * n], blocks[2 * n + 1]) for n in range(len(ids))]
+    shift, first, second = sums_ref[0:1, :], sums_ref[1:2, :], sums_ref[2:3, :]
+    acc, (first, second) = add_blocks(offs_ref, w_gain_ref, blocks, ids, shift, acc_ref[...], (first, second))
+    channels = w_gain_ref.shape[1]
+    away = first / channels
+    tok_mean = shift + away
+    inv_std = lax.rsqrt(second / channels - away * away + norm_eps)
+    stats_ref[...] = jnp.concatenate([tok_mean, inv_std, jnp.zeros((6, shift.shape[1]), F32)], axis=0)
+    pre_act = (acc - gain_sum_ref[...] * tok_mean) * inv_std
+    pre_ref[...] = pre_act
+    hidden = (pre_act * (0.5 * (1.0 + lax.erf(pre_act * 0.7071067811865476)))).astype(BF)
+    hidden_ref[...] = hidden
+    logits = dot(mix_ref[...], hidden, ((0,), (0,))) + dot(head_ref[...], x_ref[...], ((0,), (0,)))
+    core = offs_ref[2 * CHIPS]
+    chunks = logits_ref.shape[1]
+    for g in range(2 * chunks):
+        logits_ref[(g // chunks) ^ core, g % chunks] = logits[:, g * LANE : (g + 1) * LANE]
+
+
+def slope_kernel(pre_ref, stats_ref, slope_ref):
+    pre_act = pre_ref[...]
+    cum_prob = 0.5 * (1.0 + lax.erf(pre_act * 0.7071067811865476))
+    density = jnp.exp(-0.5 * pre_act * pre_act) * 0.3989422804014327
+    slope_ref[...] = (cum_prob + pre_act * density) * stats_ref[1:2, :]
+
+
+def grad_kernel(offs_ref, own_ref, sib_ref, mix_ref, slope_ref, pre_ref, gain_sum_ref, hidden_ref, grad_ref, scaled_ref, means_ref, mixed_ref):
+    core = offs_ref[2 * CHIPS]
+    chunks = own_ref.shape[0]
+    for g in range(chunks):
+        grad_ref[:, pl.ds(pl.multiple_of((core * chunks + g) * LANE, LANE), LANE)] = own_ref[g]
+        grad_ref[:, pl.ds(pl.multiple_of(((1 - core) * chunks + g) * LANE, LANE), LANE)] = sib_ref[g]
+    grad = grad_ref[...]
+    scaled = (dot(mix_ref[...], grad, ((1,), (0,))) * slope_ref[...]).astype(BF)
+    scaled_ref[...] = scaled
+    wide = scaled.astype(F32)
+    mean_part = jnp.sum(wide * gain_sum_ref[...], axis=0, keepdims=True)
+    proj_part = jnp.sum(wide * pre_ref[...], axis=0, keepdims=True)
+    rows = [part[:, g * LANE : (g + 1) * LANE] for part in (mean_part, proj_part) for g in range(8)]
+    means_ref[...] = jnp.concatenate(rows + [jnp.zeros((EXTRA - 16, LANE), F32)], axis=0)
+    mixed_ref[...] = dot(hidden_ref[...], grad, ((1,), (1,))).astype(BF)
+
+
+def message_kernel(ids, offs_ref, w_gain_t_ref, scaled_ref, w_out_ref, mixed_ref, means_ref, *outs):
+    scaled = scaled_ref[...]
+    for n, d in enumerate(ids):
+        for side in range(2):
+            off = pl.multiple_of(offs_ref[2 * d + side], LANE)
+            rows = dot(w_gain_t_ref[pl.ds(off, LANE), :], scaled, ((1,), (0,)))
+            branch = dot(mixed_ref[...], w_out_ref[:, pl.ds(off, LANE)], ((0,), (0,)))
+            branch = jnp.concatenate([branch, jnp.zeros((7 * EXTRA - CLASS_ROWS, LANE), F32)], axis=0)
+            extra = jnp.concatenate([branch[g * EXTRA : (g + 1) * EXTRA] for g in range(7)] + [means_ref[...]], axis=1)
+            message = jnp.concatenate([rows, extra], axis=0)
+            out = outs[2 * n + side]
+            out[...] = message.astype(out.dtype)
+
+
+def d_w_out_kernel(mixed_ref, head_ref, scale_ref, out_ref):
+    out_ref[...] = dot(mixed_ref[...], head_ref[...], ((1,), (1,))) * scale_ref[...]
+
+
+def d_w_in_kernel(offs_ref, scaled_ref, stats_ref, gain_ref, *refs):
+    blocks, out_ref = refs[:-1], refs[-1]
+    scaled = scaled_ref[...]
+    shift = jnp.sum(scaled.astype(F32) * stats_ref[0:1, :], axis=1, keepdims=True)
+    for d in range(CHIPS):
+        pair = jnp.concatenate([blocks[2 * d][...], blocks[2 * d + 1][...]], axis=0)
+        both = dot(scaled, pair, ((1,), (1,))) - shift
+        for side in range(2):
+            at = pl.ds(pl.multiple_of(offs_ref[2 * d + side], LANE), LANE)
+            out_ref[:, at] = both[:, side * LANE : (side + 1) * LANE] * gain_ref[:, at]
+
+
+def last_kernel(classes, mine_ref, forth_ref, back_ref, x_ref, conv_ref, stats_ref, w_ref, head_ref, scale_ref, grad_ref,
+                d_x_ref, d_dw_ref, d_scale_ref, d_head_ref, grid_pad, copies, taps, copies_x, sums):
+    rows, tokens = x_ref.shape
+    channels = rows * 2 * CHIPS
+    got = mine_ref[...].astype(F32) + forth_ref[...].astype(F32) + back_ref[...].astype(F32)
+    extra = got[rows:]
+    branch = jnp.concatenate([extra[:, g * LANE : (g + 1) * LANE] for g in range(7)], axis=0)[:CLASS_ROWS]
+    means = extra[:, 7 * LANE :]
+    tok_mean, inv_std = stats_ref[0:1, :], stats_ref[1:2, :]
+    put_taps(w_ref[...], taps)
+    clear_border(grid_pad)
+    for g in range(8):
+        put_rows(grid_pad, 4 * g, x_ref[:, g * LANE : (g + 1) * LANE].astype(F32))
+    shifted_copies(grid_pad, copies_x)
+    for g in range(8):
+        at = slice(g * LANE, (g + 1) * LANE)
+        normed = (conv_ref[:, at].astype(F32) - tok_mean[:, at]) * inv_std[:, at]
+        conv_grad = got[:rows, at] - (means[g : g + 1, :] + normed * means[8 + g : 9 + g, :]) * (1.0 / channels)
+        put_rows(grid_pad, 4 * g, conv_grad)
+    shifted_copies(grid_pad, copies)
+    out_grad = dot(head_ref[...], grad_ref[...], ((1,), (0,)))
+    for g in range(8):
+        at = slice(g * LANE, (g + 1) * LANE)
+        d_x_ref[:, at] = out_grad[:, at] + conv_rows(copies, taps, 4 * g, True).reshape(LANE, LANE).T
+        conv_grad = copies[HALF, pl.ds(4 * g + HALF, 4)]
+        for j in range(KS):
+            for i in range(KS):
+                prod = (conv_grad * copies_x[j, pl.ds(4 * g + i, 4)]).reshape(16, 8, LANE)
+                total = jnp.sum(prod, axis=0)
+                index = i * KS + j
+                if g == 0:
+                    sums[index] = total
+                else:
+                    sums[index] += total
+    d_taps = jnp.sum(sums[...], axis=1)
+    d_taps = jnp.concatenate([d_taps, jnp.zeros((LANE - KS * KS, rows), F32)], axis=0).T
+    d_dw_ref[...] = d_taps[:, : KS * KS]
+    branch = jnp.concatenate([branch, jnp.zeros((2 * LANE - CLASS_ROWS, rows), F32)], axis=0).T
+    branch = branch[:, :CLASS_ROWS]
+    d_scale_ref[...] = jnp.sum(head_ref[...].astype(F32) * branch, axis=1, keepdims=True)
+    d_head = dot(x_ref[...], grad_ref[...], ((1,), (1,))) + scale_ref[...] * branch
+    d_head_ref[...] = d_head[:, :classes]
+
+
+def gather_walk(block):
+    half = block.shape[0] // 2
+    mine = [None] * CHIPS
+    mine[0] = forth = back = block
+    for step in range(1, CHIPS // 2):
+        forth, back = send(forth, FORTH), send(back, BACK)
+        mine[(-step) % CHIPS], mine[step] = forth, back
+    upper, lower = send(forth[:half], FORTH), send(back[half:], BACK)
+    mine[CHIPS // 2] = jnp.concatenate([upper, lower], axis=0)
+    return [(b, send(b, SIBLING)) for b in mine]
+
+
+def sum_kernel(widths, *refs):
+    for n, at in enumerate(widths):
+        own, sib, arrived, out = refs[n], refs[len(widths) + n], refs[2 * len(widths) + n], refs[3 * len(widths) + n]
+        total = own[...] + sib[...].astype(F32)
+        more = arrived[...].astype(F32)
+        if at > 0:
+            total = jnp.concatenate([total[:at] + more, total[at:]], axis=0) if more.shape[0] < total.shape[0] else total + more
+        elif at < 0:
+            total = jnp.concatenate([total[:at], total[at:] + more], axis=0)
+        else:
+            total = total + more
+        out[...] = total.astype(BF)
+
+
+def far_kernel(own, sib, upper, lower):
+    total = own[...] + sib[...].astype(F32)
+    cut = upper.shape[0]
+    upper[...] = total[:cut].astype(BF)
+    lower[...] = total[cut:].astype(BF)
+
+
+def scatter_walk(own, sib):
+    height, width = own[0].shape
+    cut = 80
+    forth, back = call(far_kernel, [((cut, width), BF), ((height - cut, width), BF)], [(own[CHIPS // 2], VMEM), (sib[CHIPS // 2], VMEM)], name="far_sum")
+    forth, back = send(forth, FORTH), send(back, BACK)
+    for step in range(CHIPS // 2 - 1, 0, -1):
+        ends = (cut, cut - height) if step == CHIPS // 2 - 1 else (0, 0)
+        other = (-step) % CHIPS
+        forth, back = call(
+            functools.partial(sum_kernel, ends),
+            [((height, width), BF)] * 2,
+            [(a, VMEM) for a in (own[step], own[other], sib[step], sib[other], forth, back)],
+            name="walk_sum",
+        )
+        forth, back = send(forth, FORTH), send(back, BACK)
+    return forth, back
+
+
+def per_device(features, dw_weight, norm_gain, layer_scale, w_in, w_out, w_head, labels):
+    rows, tokens = features.shape
+    hidden_units, channels = w_in.shape
+    classes = w_head.shape[1]
+    chunks = tokens // LANE // 2
+    me = lax.axis_index("ch")
+    core = me % 2
+    rel_chip = jnp.asarray(REL)[me // 2]
+    offs = jnp.stack([rel_chip * 2 + core, rel_chip * 2 + 1 - core], 1).reshape(-1) * rows
+    offs = jnp.concatenate([offs, core[None]]).astype(jnp.int32)
+    my_scale = lax.dynamic_slice_in_dim(layer_scale, me * rows, rows, 0)[:, None]
+    head_pad = jnp.pad(w_head, ((0, 0), (0, CLASS_ROWS - classes)))
+    my_head = lax.dynamic_slice_in_dim(head_pad, me * rows, rows, 0)
+    grid_shape = pltpu.VMEM((WIN_H + 2 * HALF, WIN_W + 16, LANE), F32)
+    copies_shape = pltpu.VMEM((KS, WIN_H + 2 * HALF, WIN_W, LANE), F32)
+    taps_shape = pltpu.VMEM((LANE, LANE), F32)
+
+    (conv_out,) = call(
+        conv_kernel, [((rows, tokens), BF)], [(features, VMEM), (dw_weight, VMEM)],
+        [grid_shape, copies_shape, taps_shape], name="conv_forward",
+    )
+    pairs = gather_walk(conv_out)
+    w_gain, w_gain_t, gain_sum, mix = call(
+        weights_kernel,
+        [((hidden_units, channels), BF), ((channels, hidden_units), BF), ((hidden_units, 1), F32), ((hidden_units, CLASS_ROWS), BF)],
+        [(w_in, VMEM), (norm_gain[None, :], VMEM), (w_out, VMEM), (layer_scale[:, None], VMEM), (head_pad, VMEM)],
+        flops=4e9, moved=16e6, name="weights_ready",
+    )
+    early, late = (0, 1, 7, 2, 6), (3, 5, 4)
+    acc, sums = call(
+        functools.partial(early_kernel, early),
+        [((hidden_units, tokens), F32), ((8, tokens), F32)],
+        [(offs, SMEM), (w_gain, VMEM)] + [(b, VMEM) for d in early for b in pairs[d]],
+        flops=2e9, moved=8e6, name="forward_early",
+    )
+    pre_act, hidden, stats, logits = call(
+        functools.partial(forward_kernel, late, classes),
+        [((hidden_units, tokens), F32), ((hidden_units, tokens), BF), ((8, tokens), F32), ((2, chunks, CLASS_ROWS, LANE), F32)],
+        [(offs, SMEM), (w_gain, VMEM), (acc, VMEM), (sums, VMEM), (gain_sum, VMEM), (mix, VMEM), (my_head, VMEM), (features, VMEM)]
+        + [(b, VMEM) for d in late for b in pairs[d]],
+        flops=2e9, moved=8e6, name="forward_late",
+    )
+    (slope,) = call(slope_kernel, [((hidden_units, tokens), F32)], [(pre_act, VMEM), (stats, VMEM)], flops=1e9, moved=4e6, name="gelu_slope")
+
+    kept = logits[0] + send(logits[1], SIBLING)
+    first = core * chunks
+    for bit in (2, 4):
+        width = kept.shape[0] // 2
+        up = (me // bit) % 2
+        keep = lax.dynamic_slice_in_dim(kept, up * width, width, 0)
+        give = lax.dynamic_slice_in_dim(kept, (1 - up) * width, width, 0)
+        kept = keep + send(give, flip_perm(bit))
+        first = first + up * width
+    kept = kept[0]
+    kept = kept + send(kept, flip_perm(8))
+    labels_kept = lax.dynamic_slice_in_dim(labels, first * LANE, LANE, 0)[None, :]
+    class_id = lax.broadcasted_iota(jnp.int32, kept.shape, 0)
+    kept = jnp.where(class_id < classes, kept, -jnp.inf)
+    col_max = jnp.max(kept, axis=0, keepdims=True)
+    exp_terms = jnp.exp(kept - col_max)
+    exp_total = jnp.sum(exp_terms, axis=0, keepdims=True)
+    onehot = class_id == labels_kept
+    picked = jnp.sum(jnp.where(onehot, kept, 0.0), axis=0, keepdims=True)
+    loss = jnp.log(exp_total) + col_max - picked
+    loss_high = loss.astype(BF).astype(F32)
+    grad = exp_terms / exp_total - onehot.astype(F32)
+    grad = jnp.where(class_id == classes, loss_high, jnp.where(class_id == classes + 1, loss - loss_high, grad))
+    grad = grad.astype(BF)[None]
+    for bit in (4, 2):
+        other = send(grad, flip_perm(bit))
+        up = (me // bit) % 2 == 1
+        grad = jnp.concatenate([jnp.where(up, other, grad), jnp.where(up, grad, other)], 0)
+    sib_grad = send(grad, SIBLING)
+
+    grad, scaled, means, mixed = call(
+        grad_kernel,
+        [((CLASS_ROWS, tokens), BF), ((hidden_units, tokens), BF), ((EXTRA, LANE), F32), ((hidden_units, CLASS_ROWS), BF)],
+        [(offs, SMEM), (grad, VMEM), (sib_grad, VMEM), (mix, VMEM), (slope, VMEM), (pre_act, VMEM), (gain_sum, VMEM), (hidden, VMEM)],
+        flops=1e9, moved=8e6, name="hidden_grad",
+    )
+    mean_loss = (jnp.sum(grad[classes : classes + 2].astype(F32)) / tokens).reshape(1)
+
+    own, sib = [None] * CHIPS, [None] * CHIPS
+    height = rows + EXTRA
+    for ids in ((4,), (3, 5), (2, 6), (1, 7, 0)):
+        made = call(
+            functools.partial(message_kernel, ids),
+            [((height, tokens), F32), ((height, tokens), BF)] * len(ids),
+            [(offs, SMEM), (w_gain_t, VMEM), (scaled, VMEM), (w_out, VMEM), (mixed, VMEM), (means, VMEM)],
+            flops=4e8 * len(ids), moved=2e6, name="messages",
+        )
+        for n, d in enumerate(ids):
+            own[d], sib[d] = made[2 * n], send(made[2 * n + 1], SIBLING)
+    forth, back = scatter_walk(own, sib)
+
+    (d_w_out,) = call(
+        d_w_out_kernel, [((hidden_units, channels), F32)], [(mixed, VMEM), (head_pad, VMEM), (layer_scale[None, :], VMEM)],
+        flops=2e9, moved=8e6, name="d_w_out",
+    )
+    (d_w_in,) = call(
+        d_w_in_kernel,
+        [((hidden_units, channels), F32)],
+        [(offs, SMEM), (scaled, VMEM), (stats, VMEM), (norm_gain[None, :], VMEM)] + [(b, VMEM) for pair in pairs for b in pair],
+        flops=2e9, moved=8e6, name="d_w_in",
+    )
+    mine = own[0] + sib[0].astype(F32)
+    d_features, d_dw, d_scale, d_head = call(
+        functools.partial(last_kernel, classes),
+        [((rows, tokens), F32), ((rows, KS * KS), F32), ((rows, 1), F32), ((rows, classes), F32)],
+        [(a, VMEM) for a in (mine, forth, back, features, conv_out, stats, dw_weight, my_head, my_scale, grad)],
+        [grid_shape, copies_shape, taps_shape, copies_shape, pltpu.VMEM((KS * KS, 8, LANE), F32)], name="conv_backward",
+    )
+    return (d_features, d_dw, d_scale[:, 0], d_w_in, d_w_out, d_head, mean_loss)
 
 
 def conv_apply(in_grid, kernel):
@@ -32,7 +439,7 @@
     return (values * cum_prob, cum_prob + values * density)
 
 
-def per_device(features, dw_weight, norm_gain, layer_scale, w_in, w_out, w_head, labels):
+def plain_device(features, dw_weight, norm_gain, layer_scale, w_in, w_out, w_head, labels):
     highest = lax.Precision.HIGHEST
     my_rows = features.shape[0]
     tok_count = features.shape[1]
@@ -82,7 +489,6 @@
     d_scale = jnp.sum(out_grad * branch_sum, axis=1)
     branch_grad = (my_scale[:, None] * out_grad).astype(jnp.bfloat16)
     incoming = lax.all_gather(branch_grad, "ch", axis=0, tiled=True)
-    w_cols = w_out
     hidden_acc = jnp.dot(w_cols, incoming, preferred_element_type=jnp.float32)
     tile_grad = lax.dot_general(
         hidden, incoming, (((1,), (1,)), ((), ())), preferred_element_type=jnp.float32
@@ -110,7 +516,7 @@
 def solution(mesh):
     placed = (P("ch", "grp"), P("ch", None), P(), P(), P("ch", None), P("ch", None), P(), P("grp"))
     return jax.shard_map(
-        per_device,
+        per_device if mesh.shape["ch"] == 2 * CHIPS else plain_device,
         mesh=mesh,
         in_specs=placed,
         out_specs=(

time: 498 us -> 141 us (0.28)
  waiting for transfers between devices: 392 us -> 37.5 us
  other arithmetic: 44 us -> 3.58 us
  Pallas kernels: 0 us -> 37.8 us
  matrix products: 35 us -> 0 us
  starting transfers between devices: 0.39 us -> 28.4 us
  local copies, waits for them, and re-layouts: 9.9 us -> 29.9 us
  between operations: 16.2 us -> 3.14 us
    reduce_scatter x2 -> x0, waiting for transfers between devices: 191 us -> none  [the longest x1 102 us: per_device(): lax.psum_scatter(lax.dot_general(w_cols, hidden, (((0,), (0,)), ((), ()))...]
    all_gather x2 -> x0, waiting for transfers between devices: 110 us -> none  [the longest x1 56 us: per_device(): conv_all = lax.all_gather(conv_out, 'ch', axis=0, tiled=True)]
    psum x1 -> x0, waiting for transfers between devices: 91.7 us -> none  [per_device(): logits = lax.psum(part_logits, 'ch')]
    pallas_call x0 -> x17, Pallas kernels: none -> 37.8 us  [call(): pl.pallas_call(kernel, out_shape=[jax.ShapeDtypeStruct(s, d) for s, d in...]
    ppermute x0 -> x39, waiting for transfers between devices: none -> 37.5 us  [send(): return lax.ppermute(value, 'ch', perm)]
    dot_general x9 -> x0, matrix products: 35 us -> none  [the longest x1 7.36 us: per_device(): lax.dot_general(pre_grad, norm_out, (((1,), (1,)), ((), ())), preferred_e...]
    ppermute x0 -> x39, starting transfers between devices: none -> 28.4 us  [send(): return lax.ppermute(value, 'ch', perm)]
    unnamed x93 -> x127, local copies, waits for them, and re-layouts: 3.12 us -> 23.8 us
  transfers between devices with their start and end apart: 5 -> 39, of which waited for: 5 -> 15; matrix products, arithmetic and copies ran while one was open for 3% -> 8% of each run, Pallas kernels for 0% -> 17%
where the time goes in v1:
time: 141 us; the launch traced here: 140 us
  Pallas kernels  37.8 us (27%)
  waiting for transfers between devices  37.5 us (27%)
  local copies, waits for them, and re-layouts  29.9 us (21%)
  starting transfers between devices  28.4 us (20%)
  other arithmetic  3.58 us (3%)
  between operations  3.14 us (2%)
    pallas_call x17, Pallas kernels, call(): pl.pallas_call(kernel, out_shape=[jax.ShapeDtypeStruct(s, d) for s, d in...  37.8 us
    ppermute x39, waiting for transfers between devices, send(): return lax.ppermute(value, 'ch', perm)  37.5 us
    ppermute x39, starting transfers between devices, send(): return lax.ppermute(value, 'ch', perm)  28.4 us
    unnamed x127, local copies, waits for them, and re-layouts  23.8 us
  transfers between devices with their start and end apart: 39, of which 15 were waited for; matrix products, arithmetic and copies ran while one was open for 8% of the time, Pallas kernels for 17%

profile of v1, /device:TPU:0, one launch (start us, length us, event | category | flops | bytes accessed | tf_op | source)
XLA Modules:
  0.0 140.4 jit_solution(5782887410475691915)
XLA Ops:
  2.4 2.6 %conv_forward.1.refs_0_.conv_ref = bf16[128,1024]{1,0:T(8,128)(2,1)S(1)} custom-call(bf16[128,1024]{1,0:T(8,128)(2,1)S(1)} %copy-done.13, f32[128,49]{1,0:T(8,128)S(1)} %copy.26.w_ref), custom_call_target="tpu_custom_call" | custom-call | tf_op jit(solution)/shard_map/conv_forward/pallas_call | solution.py:47
  5.1 3.1 %collective-permute-start.3 = (bf16[128,1024]{1,0:T(8,128)(2,1)S(1)}, bf16[128,1024]{1,0:T(8,128)(2,1)}, u32[]{:S(2)}, u32[]{:S(2)}) collective-permute-start(bf16[128,1024]{1,0:T(8,128)(2,1)S(1)} %conv_forward.1.refs_0_.conv_ref), channel_id=1, source_target_pairs={{0,4},{1,5},{4,8},{5,9},{8,12},{9,13},{12,14},{13,15},{14,10},{15,... | collective-permute-start | bytes 786440 | tf_op jit(solution)/shard_map/ppermute | solution.py:38
  8.1 6.3 %collective-permute-done.3.refs_4_.refs_14_ = bf16[128,1024]{1,0:T(8,128)(2,1)} collective-permute-done((bf16[128,1024]{1,0:T(8,128)(2,1)S(1)}, bf16[128,1024]{1,0:T(8,128)(2,1)}, u32[]{:S(2)}, u32[]{:S(2)}) %collective-permute-start.3) | collective-permute-done | bytes 262176 | tf_op jit(solution)/shard_map/ppermute | solution.py:38
  14.5 1.8 %collective-permute-start.7 = (bf16[128,1024]{1,0:T(8,128)(2,1)}, bf16[128,1024]{1,0:T(8,128)(2,1)}, u32[]{:S(2)}, u32[]{:S(2)}) collective-permute-start(bf16[128,1024]{1,0:T(8,128)(2,1)} %collective-permute-done.3.refs_4_.refs_14_), channel_id=1, source_target_pairs={{0,4},{1,5},{4,8},{5,9},{8,12},{9,13},{12,14},{13,15},{14,10},{15,... | collective-permute-start | bytes 786440 | tf_op jit(solution)/shard_map/ppermute | solution.py:38
  16.5 2.2 %copy.24 = bf16[2048,150]{1,0:T(8,128)(2,1)} copy(bf16[2048,150]{0,1:T(8,128)(2,1)} %param.15) | data formatting | bytes 1228800 | tf_op args[6]
  23.0 1.8 %collective-permute-start.11 = (bf16[128,1024]{1,0:T(8,128)(2,1)}, bf16[128,1024]{1,0:T(8,128)(2,1)S(1)}, u32[]{:S(2)}, u32[]{:S(2)}) collective-permute-start(bf16[128,1024]{1,0:T(8,128)(2,1)} %collective-permute-done.7.refs_8_.refs_12_), channel_id=1, source_target_pairs={{0,4},{1,5},{4,8},{5,9},{8,12},{9,13},{12,14},{13,15},{14,10},{15,... | collective-permute-start | bytes 786440 | tf_op jit(solution)/shard_map/ppermute | solution.py:38
  34.2 1.8 %collective-permute-start.13 = (bf16[64,1024]{1,0:T(8,128)(2,1)S(1)}, bf16[64,1024]{1,0:T(8,128)(2,1)S(1)}, u32[]{:S(2)}, u32[]{:S(2)}) collective-permute-start(bf16[64,1024]{1,0:T(8,128)(2,1)S(1)} %slice.20), channel_id=1, source_target_pairs={{0,4},{1,5},{4,8},{5,9},{8,12},{9,13},{12,14},{13,15},{14,10},{15,... | collective-permute-start | bytes 393224 | tf_op jit(solution)/shard_map/ppermute | solution.py:38
  39.7 2.4 %collective-permute-done.14 = bf16[64,1024]{1,0:T(8,128)(2,1)S(1)} collective-permute-done((bf16[64,1024]{1,0:T(8,128)(2,1)S(1)}, bf16[64,1024]{1,0:T(8,128)(2,1)S(1)}, u32[]{:S(2)}, u32[]{:S(2)}) %collective-permute-start.14) | collective-permute-done | bytes 131104 | tf_op jit(solution)/shard_map/ppermute | solution.py:38
  43.8 1.7 %copy-done.60 = bf16[512,2048]{1,0:T(8,128)(2,1)S(1)} copy-done((bf16[512,2048]{1,0:T(8,128)(2,1)S(1)}, bf16[512,2048]{1,0:T(8,128)(2,1)}, u32[]{:S(2)}) %copy-start.60) | copy-done | bytes 2097176
  45.6 3.3 %forward_early.1 = (f32[512,1024]{1,0:T(8,128)S(1)}, f32[8,1024]{1,0:T(8,128)S(1)}) custom-call(s32[17]{0:T(128)S(1)} %pad_add_fusion.offs_ref, bf16[512,2048]{1,0:T(8,128)(2,1)S(1)} %copy-done.60, bf16[128,1024]{1,0:T(8,128)(2,1)S(1)} %conv_forward.1.refs_0_.conv_ref, bf16[128,1024]{1,0:T(8,128)(2,1)} %collective-permute-done.refs_1_, ...), custom_call_target="tpu_custom_call" | custom-call | flops 2000000000 | bytes 8000000 | tf_op jit(solution)/shard_map/forward_early/pallas_call | solution.py:47
  49.0 2.4 %forward_late.1 = (f32[512,1024]{1,0:T(8,128)S(1)}, bf16[512,1024]{1,0:T(8,128)(2,1)S(1)}, f32[8,1024]{1,0:T(8,128)S(1)}, f32[2,4,160,128]{3,2,1,0:T(8,128)S(1)}) custom-call(s32[17]{0:T(128)S(1)} %pad_add_fusion.offs_ref, bf16[512,2048]{1,0:T(8,128)(2,1)S(1)} %copy-done.60, f32[512,1024]{1,0:T(8,128)S(1)} %get-tuple-element.51.acc_ref, ...), custom_call_target="tpu_custom_call" | custom-call | flops 2000000000 | bytes 8000000 | tf_op jit(solution)/shard_map/forward_late/pallas_call | solution.py:47
  56.6 5.2 %collective-permute-done.17 = f32[2,160,128]{2,1,0:T(8,128)S(1)} collective-permute-done((f32[2,160,128]{2,1,0:T(8,128)S(1)}, f32[2,160,128]{2,1,0:T(8,128)S(1)}, u32[]{:S(2)}, u32[]{:S(2)}) %collective-permute-start.17) | collective-permute-done | bytes 163872 | tf_op jit(solution)/shard_map/ppermute | solution.py:38
  61.9 1.6 %collective-permute-start.18 = (f32[1,160,128]{2,1,0:T(8,128)S(1)}, f32[1,160,128]{2,1,0:T(8,128)S(1)}, u32[]{:S(2)}, u32[]{:S(2)}) collective-permute-start(f32[1,160,128]{2,1,0:T(8,128)S(1)} %constant_dynamic-slice_fusion), channel_id=1, source_target_pairs={{0,4},{1,5},{2,6},{3,7},{4,0},{5,1},{6,2},{7,3},{8,12},{9,13},{10,... | collective-permute-start | bytes 245768 | tf_op jit(solution)/shard_map/ppermute | solution.py:38
  63.5 2.9 %collective-permute-done.18 = f32[1,160,128]{2,1,0:T(8,128)S(1)} collective-permute-done((f32[1,160,128]{2,1,0:T(8,128)S(1)}, f32[1,160,128]{2,1,0:T(8,128)S(1)}, u32[]{:S(2)}, u32[]{:S(2)}) %collective-permute-start.18) | collective-permute-done | bytes 81952 | tf_op jit(solution)/shard_map/ppermute | solution.py:38
  66.4 2.7 %collective-permute-start.19 = (f32[160,128]{1,0:T(8,128)S(1)}, f32[160,128]{1,0:T(8,128)S(1)}, u32[]{:S(2)}, u32[]{:S(2)}) collective-permute-start(f32[160,128]{1,0:T(8,128)S(1)} %add_bitcast_fusion), channel_id=1, source_target_pairs={{0,8},{1,9},{2,10},{3,11},{4,12},{5,13},{6,14},{7,15},{8,0},{9,1},... | collective-permute-start | bytes 245768 | tf_op jit(solution)/shard_map/ppermute | solution.py:38
  69.1 2.7 %collective-permute-done.19 = f32[160,128]{1,0:T(8,128)S(1)} collective-permute-done((f32[160,128]{1,0:T(8,128)S(1)}, f32[160,128]{1,0:T(8,128)S(1)}, u32[]{:S(2)}, u32[]{:S(2)}) %collective-permute-start.19) | collective-permute-done | bytes 81952 | tf_op jit(solution)/shard_map/ppermute | solution.py:38
  72.1 1.6 %collective-permute-start.20 = (bf16[1,160,128]{2,1,0:T(8,128)(2,1)S(1)}, bf16[1,160,128]{2,1,0:T(8,128)(2,1)S(1)}, u32[]{:S(2)}, u32[]{:S(2)}) collective-permute-start(bf16[1,160,128]{2,1,0:T(8,128)(2,1)S(1)} %fusion.1), channel_id=1, source_target_pairs={{0,4},{1,5},{2,6},{3,7},{4,0},{5,1},{6,2},{7,3},{8,12},{9,13},{10,... | collective-permute-start | bytes 122888 | tf_op jit(solution)/shard_map/ppermute | solution.py:38
  73.7 2.4 %collective-permute-done.20 = bf16[1,160,128]{2,1,0:T(8,128)(2,1)S(1)} collective-permute-done((bf16[1,160,128]{2,1,0:T(8,128)(2,1)S(1)}, bf16[1,160,128]{2,1,0:T(8,128)(2,1)S(1)}, u32[]{:S(2)}, u32[]{:S(2)}) %collective-permute-start.20) | collective-permute-done | bytes 40992 | tf_op jit(solution)/shard_map/ppermute | solution.py:38
  76.7 4.1 %collective-permute-done.21 = bf16[2,160,128]{2,1,0:T(8,128)(2,1)S(1)} collective-permute-done((bf16[2,160,128]{2,1,0:T(8,128)(2,1)S(1)}, bf16[2,160,128]{2,1,0:T(8,128)(2,1)S(1)}, u32[]{:S(2)}, u32[]{:S(2)}) %collective-permute-start.21) | collective-permute-done | bytes 81952 | tf_op jit(solution)/shard_map/ppermute | solution.py:38
  89.9 1.6 %collective-permute-start.31 = (bf16[80,1024]{1,0:T(8,128)(2,1)S(1)}, bf16[80,1024]{1,0:T(8,128)(2,1)S(1)}, u32[]{:S(2)}, u32[]{:S(2)}) collective-permute-start(bf16[80,1024]{1,0:T(8,128)(2,1)S(1)} %get-tuple-element.78), channel_id=1, source_target_pairs={{0,4},{1,5},{4,8},{5,9},{8,12},{9,13},{12,14},{13,15},{14,10},{15,... | collective-permute-start | bytes 491528 | tf_op jit(solution)/shard_map/ppermute | solution.py:38
  92.0 2.2 %messages.5 = (f32[152,1024]{1,0:T(8,128)S(1)}, bf16[152,1024]{1,0:T(8,128)(2,1)}, f32[152,1024]{1,0:T(8,128)S(1)}, bf16[152,1024]{1,0:T(8,128)(2,1)}) custom-call(s32[17]{0:T(128)S(1)} %pad_add_fusion.offs_ref, bf16[2048,512]{1,0:T(8,128)(2,1)S(1)} %copy-done.2, bf16[512,1024]{1,0:T(8,128)(2,1)S(1)} %get-tuple-element.59.scaled_ref, ...), custom_call_target="tpu_custom_call" | custom-call | flops 800000000 | bytes 2000000 | tf_op jit(solution)/shard_map/messages/pallas_call | solution.py:47
  98.2 2.0 %collective-permute-start.33 = (bf16[152,1024]{1,0:T(8,128)(2,1)}, bf16[152,1024]{1,0:T(8,128)(2,1)}, u32[]{:S(2)}, u32[]{:S(2)}) collective-permute-start(bf16[152,1024]{1,0:T(8,128)(2,1)} %get-tuple-element.80), channel_id=1, source_target_pairs={{0,4},{1,5},{4,8},{5,9},{8,12},{9,13},{12,14},{13,15},{14,10},{15,... | collective-permute-start | bytes 933896 | tf_op jit(solution)/shard_map/ppermute | solution.py:38
  101.0 1.6 %copy-done.3 = bf16[2048,512]{1,0:T(8,128)(2,1)S(1)} copy-done((bf16[2048,512]{1,0:T(8,128)(2,1)S(1)}, bf16[2048,512]{1,0:T(8,128)(2,1)}, u32[]{:S(2)}) %copy-start.3) | copy-done | bytes 2097176
  102.6 2.6 %messages.4 = (f32[152,1024]{1,0:T(8,128)S(1)}, bf16[152,1024]{1,0:T(8,128)(2,1)S(1)}, f32[152,1024]{1,0:T(8,128)S(1)}, bf16[152,1024]{1,0:T(8,128)(2,1)S(1)}, f...) custom-call(s32[17]{0:T(128)S(1)} %pad_add_fusion.offs_ref, bf16[2048,512]{1,0:T(8,128)(2,1)S(1)} %copy-done.3, ...), custom_call_target="tpu_custom_call" | custom-call | flops 1200000000 | bytes 2000000 | tf_op jit(solution)/shard_map/messages/pallas_call | solution.py:47
  107.0 1.8 %collective-permute-done.34.refs_5_ = bf16[152,1024]{1,0:T(8,128)(2,1)} collective-permute-done((bf16[152,1024]{1,0:T(8,128)(2,1)}, bf16[152,1024]{1,0:T(8,128)(2,1)}, u32[]{:S(2)}, u32[]{:S(2)}) %collective-permute-start.34) | collective-permute-done | bytes 311328 | tf_op jit(solution)/shard_map/ppermute | solution.py:38
  110.2 1.7 %collective-permute-start.35 = (bf16[152,1024]{1,0:T(8,128)(2,1)S(1)}, bf16[152,1024]{1,0:T(8,128)(2,1)S(1)}, u32[]{:S(2)}, u32[]{:S(2)}) collective-permute-start(bf16[152,1024]{1,0:T(8,128)(2,1)S(1)} %get-tuple-element.82), channel_id=1, source_target_pairs={{0,4},{1,5},{4,8},{5,9},{8,12},{9,13},{12,14},{13,15},{14,10},{15,... | collective-permute-start | bytes 933896 | tf_op jit(solution)/shard_map/ppermute | solution.py:38
  112.4 2.8 %d_w_out.1 = f32[512,2048]{1,0:T(8,128)} custom-call(bf16[512,160]{1,0:T(8,128)(2,1)S(1)} %get-tuple-element.60.mixed_ref, bf16[2048,160]{1,0:T(8,128)(2,1)S(1)} %copy-done.12, f32[1,2048]{1,0:T(1,128)S(1)} %bitcast.22), custom_call_target="tpu_custom_call" | custom-call | flops 2000000000 | bytes 8000000 | tf_op jit(solution)/shard_map/d_w_out/pallas_call | solution.py:47
  115.3 6.2 %d_w_in.1 = f32[512,2048]{1,0:T(8,128)} custom-call(s32[17]{0:T(128)S(1)} %pad_add_fusion.offs_ref, bf16[512,1024]{1,0:T(8,128)(2,1)S(1)} %get-tuple-element.59.scaled_ref, f32[8,1024]{1,0:T(8,128)S(1)} %get-tuple-element.57.stats_ref, f32[1,2048]{1,0:T(1,128)S(1)} %bitcast.24, bf16[128,1024]{1,0:T(8,128)(2,1)S(1)} %copy-done.8, ...), custom_call_target="tpu_custom_call" | custom-call | flops 2000000000 | bytes 8000000 | tf_op jit(solution)/shard_map/d_w_in/pallas_call | solution.py:47
  122.4 1.7 %collective-permute-start.37 = (bf16[152,1024]{1,0:T(8,128)(2,1)}, bf16[152,1024]{1,0:T(8,128)(2,1)S(1)}, u32[]{:S(2)}, u32[]{:S(2)}) collective-permute-start(bf16[152,1024]{1,0:T(8,128)(2,1)} %get-tuple-element.84), channel_id=1, source_target_pairs={{0,4},{1,5},{4,8},{5,9},{8,12},{9,13},{12,14},{13,15},{14,10},{15,... | collective-permute-start | bytes 933896 | tf_op jit(solution)/shard_map/ppermute | solution.py:38
  126.7 2.8 %collective-permute-done.37.forth_ref = bf16[152,1024]{1,0:T(8,128)(2,1)S(1)} collective-permute-done((bf16[152,1024]{1,0:T(8,128)(2,1)}, bf16[152,1024]{1,0:T(8,128)(2,1)S(1)}, u32[]{:S(2)}, u32[]{:S(2)}) %collective-permute-start.37) | collective-permute-done | bytes 311328 | tf_op jit(solution)/shard_map/ppermute | solution.py:38
  129.5 1.8 %collective-permute-done.38.back_ref = bf16[152,1024]{1,0:T(8,128)(2,1)S(1)} collective-permute-done((bf16[152,1024]{1,0:T(8,128)(2,1)S(1)}, bf16[152,1024]{1,0:T(8,128)(2,1)S(1)}, u32[]{:S(2)}, u32[]{:S(2)}) %collective-permute-start.38) | collective-permute-done | bytes 311328 | tf_op jit(solution)/shard_map/ppermute | solution.py:38
  131.3 5.9 %conv_backward.1 = (f32[128,1024]{1,0:T(8,128)}, f32[128,49]{1,0:T(8,128)S(1)}, f32[128,1]{1,0:T(8,128)S(1)}, f32[128,150]{1,0:T(8,128)S(1)}) custom-call(f32[152,1024]{1,0:T(8,128)S(1)} %convert_add_fusion.mine_ref, bf16[152,1024]{1,0:T(8,128)(2,1)S(1)} %collective-permute-done.37.forth_ref, bf16[152,1024]{1,0:T(8,128)(2,1)S(1)} %collective-permute-done.38.back_ref, ...), custom_call_target="tpu_custom_call" | custom-call | tf_op jit(solution)/shard_map/conv_backward/pallas_call | solution.py:47
  (224 shorter events, 50.0 us)
Async XLA Ops:
  5.1 9.4 %collective-permute-start.3 = (bf16[128,1024]{1,0:T(8,128)(2,1)S(1)}, bf16[128,1024]{1,0:T(8,128)(2,1)}, u32[]{:S(2)}, u32[]{:S(2)}) collective-permute-start(bf16[128,1024]{1,0:T(8,128)(2,1)S(1)} %conv_forward.1.refs_0_.conv_ref), channel_id=1, source_target_pairs={{0,4},{1,5},{4,8},{5,9},{8,12},{9,13},{12,14},{13,15},{14,10},{15,... | collective-permute-start | bytes 786440 | tf_op jit(solution)/shard_map/ppermute | solution.py:38
  8.1 8.2 %collective-permute-start.1 = (bf16[128,1024]{1,0:T(8,128)(2,1)S(1)}, bf16[128,1024]{1,0:T(8,128)(2,1)}, u32[]{:S(2)}, u32[]{:S(2)}) collective-permute-start(bf16[128,1024]{1,0:T(8,128)(2,1)S(1)} %conv_forward.1.refs_0_.conv_ref), channel_id=1, source_target_pairs={{0,2},{1,3},{4,0},{5,1},{8,4},{9,5},{12,8},{13,9},{14,12},{15,13},... | collective-permute-start | bytes 786440 | tf_op jit(solution)/shard_map/ppermute | solution.py:38
  14.5 8.5 %collective-permute-start.7 = (bf16[128,1024]{1,0:T(8,128)(2,1)}, bf16[128,1024]{1,0:T(8,128)(2,1)}, u32[]{:S(2)}, u32[]{:S(2)}) collective-permute-start(bf16[128,1024]{1,0:T(8,128)(2,1)} %collective-permute-done.3.refs_4_.refs_14_), channel_id=1, source_target_pairs={{0,4},{1,5},{4,8},{5,9},{8,12},{9,13},{12,14},{13,15},{14,10},{15,... | collective-permute-start | bytes 786440 | tf_op jit(solution)/shard_map/ppermute | solution.py:38
  16.3 8.5 %collective-permute-start.5 = (bf16[128,1024]{1,0:T(8,128)(2,1)}, bf16[128,1024]{1,0:T(8,128)(2,1)}, u32[]{:S(2)}, u32[]{:S(2)}) collective-permute-start(bf16[128,1024]{1,0:T(8,128)(2,1)} %collective-permute-done.1.refs_2_), channel_id=1, source_target_pairs={{0,2},{1,3},{4,0},{5,1},{8,4},{9,5},{12,8},{13,9},{14,12},{15,13},... | collective-permute-start | bytes 786440 | tf_op jit(solution)/shard_map/ppermute | solution.py:38
  16.5 25.6 %collective-permute-start = (bf16[128,1024]{1,0:T(8,128)(2,1)S(1)}, bf16[128,1024]{1,0:T(8,128)(2,1)}, u32[]{:S(2)}, u32[]{:S(2)}) collective-permute-start(bf16[128,1024]{1,0:T(8,128)(2,1)S(1)} %conv_forward.1.refs_0_.conv_ref), channel_id=1, source_target_pairs={{0,1},{1,0},{2,3},{3,2},{4,5},{5,4},{6,7},{7,6},{8,9},{9,8},{10,11... | collective-permute-start | bytes 786440 | tf_op jit(solution)/shard_map/ppermute | solution.py:38
  23.0 10.5 %collective-permute-start.11 = (bf16[128,1024]{1,0:T(8,128)(2,1)}, bf16[128,1024]{1,0:T(8,128)(2,1)S(1)}, u32[]{:S(2)}, u32[]{:S(2)}) collective-permute-start(bf16[128,1024]{1,0:T(8,128)(2,1)} %collective-permute-done.7.refs_8_.refs_12_), channel_id=1, source_target_pairs={{0,4},{1,5},{4,8},{5,9},{8,12},{9,13},{12,14},{13,15},{14,10},{15,... | collective-permute-start | bytes 786440 | tf_op jit(solution)/shard_map/ppermute | solution.py:38
  24.8 11.2 %collective-permute-start.9 = (bf16[128,1024]{1,0:T(8,128)(2,1)}, bf16[128,1024]{1,0:T(8,128)(2,1)S(1)}, u32[]{:S(2)}, u32[]{:S(2)}) collective-permute-start(bf16[128,1024]{1,0:T(8,128)(2,1)} %collective-permute-done.5.refs_6_.refs_4_), channel_id=1, source_target_pairs={{0,2},{1,3},{4,0},{5,1},{8,4},{9,5},{12,8},{13,9},{14,12},{15,13},... | collective-permute-start | bytes 786440 | tf_op jit(solution)/shard_map/ppermute | solution.py:38
  34.2 5.5 %collective-permute-start.13 = (bf16[64,1024]{1,0:T(8,128)(2,1)S(1)}, bf16[64,1024]{1,0:T(8,128)(2,1)S(1)}, u32[]{:S(2)}, u32[]{:S(2)}) collective-permute-start(bf16[64,1024]{1,0:T(8,128)(2,1)S(1)} %slice.20), channel_id=1, source_target_pairs={{0,4},{1,5},{4,8},{5,9},{8,12},{9,13},{12,14},{13,15},{14,10},{15,... | collective-permute-start | bytes 393224 | tf_op jit(solution)/shard_map/ppermute | solution.py:38
  36.8 5.3 %collective-permute-start.14 = (bf16[64,1024]{1,0:T(8,128)(2,1)S(1)}, bf16[64,1024]{1,0:T(8,128)(2,1)S(1)}, u32[]{:S(2)}, u32[]{:S(2)}) collective-permute-start(bf16[64,1024]{1,0:T(8,128)(2,1)S(1)} %slice.21), channel_id=1, source_target_pairs={{0,2},{1,3},{4,0},{5,1},{8,4},{9,5},{12,8},{13,9},{14,12},{15,13},... | collective-permute-start | bytes 393224 | tf_op jit(solution)/shard_map/ppermute | solution.py:38
  37.9 4.8 %collective-permute-start.2 = (bf16[128,1024]{1,0:T(8,128)(2,1)}, bf16[128,1024]{1,0:T(8,128)(2,1)S(1)}, u32[]{:S(2)}, u32[]{:S(2)}) collective-permute-start(bf16[128,1024]{1,0:T(8,128)(2,1)} %collective-permute-done.1.refs_2_), channel_id=1, source_target_pairs={{0,1},{1,0},{2,3},{3,2},{4,5},{5,4},{6,7},{7,6},{8,9},{9,8},{10,11... | collective-permute-start | bytes 786440 | tf_op jit(solution)/shard_map/ppermute | solution.py:38
  37.9 4.9 %collective-permute-start.4 = (bf16[128,1024]{1,0:T(8,128)(2,1)}, bf16[128,1024]{1,0:T(8,128)(2,1)S(1)}, u32[]{:S(2)}, u32[]{:S(2)}) collective-permute-start(bf16[128,1024]{1,0:T(8,128)(2,1)} %collective-permute-done.3.refs_4_.refs_14_), channel_id=1, source_target_pairs={{0,1},{1,0},{2,3},{3,2},{4,5},{5,4},{6,7},{7,6},{8,9},{9,8},{10,11... | collective-permute-start | bytes 786440 | tf_op jit(solution)/shard_map/ppermute | solution.py:38
  42.1 6.7 %collective-permute-start.10 = (bf16[128,1024]{1,0:T(8,128)(2,1)}, bf16[128,1024]{1,0:T(8,128)(2,1)S(1)}, u32[]{:S(2)}, u32[]{:S(2)}) collective-permute-start(bf16[128,1024]{1,0:T(8,128)(2,1)} %copy-done.26), channel_id=1, source_target_pairs={{0,1},{1,0},{2,3},{3,2},{4,5},{5,4},{6,7},{7,6},{8,9},{9,8},{10,11... | collective-permute-start | bytes 786440 | tf_op jit(solution)/shard_map/ppermute | solution.py:38
  42.7 6.2 %collective-permute-start.12 = (bf16[128,1024]{1,0:T(8,128)(2,1)}, bf16[128,1024]{1,0:T(8,128)(2,1)S(1)}, u32[]{:S(2)}, u32[]{:S(2)}) collective-permute-start(bf16[128,1024]{1,0:T(8,128)(2,1)} %copy-done.23), channel_id=1, source_target_pairs={{0,1},{1,0},{2,3},{3,2},{4,5},{5,4},{6,7},{7,6},{8,9},{9,8},{10,11... | collective-permute-start | bytes 786440 | tf_op jit(solution)/shard_map/ppermute | solution.py:38
  42.8 6.1 %collective-permute-start.15 = (bf16[128,1024]{1,0:T(8,128)(2,1)S(1)}, bf16[128,1024]{1,0:T(8,128)(2,1)S(1)}, u32[]{:S(2)}, u32[]{:S(2)}) collective-permute-start(bf16[128,1024]{1,0:T(8,128)(2,1)S(1)} %constant_dynamic-update-slice_fusion.refs_4_.refs_8_), channel_id=1, source_target_pairs={{0,1},{1,0},{2,3},{3,2},{4,5},{5,4},{6,7},{7,6},{8,9},{9,8},{10,11... | collective-permute-start | bytes 786440 | tf_op jit(solution)/shard_map/ppermute | solution.py:38
  55.5 6.3 %collective-permute-start.17 = (f32[2,160,128]{2,1,0:T(8,128)S(1)}, f32[2,160,128]{2,1,0:T(8,128)S(1)}, u32[]{:S(2)}, u32[]{:S(2)}) collective-permute-start(f32[2,160,128]{2,1,0:T(8,128)S(1)} %constant_dynamic-slice_fusion.1), channel_id=1, source_target_pairs={{0,2},{1,3},{2,0},{3,1},{4,6},{5,7},{6,4},{7,5},{8,10},{9,11},{10,... | collective-permute-start | bytes 491528 | tf_op jit(solution)/shard_map/ppermute | solution.py:38
  66.4 5.4 %collective-permute-start.19 = (f32[160,128]{1,0:T(8,128)S(1)}, f32[160,128]{1,0:T(8,128)S(1)}, u32[]{:S(2)}, u32[]{:S(2)}) collective-permute-start(f32[160,128]{1,0:T(8,128)S(1)} %add_bitcast_fusion), channel_id=1, source_target_pairs={{0,8},{1,9},{2,10},{3,11},{4,12},{5,13},{6,14},{7,15},{8,0},{9,1},... | collective-permute-start | bytes 245768 | tf_op jit(solution)/shard_map/ppermute | solution.py:38
  76.3 4.5 %collective-permute-start.21 = (bf16[2,160,128]{2,1,0:T(8,128)(2,1)S(1)}, bf16[2,160,128]{2,1,0:T(8,128)(2,1)S(1)}, u32[]{:S(2)}, u32[]{:S(2)}) collective-permute-start(bf16[2,160,128]{2,1,0:T(8,128)(2,1)S(1)} %pad_maximum_fusion.1), channel_id=1, source_target_pairs={{0,2},{1,3},{2,0},{3,1},{4,6},{5,7},{6,4},{7,5},{8,10},{9,11},{10,... | collective-permute-start | bytes 245768 | tf_op jit(solution)/shard_map/ppermute | solution.py:38
  89.3 6.6 %collective-permute-start.28 = (bf16[152,1024]{1,0:T(8,128)(2,1)S(1)}, bf16[152,1024]{1,0:T(8,128)(2,1)S(1)}, u32[]{:S(2)}, u32[]{:S(2)}) collective-permute-start(bf16[152,1024]{1,0:T(8,128)(2,1)S(1)} %get-tuple-element.74), channel_id=1, source_target_pairs={{0,1},{1,0},{2,3},{3,2},{4,5},{5,4},{6,7},{7,6},{8,9},{9,8},{10,11... | collective-permute-start | bytes 933896 | tf_op jit(solution)/shard_map/ppermute | solution.py:38
  89.4 7.0 %collective-permute-start.29 = (bf16[152,1024]{1,0:T(8,128)(2,1)S(1)}, bf16[152,1024]{1,0:T(8,128)(2,1)S(1)}, u32[]{:S(2)}, u32[]{:S(2)}) collective-permute-start(bf16[152,1024]{1,0:T(8,128)(2,1)S(1)} %get-tuple-element.75), channel_id=1, source_target_pairs={{0,1},{1,0},{2,3},{3,2},{4,5},{5,4},{6,7},{7,6},{8,9},{9,8},{10,11... | collective-permute-start | bytes 933896 | tf_op jit(solution)/shard_map/ppermute | solution.py:38
  89.9 7.3 %collective-permute-start.31 = (bf16[80,1024]{1,0:T(8,128)(2,1)S(1)}, bf16[80,1024]{1,0:T(8,128)(2,1)S(1)}, u32[]{:S(2)}, u32[]{:S(2)}) collective-permute-start(bf16[80,1024]{1,0:T(8,128)(2,1)S(1)} %get-tuple-element.78), channel_id=1, source_target_pairs={{0,4},{1,5},{4,8},{5,9},{8,12},{9,13},{12,14},{13,15},{14,10},{15,... | collective-permute-start | bytes 491528 | tf_op jit(solution)/shard_map/ppermute | solution.py:38
  91.5 5.7 %collective-permute-start.32 = (bf16[72,1024]{1,0:T(8,128)(2,1)S(1)}, bf16[72,1024]{1,0:T(8,128)(2,1)S(1)}, u32[]{:S(2)}, u32[]{:S(2)}) collective-permute-start(bf16[72,1024]{1,0:T(8,128)(2,1)S(1)} %get-tuple-element.79), channel_id=1, source_target_pairs={{0,2},{1,3},{4,0},{5,1},{8,4},{9,5},{12,8},{13,9},{14,12},{15,13},... | collective-permute-start | bytes 442376 | tf_op jit(solution)/shard_map/ppermute | solution.py:38
  95.9 9.4 %collective-permute-start.26 = (bf16[152,1024]{1,0:T(8,128)(2,1)}, bf16[152,1024]{1,0:T(8,128)(2,1)}, u32[]{:S(2)}, u32[]{:S(2)}) collective-permute-start(bf16[152,1024]{1,0:T(8,128)(2,1)} %get-tuple-element.70), channel_id=1, source_target_pairs={{0,1},{1,0},{2,3},{3,2},{4,5},{5,4},{6,7},{7,6},{8,9},{9,8},{10,11... | collective-permute-start | bytes 933896 | tf_op jit(solution)/shard_map/ppermute | solution.py:38
  95.9 9.9 %collective-permute-start.27 = (bf16[152,1024]{1,0:T(8,128)(2,1)}, bf16[152,1024]{1,0:T(8,128)(2,1)}, u32[]{:S(2)}, u32[]{:S(2)}) collective-permute-start(bf16[152,1024]{1,0:T(8,128)(2,1)} %get-tuple-element.71), channel_id=1, source_target_pairs={{0,1},{1,0},{2,3},{3,2},{4,5},{5,4},{6,7},{7,6},{8,9},{9,8},{10,11... | collective-permute-start | bytes 933896 | tf_op jit(solution)/shard_map/ppermute | solution.py:38
  98.2 8.8 %collective-permute-start.33 = (bf16[152,1024]{1,0:T(8,128)(2,1)}, bf16[152,1024]{1,0:T(8,128)(2,1)}, u32[]{:S(2)}, u32[]{:S(2)}) collective-permute-start(bf16[152,1024]{1,0:T(8,128)(2,1)} %get-tuple-element.80), channel_id=1, source_target_pairs={{0,4},{1,5},{4,8},{5,9},{8,12},{9,13},{12,14},{13,15},{14,10},{15,... | collective-permute-start | bytes 933896 | tf_op jit(solution)/shard_map/ppermute | solution.py:38
  100.2 8.5 %collective-permute-start.34 = (bf16[152,1024]{1,0:T(8,128)(2,1)}, bf16[152,1024]{1,0:T(8,128)(2,1)}, u32[]{:S(2)}, u32[]{:S(2)}) collective-permute-start(bf16[152,1024]{1,0:T(8,128)(2,1)} %get-tuple-element.81), channel_id=1, source_target_pairs={{0,2},{1,3},{4,0},{5,1},{8,4},{9,5},{12,8},{13,9},{14,12},{15,13},... | collective-permute-start | bytes 933896 | tf_op jit(solution)/shard_map/ppermute | solution.py:38
  105.3 16.2 %collective-permute-start.24 = (bf16[152,1024]{1,0:T(8,128)(2,1)S(1)}, bf16[152,1024]{1,0:T(8,128)(2,1)S(1)}, u32[]{:S(2)}, u32[]{:S(2)}) collective-permute-start(bf16[152,1024]{1,0:T(8,128)(2,1)S(1)} %get-tuple-element.66), channel_id=1, source_target_pairs={{0,1},{1,0},{2,3},{3,2},{4,5},{5,4},{6,7},{7,6},{8,9},{9,8},{10,11... | collective-permute-start | bytes 933896 | tf_op jit(solution)/shard_map/ppermute | solution.py:38
  105.3 16.2 %collective-permute-start.25 = (bf16[152,1024]{1,0:T(8,128)(2,1)S(1)}, bf16[152,1024]{1,0:T(8,128)(2,1)S(1)}, u32[]{:S(2)}, u32[]{:S(2)}) collective-permute-start(bf16[152,1024]{1,0:T(8,128)(2,1)S(1)} %get-tuple-element.67), channel_id=1, source_target_pairs={{0,1},{1,0},{2,3},{3,2},{4,5},{5,4},{6,7},{7,6},{8,9},{9,8},{10,11... | collective-permute-start | bytes 933896 | tf_op jit(solution)/shard_map/ppermute | solution.py:38
  105.8 19.9 %collective-permute-start.23 = (bf16[152,1024]{1,0:T(8,128)(2,1)}, bf16[152,1024]{1,0:T(8,128)(2,1)}, u32[]{:S(2)}, u32[]{:S(2)}) collective-permute-start(bf16[152,1024]{1,0:T(8,128)(2,1)} %get-tuple-element.63), channel_id=1, source_target_pairs={{0,1},{1,0},{2,3},{3,2},{4,5},{5,4},{6,7},{7,6},{8,9},{9,8},{10,11... | collective-permute-start | bytes 933896 | tf_op jit(solution)/shard_map/ppermute | solution.py:38
  110.2 11.2 %collective-permute-start.35 = (bf16[152,1024]{1,0:T(8,128)(2,1)S(1)}, bf16[152,1024]{1,0:T(8,128)(2,1)S(1)}, u32[]{:S(2)}, u32[]{:S(2)}) collective-permute-start(bf16[152,1024]{1,0:T(8,128)(2,1)S(1)} %get-tuple-element.82), channel_id=1, source_target_pairs={{0,4},{1,5},{4,8},{5,9},{8,12},{9,13},{12,14},{13,15},{14,10},{15,... | collective-permute-start | bytes 933896 | tf_op jit(solution)/shard_map/ppermute | solution.py:38
  111.9 9.5 %collective-permute-start.36 = (bf16[152,1024]{1,0:T(8,128)(2,1)S(1)}, bf16[152,1024]{1,0:T(8,128)(2,1)S(1)}, u32[]{:S(2)}, u32[]{:S(2)}) collective-permute-start(bf16[152,1024]{1,0:T(8,128)(2,1)S(1)} %get-tuple-element.83), channel_id=1, source_target_pairs={{0,2},{1,3},{4,0},{5,1},{8,4},{9,5},{12,8},{13,9},{14,12},{15,13},... | collective-permute-start | bytes 933896 | tf_op jit(solution)/shard_map/ppermute | solution.py:38
  122.4 7.1 %collective-permute-start.37 = (bf16[152,1024]{1,0:T(8,128)(2,1)}, bf16[152,1024]{1,0:T(8,128)(2,1)S(1)}, u32[]{:S(2)}, u32[]{:S(2)}) collective-permute-start(bf16[152,1024]{1,0:T(8,128)(2,1)} %get-tuple-element.84), channel_id=1, source_target_pairs={{0,4},{1,5},{4,8},{5,9},{8,12},{9,13},{12,14},{13,15},{14,10},{15,... | collective-permute-start | bytes 933896 | tf_op jit(solution)/shard_map/ppermute | solution.py:38
  124.0 7.3 %collective-permute-start.38 = (bf16[152,1024]{1,0:T(8,128)(2,1)S(1)}, bf16[152,1024]{1,0:T(8,128)(2,1)S(1)}, u32[]{:S(2)}, u32[]{:S(2)}) collective-permute-start(bf16[152,1024]{1,0:T(8,128)(2,1)S(1)} %get-tuple-element.85), channel_id=1, source_target_pairs={{0,2},{1,3},{4,0},{5,1},{8,4},{9,5},{12,8},{13,9},{14,12},{15,13},... | collective-permute-start | bytes 933896 | tf_op jit(solution)/shard_map/ppermute | solution.py:38
  (68 other events, 281.8 us)

commit v2 on v0

--- a/solution.py
+++ b/solution.py
@@ -1,14 +1,540 @@
+import functools
+
 import jax
 import jax.numpy as jnp
+import numpy as np
 from jax import lax
+from jax.experimental import pallas as pl
+from jax.experimental.pallas import tpu as pltpu
 from jax.sharding import PartitionSpec as P
 
 KS = 7
+HALF = KS // 2
 WIN_H = 32
 WIN_W = 32
-
-
 norm_eps = 1e-06
+BF = jnp.bfloat16
+F32 = jnp.float32
+
+WALK = (0, 2, 4, 6, 7, 5, 3, 1)
+CHIPS = len(WALK)
+CORES = 2
+REL = np.array([[WALK[(WALK.index(chip) + d) % CHIPS] for d in range(CHIPS)] for chip in range(CHIPS)], np.int32)
+PLACES = np.array(
+    [
+        [REL[dev // 2][d] * 2 + (dev % 2 ^ side) for d in range(CHIPS) for side in range(2)] + [dev % 2, dev]
+        for dev in range(2 * CHIPS)
+    ],
+    np.int32,
+)
+CORE, MINE = 2 * CHIPS, 2 * CHIPS + 1
+MARKS = np.broadcast_to(
+    np.array([[dev >> bit & 1 for bit in range(8)] for dev in range(2 * CHIPS)], np.int32)[:, :, None], (2 * CHIPS, 8, 128)
+)
+CLASS_ROWS = 160
+EXTRA = 24
+SUB_ROWS = 16
+LANE = 128
+
+
+def walk_perm(step):
+    return [
+        (WALK[p] * 2 + c, WALK[(p + step) % CHIPS] * 2 + c) for p in range(CHIPS) for c in range(2)
+    ]
+
+
+def flip_perm(bit):
+    return [(i, i ^ bit) for i in range(2 * CHIPS)]
+
+
+def send(value, perm):
+    return lax.ppermute(value, "ch", perm)
+
+
+FORTH, BACK, SIBLING = walk_perm(1), walk_perm(-1), flip_perm(1)
+VMEM = pl.BlockSpec(memory_space=pltpu.VMEM)
+SMEM = pl.BlockSpec(memory_space=pltpu.SMEM)
+
+
+def call(kernel, outs, ins, scratch=(), flops=0, moved=0, limit=40, name=None, after=(), out_spaces=None):
+    count = len(ins)
+
+    def body(*refs):
+        kernel(*refs[:count], *refs[count + len(after) :])
+
+    result = pl.pallas_call(
+        body,
+        out_shape=[jax.ShapeDtypeStruct(s, d) for s, d in outs],
+        in_specs=[s for _, s in ins] + [pl.BlockSpec(memory_space=pl.ANY)] * len(after),
+        out_specs=[pl.BlockSpec(memory_space=space) for space in out_spaces or [pltpu.VMEM] * len(outs)],
+        scratch_shapes=list(scratch),
+        compiler_params=pltpu.CompilerParams(vmem_limit_bytes=limit << 20),
+        cost_estimate=pl.CostEstimate(flops=int(flops), bytes_accessed=int(moved), transcendentals=0),
+        name=name,
+    )(*[a for a, _ in ins], *after)
+    return result
+
+
+def dot(a, b, dims):
+    return lax.dot_general(a, b, (dims, ((), ())), preferred_element_type=F32)
+
+
+def shifted_copies(grid_pad, copies):
+    for j in range(KS):
+        copies[j] = grid_pad[:, pl.ds(8 + j - HALF, WIN_W), :]
+
+
+def clear_border(grid_pad):
+    grid_pad[...] = jnp.zeros_like(grid_pad)
+
+
+def put_rows(grid_pad, row, tile):
+    grid_pad[pl.ds(row + HALF, 4), pl.ds(8, WIN_W), :] = tile.T.reshape(4, WIN_W, tile.shape[0])
+
+
+def conv_rows(copies, taps, row, flip):
+    acc = None
+    for j in range(KS):
+        for i in range(KS):
+            index = (KS - 1 - i) * KS + KS - 1 - j if flip else i * KS + j
+            term = taps[index : index + 1, :][None] * copies[j, pl.ds(row + i, 4)]
+            acc = term if acc is None else acc + term
+    return acc
+
+
+def conv_kernel(x_ref, taps, out_ref, grid_pad, copies):
+    clear_border(grid_pad)
+    for g in range(8):
+        put_rows(grid_pad, 4 * g, x_ref[:, g * LANE : (g + 1) * LANE].astype(F32))
+    shifted_copies(grid_pad, copies)
+    for g in range(8):
+        acc = conv_rows(copies, taps, 4 * g, False)
+        out_ref[:, g * LANE : (g + 1) * LANE] = acc.reshape(LANE, LANE).T.astype(BF)
+
+
+def copies_kernel(x_ref, copies, grid_pad):
+    clear_border(grid_pad)
+    for g in range(8):
+        put_rows(grid_pad, 4 * g, x_ref[:, g * LANE : (g + 1) * LANE].astype(F32))
+    shifted_copies(grid_pad, copies)
+
+
+def columns(places_ref, entry):
+    return pl.ds(pl.multiple_of(places_ref[entry] * LANE, LANE), LANE)
+
+
+def weights_kernel(places_ref, w_in_ref, gain_ref, own_ref, sib_ref, gain_sum_ref):
+    total = None
+    for d in range(CHIPS):
+        for side, out in enumerate((own_ref, sib_ref)):
+            at = columns(places_ref, 2 * d + side)
+            part = (w_in_ref[:, at].astype(F32) * gain_ref[:, at]).astype(BF)
+            out[:, d * LANE : (d + 1) * LANE] = part
+            wide = part.astype(F32)
+            total = wide if total is None else total + wide
+    gain_sum_ref[...] = jnp.sum(total, axis=1, keepdims=True)
+
+
+def mix_kernel(w_out_ref, scale_ref, head_ref, head_pad_ref, mix_ref):
+    head_pad_ref[...] = jnp.zeros_like(head_pad_ref)
+    head_pad_ref[0 : head_ref.shape[0], :] = head_ref[...]
+    head = head_pad_ref[...]
+    scaled = (head.astype(F32) * scale_ref[...]).astype(BF)
+    mix_ref[...] = dot(w_out_ref[...], scaled, ((1,), (1,))).astype(BF)
+
+
+def turn_kernel(own_ref, sib_ref, out_ref):
+    units = own_ref.shape[0]
+    out_ref[:, :units] = own_ref[...].T
+    out_ref[:, units:] = sib_ref[...].T
+
+
+def add_blocks(own_ref, sib_ref, held, ids, shift, sums):
+    away = held.astype(F32) - shift
+    first = jnp.sum(away, axis=0, keepdims=True)
+    second = jnp.sum(away * away, axis=0, keepdims=True)
+    if sums is not None:
+        first, second = sums[0] + first, sums[1] + second
+    pick = lambda ref: jnp.concatenate([ref[:, d * LANE : (d + 1) * LANE] for d in ids], axis=1)
+    return dot(pick(own_ref), held, ((1,), (0,))), dot(pick(sib_ref), held, ((1,), (0,))), first, second
+
+
+def first_kernel(ids, own_ref, sib_ref, *refs):
+    blocks, (acc_ref, give_ref, sums_ref) = refs[:-3], refs[-3:]
+    shift = jnp.mean(blocks[0][...].astype(F32), axis=0, keepdims=True)
+    held = jnp.concatenate([b[...] for b in blocks], axis=0)
+    acc, give, first, second = add_blocks(own_ref, sib_ref, held, ids, shift, None)
+    acc_ref[...] = acc
+    give_ref[...] = give
+    sums_ref[...] = jnp.concatenate([shift, first, second, jnp.zeros((5, shift.shape[1]), F32)], axis=0)
+
+
+def next_kernel(ids, own_ref, sib_ref, acc_in_ref, give_in_ref, sums_in_ref, *refs):
+    blocks, (acc_ref, give_ref, sums_ref) = refs[:-3], refs[-3:]
+    shift, first, second = sums_in_ref[0:1, :], sums_in_ref[1:2, :], sums_in_ref[2:3, :]
+    held = jnp.concatenate([b[...] for b in blocks], axis=0)
+    acc, give, first, second = add_blocks(own_ref, sib_ref, held, ids, shift, (first, second))
+    acc_ref[...] = acc_in_ref[...] + acc
+    give_ref[...] = (give_in_ref[...] + give).astype(give_ref.dtype)
+    sums_ref[...] = jnp.concatenate([shift, first, second, jnp.zeros((5, shift.shape[1]), F32)], axis=0)
+
+
+def pack_kernel(*refs):
+    refs[-1][...] = jnp.concatenate([ref[...] for ref in refs[:-1]], axis=0)
+
+
+def forward_kernel(places_ref, acc_ref, got_ref, sums_ref, sib_sums_ref, gain_sum_ref, mix_ref, head_ref, x_ref, own_ref, sib_ref, *refs):
+    blocks, (pre_ref, hidden_ref, stats_ref, keep_ref, give_ref, scratch) = refs[:-6], refs[-6:]
+    held = jnp.concatenate([b[...] for b in blocks], axis=0)
+    at = slice(CHIPS // 2 * LANE, (CHIPS // 2 + 1) * LANE)
+    acc = dot(jnp.concatenate([own_ref[:, at], sib_ref[:, at]], axis=1), held, ((1,), (0,)))
+    shift = sums_ref[0:1, :]
+    away = held.astype(F32) - shift
+    sets = [(held.shape[0], shift, jnp.sum(away, axis=0, keepdims=True), jnp.sum(away * away, axis=0, keepdims=True))]
+    sets += [((CHIPS - 1) * LANE, ref[0:1, :], ref[1:2, :], ref[2:3, :]) for ref in (sums_ref, sib_sums_ref)]
+    means = [base + first / count for count, base, first, _ in sets]
+    channels = 2 * CHIPS * LANE
+    tok_mean = sum(s[0] * mean for s, mean in zip(sets, means)) / channels
+    spread = sum(second - first * first / count + count * (mean - tok_mean) ** 2 for (count, _, first, second), mean in zip(sets, means))
+    inv_std = lax.rsqrt(spread / channels + norm_eps)
+    stats_ref[...] = jnp.concatenate([tok_mean, inv_std, jnp.zeros((6, tok_mean.shape[1]), F32)], axis=0)
+    pre_act = (acc + acc_ref[...] + got_ref[...].astype(F32) - gain_sum_ref[...] * tok_mean) * inv_std
+    pre_ref[...] = pre_act
+    hidden = (pre_act * (0.5 * (1.0 + lax.erf(pre_act * 0.7071067811865476)))).astype(BF)
+    hidden_ref[...] = hidden
+    my_head = head_ref[:, columns(places_ref, MINE)]
+    logits = dot(mix_ref[...], hidden, ((0,), (0,))) + dot(my_head, x_ref[...], ((1,), (0,)))
+    core = places_ref[CORE]
+    chunks = keep_ref.shape[0]
+    for g in range(2 * chunks):
+        scratch[g] = logits[:, g * LANE : (g + 1) * LANE]
+    keep_ref[...] = scratch[pl.ds(chunks * core, chunks)]
+    give_ref[...] = scratch[pl.ds(chunks - chunks * core, chunks)]
+
+
+def slope_kernel(pre_ref, stats_ref, slope_ref):
+    pre_act = pre_ref[...]
+    cum_prob = 0.5 * (1.0 + lax.erf(pre_act * 0.7071067811865476))
+    density = jnp.exp(-0.5 * pre_act * pre_act) * 0.3989422804014327
+    slope_ref[...] = (cum_prob + pre_act * density) * stats_ref[1:2, :]
+
+
+def fold_kernel(row, marks_ref, keep_ref, got_ref, kept_ref, give_ref):
+    bit = jnp.broadcast_to(marks_ref[row : row + 1, :], kept_ref.shape[-2:]) == 1
+    half = keep_ref.shape[0] // 2
+    for g in range(half):
+        low, high = keep_ref[g] + got_ref[g], keep_ref[half + g] + got_ref[half + g]
+        kept_ref[g] = jnp.where(bit, high, low)
+        give_ref[g] = jnp.where(bit, low, high)
+
+
+def add_kernel(a_ref, b_ref, out_ref):
+    out_ref[...] = a_ref[...] + b_ref[...]
+
+
+def softmax_kernel(classes, marks_ref, kept_ref, got_ref, labels_ref, grad_ref):
+    kept = kept_ref[0] + got_ref[0]
+    chunk = 4 * marks_ref[0:1, :] + 2 * marks_ref[1:2, :] + marks_ref[2:3, :]
+    labels = labels_ref[:, :LANE]
+    for g in range(1, labels_ref.shape[1] // LANE):
+        labels = jnp.where(chunk == g, labels_ref[:, g * LANE : (g + 1) * LANE], labels)
+    class_id = lax.broadcasted_iota(jnp.int32, kept.shape, 0)
+    kept = jnp.where(class_id < classes, kept, -jnp.inf)
+    col_max = jnp.max(kept, axis=0, keepdims=True)
+    exp_terms = jnp.exp(kept - col_max)
+    exp_total = jnp.sum(exp_terms, axis=0, keepdims=True)
+    onehot = class_id == labels
+    picked = jnp.sum(jnp.where(onehot, kept, 0.0), axis=0, keepdims=True)
+    loss = jnp.log(exp_total) + col_max - picked
+    loss_high = loss.astype(BF).astype(F32)
+    grad = exp_terms / exp_total - onehot.astype(F32)
+    grad = jnp.where(class_id == classes, loss_high, jnp.where(class_id == classes + 1, loss - loss_high, grad))
+    grad_ref[0] = grad.astype(BF)
+
+
+def join_kernel(row, marks_ref, own_ref, other_ref, out_ref):
+    bit = jnp.broadcast_to(marks_ref[row : row + 1, :], own_ref.shape[1:]) == 1
+    half = own_ref.shape[0]
+    for g in range(half):
+        own, other = own_ref[g].astype(F32), other_ref[g].astype(F32)
+        out_ref[g] = jnp.where(bit, other, own).astype(BF)
+        out_ref[half + g] = jnp.where(bit, own, other).astype(BF)
+
+
+def grad_kernel(places_ref, own_ref, sib_ref, mix_ref, slope_ref, pre_ref, gain_sum_ref, grad_ref, scaled_ref, means_ref):
+    core = places_ref[CORE]
+    chunks = own_ref.shape[0]
+    for g in range(chunks):
+        grad_ref[:, pl.ds(pl.multiple_of((core * chunks + g) * LANE, LANE), LANE)] = own_ref[g]
+        grad_ref[:, pl.ds(pl.multiple_of(((1 - core) * chunks + g) * LANE, LANE), LANE)] = sib_ref[g]
+    scaled = (dot(mix_ref[...], grad_ref[...], ((1,), (0,))) * slope_ref[...]).astype(BF)
+    scaled_ref[...] = scaled
+    wide = scaled.astype(F32)
+    mean_part = jnp.sum(wide * gain_sum_ref[...], axis=0, keepdims=True)
+    proj_part = jnp.sum(wide * pre_ref[...], axis=0, keepdims=True)
+    means_ref[...] = jnp.concatenate([mean_part, proj_part, jnp.zeros((SUB_ROWS - 2, wide.shape[1]), F32)], axis=0)
+
+
+def branch_kernel(places_ref, hidden_ref, grad_ref, w_out_ref, means_ref, mixed_ref, keep_ref, give_ref):
+    mixed = dot(hidden_ref[...], grad_ref[...], ((1,), (1,))).astype(BF)
+    mixed_ref[...] = mixed
+    for side, out in enumerate((keep_ref, give_ref)):
+        cols = jnp.concatenate([w_out_ref[:, columns(places_ref, 2 * d + side)] for d in range(CHIPS)], axis=1)
+        both = jnp.concatenate([dot(mixed, cols, ((0,), (0,))), means_ref[...]], axis=0)
+        out[...] = both.astype(out.dtype)
+
+
+def message_of(d, turned_ref, own_ref, got_ref, keep_ref, sib_ref):
+    units = own_ref.shape[0]
+    at = slice(d * LANE, (d + 1) * LANE)
+    rows = dot(turned_ref[at, :units], own_ref[...], ((1,), (0,))) + dot(turned_ref[at, units:], got_ref[...], ((1,), (0,)))
+    means = keep_ref[CLASS_ROWS:, :] + sib_ref[CLASS_ROWS:, :].astype(F32)
+    means = [means[n : n + 1, g * LANE : (g + 1) * LANE] for n in range(2) for g in range(8)]
+    means = jnp.concatenate(means + [jnp.zeros((EXTRA - 16, LANE), F32)], axis=0)
+    branch = keep_ref[:CLASS_ROWS, at] + sib_ref[:CLASS_ROWS, at].astype(F32)
+    branch = jnp.concatenate([branch, jnp.zeros((7 * EXTRA - CLASS_ROWS, LANE), F32)], axis=0)
+    extra = jnp.concatenate([branch[g * EXTRA : (g + 1) * EXTRA] for g in range(7)] + [means], axis=1)
+    return jnp.concatenate([rows, extra], axis=0)
+
+
+def message_kernel(ids, *refs):
+    for d, out in zip(ids, refs[-len(ids) :]):
+        out[...] = message_of(d, *refs[: -len(ids)])
+
+
+def far_kernel(*refs):
+    upper, lower = refs[-2:]
+    cut = upper.shape[0]
+    total = message_of(CHIPS // 2, *refs[:-2])
+    upper[...] = total[:cut].astype(BF)
+    lower[...] = total[cut:].astype(BF)
+
+
+def sum_kernel(ahead, behind, forth, back, ahead_out, behind_out):
+    ahead, behind = ahead[...], behind[...]
+    height, cut = ahead.shape[0], forth.shape[0]
+    if cut < height:
+        ahead_out[...] = jnp.concatenate([ahead[:cut] + forth[...].astype(F32), ahead[cut:]], axis=0).astype(BF)
+        behind_out[...] = jnp.concatenate([behind[:cut], behind[cut:] + back[...].astype(F32)], axis=0).astype(BF)
+    else:
+        ahead_out[...] = (ahead + forth[...].astype(F32)).astype(BF)
+        behind_out[...] = (behind + back[...].astype(F32)).astype(BF)
+
+
+def d_w_out_kernel(mixed_ref, head_ref, scale_ref, out_ref, done_ref, held, sems):
+    done_ref[...] = jnp.zeros_like(done_ref)
+    mixed = mixed_ref[...]
+    copies = []
+    for n in range(sems.shape[0]):
+        at = slice(n * held.shape[1] // sems.shape[0], (n + 1) * held.shape[1] // sems.shape[0])
+        held[:, at] = dot(mixed, head_ref[:, at], ((1,), (0,))) * scale_ref[:, at]
+        copies.append(pltpu.make_async_copy(held.at[:, at], out_ref.at[:, at], sems.at[n]))
+        copies[-1].start()
+    for copy in copies:
+        copy.wait()
+
+
+def d_w_in_kernel(places_ref, gain_ref, scaled_ref, stats_ref, own_ref, sib_ref, out_ref, done_ref, held, sems):
+    done_ref[...] = jnp.zeros_like(done_ref)
+    scaled = scaled_ref[...]
+    shift = jnp.sum(scaled.astype(F32) * stats_ref[0:1, :], axis=1, keepdims=True)
+    copies = []
+    for side, blocks in enumerate((own_ref, sib_ref)):
+        for n in range(0, CHIPS, 2):
+            both = dot(scaled, blocks[n * LANE : (n + 2) * LANE, :], ((1,), (1,))) - shift
+            for k in range(2):
+                at = columns(places_ref, 2 * (n + k) + side)
+                slot = len(copies)
+                held[slot] = both[:, k * LANE : (k + 1) * LANE] * gain_ref[:, at]
+                copies.append(pltpu.make_async_copy(held.at[slot], out_ref.at[:, at], sems.at[slot]))
+                copies[-1].start()
+    for copy in copies:
+        copy.wait()
+
+
+def head_kernel(classes, places_ref, x_ref, head_ref, grad_ref, out_grad_ref, d_head_ref, loss_ref):
+    my_head = head_ref[:, columns(places_ref, MINE)]
+    grad = grad_ref[...]
+    out_grad_ref[...] = dot(my_head, grad, ((0,), (0,)))
+    d_head_ref[...] = dot(grad, x_ref[...], ((1,), (1,)))
+    loss_ref[...] = (jnp.sum(grad[classes : classes + 2].astype(F32)) / grad.shape[1]).reshape(1, 1)
+
+
+def last_kernel(classes, places_ref, mine_ref, forth_ref, back_ref, conv_ref, stats_ref, taps, copies_x, out_grad_ref, head_grad_ref, head_ref, scale_ref,
+                d_x_ref, d_dw_ref, d_scale_ref, d_head_ref, grid_pad, copies, sums):
+    rows = conv_ref.shape[0]
+    channels = rows * 2 * CHIPS
+    got = mine_ref[...] + forth_ref[...].astype(F32) + back_ref[...].astype(F32)
+    extra = got[rows:]
+    branch = jnp.concatenate([extra[:, g * LANE : (g + 1) * LANE] for g in range(7)], axis=0)[:CLASS_ROWS]
+    means = extra[:, 7 * LANE :]
+    clear_border(grid_pad)
+    for g in range(8):
+        at = slice(g * LANE, (g + 1) * LANE)
+        normed = (conv_ref[:, at].astype(F32) - stats_ref[0:1, at]) * stats_ref[1:2, at]
+        conv_grad = got[:rows, at] - (means[g : g + 1, :] + normed * means[8 + g : 9 + g, :]) * (1.0 / channels)
+        put_rows(grid_pad, 4 * g, conv_grad)
+    shifted_copies(grid_pad, copies)
+    for g in range(8):
+        at = slice(g * LANE, (g + 1) * LANE)
+        d_x_ref[:, at] = out_grad_ref[:, at] + conv_rows(copies, taps, 4 * g, True).reshape(LANE, LANE).T
+    for g in range(8):
+        conv_grad = copies[HALF, pl.ds(4 * g + HALF, 4)]
+        for j in range(KS):
+            for i in range(KS):
+                prod = (conv_grad * copies_x[j, pl.ds(4 * g + i, 4)]).reshape(16, 8, LANE)
+                total = jnp.sum(prod, axis=0)
+                index = i * KS + j
+                if g == 0:
+                    sums[index] = total
+                else:
+                    sums[index] += total
+    d_dw_ref[...] = jnp.sum(sums[...], axis=1)
+    at = columns(places_ref, MINE)
+    d_scale_ref[...] = jnp.sum(head_ref[:, at].astype(F32) * branch, axis=0, keepdims=True)
+    d_head_ref[...] = (head_grad_ref[...] + scale_ref[:, at] * branch)[:classes]
+
+
+def walk_step(walk, step):
+    forth, back = walk[(1 - step) % CHIPS][0], walk[step - 1][0]
+    half = forth.shape[0] // 2
+    if step < CHIPS // 2:
+        walk[(-step) % CHIPS], walk[step] = (send(forth, FORTH),), (send(back, BACK),)
+    else:
+        walk[step] = (send(forth[:half], FORTH), send(back[half:], BACK))
+
+
+def hold(walk, step, *others):
+    spots = [((-step) % CHIPS), step]
+    held = lax.optimization_barrier((walk[spots[0]][0], walk[spots[1]][0], *others))
+    walk[spots[0]], walk[spots[1]] = (held[0],), (held[1],)
+    return held[2:]
+
+
+def per_device(features, dw_weight, norm_gain, layer_scale, w_in, w_out, w_head, labels):
+    rows, tokens = features.shape
+    units, channels = w_in.shape
+    classes = w_head.shape[1]
+    me = lax.axis_index("ch")
+    places = lax.dynamic_index_in_dim(jnp.asarray(PLACES), me, 0, keepdims=False)
+    marks = lax.dynamic_index_in_dim(jnp.asarray(MARKS), me, 0, keepdims=False)
+    taps = dw_weight.T
+    scale_row, gain_row, labels_row = layer_scale[None, :], norm_gain[None, :], labels[None, :]
+    grid_shape = pltpu.VMEM((WIN_H + 2 * HALF, WIN_W + 16, LANE), F32)
+    copies_size = (KS, WIN_H + 2 * HALF, WIN_W, LANE)
+    half_channels = CHIPS * rows
+    vm = lambda *arrays: [(a, VMEM) for a in arrays]
+    spot, mark = [(places, SMEM)], vm(marks)
+    f32s, bf16s, sums_size = ((units, tokens), F32), ((units, tokens), BF), ((8, tokens), F32)
+
+    (conv_out,) = call(
+        conv_kernel, [((rows, tokens), BF)], vm(features, taps), [grid_shape, pltpu.VMEM(copies_size, F32)], limit=12, name="conv_forward",
+        after=[places, marks],
+    )
+    walk = {0: (conv_out,)}
+    walk_step(walk, 1)
+    w_own, w_give, gain_sum = call(
+        weights_kernel,
+        [((units, half_channels), BF), ((units, half_channels), BF), ((units, 1), F32)],
+        spot + vm(w_in, gain_row), flops=4e8, moved=4e6, limit=12, name="weights_ready", after=[conv_out],
+    )
+    w_own, w_give, gain_sum = hold(walk, 1, w_own, w_give, gain_sum)
+    w_sib = send(w_give, SIBLING)
+    walk_step(walk, 2)
+    so_far = call(
+        functools.partial(first_kernel, (0, 1, 7)), [f32s, f32s, sums_size],
+        vm(w_own, w_sib, *walk[0], *walk[1], *walk[7]), flops=1e9, moved=4e6, limit=16, name="forward_first",
+    )
+    so_far = hold(walk, 2, *so_far)
+    walk_step(walk, 3)
+    head_pad, mix = call(
+        mix_kernel,
+        [((CLASS_ROWS, channels), BF), ((units, CLASS_ROWS), BF)],
+        vm(w_out, scale_row, w_head.T), flops=1e9, moved=4e6, limit=12, name="mix_ready", after=[so_far[2]],
+    )
+    so_far = call(
+        functools.partial(next_kernel, (2, 6)), [f32s, f32s, sums_size],
+        vm(w_own, w_sib, *so_far, *walk[2], *walk[6]), flops=6e8, moved=4e6, limit=16, name="forward_next",
+    )
+    *so_far, head_pad, mix = hold(walk, 3, *so_far, head_pad, mix)
+    walk_step(walk, 4)
+    acc, give, sums = call(
+        functools.partial(next_kernel, (3, 5)), [f32s, bf16s, sums_size],
+        vm(w_own, w_sib, *so_far, *walk[3], *walk[5]), flops=6e8, moved=4e6, limit=16, name="forward_next",
+    )
+    got, sib_sums = send(give, SIBLING), send(sums, SIBLING)
+    far = [*walk[4], *[send(b, SIBLING) for b in walk[4]]]
+    chunks = tokens // LANE // 2
+    chunk = lambda count, kind=F32: ((count, CLASS_ROWS, LANE), kind)
+    pre_act, hidden, stats, keep, give = call(
+        forward_kernel, [f32s, bf16s, sums_size, chunk(chunks), chunk(chunks)],
+        spot + vm(acc, got, sums, sib_sums, gain_sum, mix, head_pad, features, w_own, w_give, *far),
+        [pltpu.VMEM((2 * chunks, CLASS_ROWS, LANE), F32)], flops=1e9, moved=4e6, limit=16, name="forward_hidden",
+    )
+
+    kept, give = call(functools.partial(fold_kernel, 1), [chunk(2), chunk(2)], mark + vm(keep, send(give, SIBLING)), limit=4, name="fold_core")
+    (packed,) = call(
+        pack_kernel, [((half_channels, tokens), BF)], vm(*[b for d in range(CHIPS) for b in walk[d]]), flops=4e8, moved=4e6, limit=10, name="pack_blocks", after=[kept],
+    )
+    sib_packed = send(packed, SIBLING)
+    kept, give = call(functools.partial(fold_kernel, 2), [chunk(1), chunk(1)], mark + vm(kept, send(give, flip_perm(2))), limit=4, name="fold_y", after=[packed])
+    (slope,) = call(slope_kernel, [f32s], vm(pre_act, stats), flops=5e8, moved=4e6, limit=8, name="gelu_slope", after=[kept])
+    (kept,) = call(add_kernel, [chunk(1)], vm(kept, send(give, flip_perm(4))), limit=4, name="fold_z", after=[slope])
+    (turned,) = call(turn_kernel, [((half_channels, 2 * units), BF)], vm(w_own, w_sib), flops=4e8, moved=4e6, limit=10, name="weights_turned", after=[kept])
+    (grad,) = call(
+        functools.partial(softmax_kernel, classes), [chunk(1, BF)], mark + vm(kept, send(kept, flip_perm(8)), labels_row), limit=4, name="class_grad", after=[turned, sib_packed],
+    )
+    (copies_x,) = call(copies_kernel, [(copies_size, F32)], vm(features), [grid_shape], flops=4e8, moved=4e6, limit=12, name="window_copies", after=[grad])
+    (grad,) = call(functools.partial(join_kernel, 2), [chunk(2, BF)], mark + vm(grad, send(grad, flip_perm(4))), limit=4, name="join_z", after=[copies_x])
+    (grad,) = call(functools.partial(join_kernel, 1), [chunk(4, BF)], mark + vm(grad, send(grad, flip_perm(2))), limit=4, name="join_y")
+
+    grad, scaled, means = call(
+        grad_kernel, [((CLASS_ROWS, tokens), BF), bf16s, ((SUB_ROWS, tokens), F32)],
+        spot + vm(grad, send(grad, SIBLING), mix, slope, pre_act, gain_sum), flops=6e8, moved=4e6, limit=12, name="hidden_grad",
+    )
+    got = send(scaled, SIBLING)
+    extra_rows = CLASS_ROWS + SUB_ROWS
+    mixed, keep, give = call(
+        branch_kernel, [((units, CLASS_ROWS), BF), ((extra_rows, half_channels), F32), ((extra_rows, half_channels), BF)],
+        spot + vm(hidden, grad, w_out, means), flops=8e8, moved=4e6, limit=12, name="class_products",
+    )
+    sources = vm(turned, scaled, got, keep, send(give, SIBLING))
+    height = rows + EXTRA
+    cut = 80
+    forth, back = call(far_kernel, [((cut, tokens), BF), ((height - cut, tokens), BF)], sources, flops=3e8, moved=2e6, limit=8, name="message_far")
+    forth, back = send(forth, FORTH), send(back, BACK)
+    d_w_out, d_w_out_done = call(
+        d_w_out_kernel, [((units, channels), F32), ((8, LANE), F32)], vm(mixed, head_pad, scale_row),
+        [pltpu.VMEM((units, channels), F32), pltpu.SemaphoreType.DMA((4,))], flops=1e9, moved=8e6, limit=12, name="d_w_out", out_spaces=(pl.ANY, pltpu.VMEM),
+        after=[forth],
+    )
+    out_grad, head_grad, mean_loss = call(
+        functools.partial(head_kernel, classes), [((rows, tokens), F32), ((CLASS_ROWS, rows), F32), ((1, 1), F32)],
+        spot + vm(features, head_pad, grad), flops=4e8, moved=2e6, limit=8, name="class_head", after=[forth],
+    )
+    beside = {3: [], 2: [d_w_out_done, out_grad], 1: []}
+    for step in range(CHIPS // 2 - 1, 0, -1):
+        ahead, behind = call(
+            functools.partial(message_kernel, (step, CHIPS - step)), [((height, tokens), F32)] * 2, sources,
+            flops=6e8, moved=2e6, limit=8, name="messages",
+        )
+        forth, back = call(sum_kernel, [((height, tokens), BF)] * 2, vm(ahead, behind, forth, back), limit=6, name="walk_sum", after=beside[step])
+        if step == 2:
+            d_w_in, d_w_in_done = call(
+                d_w_in_kernel, [((units, channels), F32), ((8, LANE), F32)], spot + vm(gain_row, scaled, stats, packed, sib_packed),
+                [pltpu.VMEM((2 * CHIPS, units, LANE), F32), pltpu.SemaphoreType.DMA((2 * CHIPS,))],
+                flops=2e9, moved=8e6, limit=12, name="d_w_in", out_spaces=(pl.ANY, pltpu.VMEM), after=[forth],
+            )
+            beside[1] = [d_w_in_done]
+        forth, back = send(forth, FORTH), send(back, BACK)
+    (mine,) = call(functools.partial(message_kernel, (0,)), [((height, tokens), F32)], sources, flops=3e8, moved=2e6, limit=8, name="messages", after=[ahead])
+    d_features, d_dw, d_scale, d_head = call(
+        functools.partial(last_kernel, classes),
+        [((rows, tokens), F32), ((KS * KS, rows), F32), ((1, rows), F32), ((classes, rows), F32)],
+        spot + vm(mine, forth, back, conv_out, stats, taps, copies_x, out_grad, head_grad, head_pad, scale_row),
+        [grid_shape, pltpu.VMEM(copies_size, F32), pltpu.VMEM((KS * KS, 8, LANE), F32)], limit=16, name="conv_backward",
+    )
+    return (d_features, d_dw.T, d_scale[0], d_w_in, d_w_out, d_head.T, mean_loss[0])
 
 
 def conv_apply(in_grid, kernel):
@@ -32,7 +558,7 @@
     return (values * cum_prob, cum_prob + values * density)
 
 
-def per_device(features, dw_weight, norm_gain, layer_scale, w_in, w_out, w_head, labels):
+def plain_device(features, dw_weight, norm_gain, layer_scale, w_in, w_out, w_head, labels):
     highest = lax.Precision.HIGHEST
     my_rows = features.shape[0]
     tok_count = features.shape[1]
@@ -82,7 +608,6 @@
     d_scale = jnp.sum(out_grad * branch_sum, axis=1)
     branch_grad = (my_scale[:, None] * out_grad).astype(jnp.bfloat16)
     incoming = lax.all_gather(branch_grad, "ch", axis=0, tiled=True)
-    w_cols = w_out
     hidden_acc = jnp.dot(w_cols, incoming, preferred_element_type=jnp.float32)
     tile_grad = lax.dot_general(
         hidden, incoming, (((1,), (1,)), ((), ())), preferred_element_type=jnp.float32
@@ -110,7 +635,7 @@
 def solution(mesh):
     placed = (P("ch", "grp"), P("ch", None), P(), P(), P("ch", None), P("ch", None), P(), P("grp"))
     return jax.shard_map(
-        per_device,
+        per_device if mesh.shape["ch"] == 2 * CHIPS else plain_device,
         mesh=mesh,
         in_specs=placed,
         out_specs=(

time: 498 us -> 123 us (0.25)
  waiting for transfers between devices: 392 us -> 55.7 us
  other arithmetic: 44 us -> 0 us
  matrix products: 35 us -> 0 us
  Pallas kernels: 0 us -> 33.5 us
  starting transfers between devices: 0.39 us -> 26.7 us
  between operations: 16.2 us -> 0.9 us
    reduce_scatter x2 -> x0, waiting for transfers between devices: 191 us -> none  [the longest x1 102 us: per_device(): lax.psum_scatter(lax.dot_general(w_cols, hidden, (((0,), (0,)), ((), ()))...]
    all_gather x2 -> x0, waiting for transfers between devices: 110 us -> none  [the longest x1 56 us: per_device(): conv_all = lax.all_gather(conv_out, 'ch', axis=0, tiled=True)]
    psum x1 -> x0, waiting for transfers between devices: 91.7 us -> none  [per_device(): logits = lax.psum(part_logits, 'ch')]
    ppermute x0 -> x31, waiting for transfers between devices: none -> 55.7 us  [send(): return lax.ppermute(value, 'ch', perm)]
    dot_general x9 -> x0, matrix products: 35 us -> none  [the longest x1 7.36 us: per_device(): lax.dot_general(pre_grad, norm_out, (((1,), (1,)), ((), ())), preferred_e...]
    pallas_call x0 -> x31, Pallas kernels: none -> 33.5 us  [call(): pl.pallas_call(body, out_shape=[jax.ShapeDtypeStruct(s, d) for s, d in ou...]
    ppermute x0 -> x31, starting transfers between devices: none -> 26.7 us  [send(): return lax.ppermute(value, 'ch', perm)]
    reduce_sum x10 -> x0, other arithmetic: 12.7 us -> none  [the longest x4 3.6 us: conv_apply(): tap[:, None, None]]
  transfers between devices with their start and end apart: 5 -> 31, of which waited for: 5 -> 25; matrix products, arithmetic and copies ran while one was open for 3% -> 0% of each run, Pallas kernels for 0% -> 15%
where the time goes in v2:
time: 123 us; the launch traced here: 122 us
  waiting for transfers between devices  55.7 us (45%)
  Pallas kernels  33.5 us (27%)
  starting transfers between devices  26.7 us (22%)
  local copies, waits for them, and re-layouts  5.49 us (4%)
    ppermute x31, waiting for transfers between devices, send(): return lax.ppermute(value, 'ch', perm)  55.7 us
    pallas_call x31, Pallas kernels, call(): pl.pallas_call(body, out_shape=[jax.ShapeDtypeStruct(s, d) for s, d in ou...  33.5 us
    ppermute x31, starting transfers between devices, send(): return lax.ppermute(value, 'ch', perm)  26.7 us
    unnamed x22, local copies, waits for them, and re-layouts  4.01 us
  transfers between devices with their start and end apart: 31, of which 25 were waited for; matrix products, arithmetic and copies ran while one was open for 0% of the time, Pallas kernels for 15%

profile of v2, /device:TPU:0, one launch (start us, length us, event | category | flops | bytes accessed | tf_op | source)
XLA Modules:
  0.0 122.3 jit_solution(695475464075637381)
XLA Ops:
  3.8 2.5 %conv_forward.1.refs_3_.refs_2_.refs_0_.refs_4_ = bf16[128,1024]{1,0:T(8,128)(2,1)S(1)} custom-call(bf16[128,1024]{1,0:T(8,128)(2,1)S(1)} %copy-done, f32[49,128]{1,0:T(8,128)S(1)} %bitcast.13, s32[18]{0:T(128)S(1)} %dynamic-slice_bitcast_fusion.1.refs_2_.refs_0_, s32[8,128]{1,0:T(8,128)S(1)} %broadcast.2.refs_3_.refs_0_), custom_call_target="tpu_custom_call" | custom-call | tf_op jit(solution)/shard_map/conv_forward/pallas_call | solution.py:65
  6.3 3.0 %collective-permute-start.1 = (bf16[128,1024]{1,0:T(8,128)(2,1)S(1)}, bf16[128,1024]{1,0:T(8,128)(2,1)S(1)}, u32[]{:S(2)}, u32[]{:S(2)}) collective-permute-start(bf16[128,1024]{1,0:T(8,128)(2,1)S(1)} %conv_forward.1.refs_3_.refs_2_.refs_0_.refs_4_), channel_id=1, source_target_pairs={{0,2},{1,3},{4,0},{5,1},{8,4},{9,5},{12,8},{13,9},{14,12},{15,13},... | collective-permute-start | bytes 786440 | tf_op jit(solution)/shard_map/ppermute | solution.py:51
  9.5 1.6 %copy-done.2 = bf16[512,2048]{1,0:T(8,128)(2,1)S(1)} copy-done((bf16[512,2048]{1,0:T(8,128)(2,1)S(1)}, bf16[512,2048]{1,0:T(8,128)(2,1)}, u32[]{:S(2)}) %copy-start.2) | copy-done | bytes 2097176
  13.1 2.6 %collective-permute-done.1.refs_3_.refs_1_ = bf16[128,1024]{1,0:T(8,128)(2,1)S(1)} collective-permute-done((bf16[128,1024]{1,0:T(8,128)(2,1)S(1)}, bf16[128,1024]{1,0:T(8,128)(2,1)S(1)}, u32[]{:S(2)}, u32[]{:S(2)}) %collective-permute-start.1) | collective-permute-done | bytes 262176 | tf_op jit(solution)/shard_map/ppermute | solution.py:51
  17.5 1.6 %collective-permute-start.4 = (bf16[128,1024]{1,0:T(8,128)(2,1)S(1)}, bf16[128,1024]{1,0:T(8,128)(2,1)S(1)}, u32[]{:S(2)}, u32[]{:S(2)}) collective-permute-start(bf16[128,1024]{1,0:T(8,128)(2,1)S(1)} %collective-permute-done.1.refs_3_.refs_1_), channel_id=1, source_target_pairs={{0,2},{1,3},{4,0},{5,1},{8,4},{9,5},{12,8},{13,9},{14,12},{15,13},... | collective-permute-start | bytes 786440 | tf_op jit(solution)/shard_map/ppermute | solution.py:51
  21.2 4.7 %collective-permute-done.3.refs_6_.refs_7_ = bf16[128,1024]{1,0:T(8,128)(2,1)S(1)} collective-permute-done((bf16[128,1024]{1,0:T(8,128)(2,1)S(1)}, bf16[128,1024]{1,0:T(8,128)(2,1)S(1)}, u32[]{:S(2)}, u32[]{:S(2)}) %collective-permute-start.3) | collective-permute-done | bytes 262176 | tf_op jit(solution)/shard_map/ppermute | solution.py:51
  26.0 1.7 %collective-permute-start.5 = (bf16[128,1024]{1,0:T(8,128)(2,1)S(1)}, bf16[128,1024]{1,0:T(8,128)(2,1)S(1)}, u32[]{:S(2)}, u32[]{:S(2)}) collective-permute-start(bf16[128,1024]{1,0:T(8,128)(2,1)S(1)} %collective-permute-done.3.refs_6_.refs_7_), channel_id=1, source_target_pairs={{0,4},{1,5},{4,8},{5,9},{8,12},{9,13},{12,14},{13,15},{14,10},{15,... | collective-permute-start | bytes 786440 | tf_op jit(solution)/shard_map/ppermute | solution.py:51
  29.6 4.3 %collective-permute-done.5.refs_6_ = bf16[128,1024]{1,0:T(8,128)(2,1)S(1)} collective-permute-done((bf16[128,1024]{1,0:T(8,128)(2,1)S(1)}, bf16[128,1024]{1,0:T(8,128)(2,1)S(1)}, u32[]{:S(2)}, u32[]{:S(2)}) %collective-permute-start.5) | collective-permute-done | bytes 262176 | tf_op jit(solution)/shard_map/ppermute | solution.py:51
  35.9 1.6 %collective-permute-start.9 = (bf16[64,1024]{1,0:T(8,128)(2,1)S(1)}, bf16[64,1024]{1,0:T(8,128)(2,1)S(1)}, u32[]{:S(2)}, u32[]{:S(2)}) collective-permute-start(bf16[64,1024]{1,0:T(8,128)(2,1)S(1)} %slice.6), channel_id=1, source_target_pairs={{0,4},{1,5},{4,8},{5,9},{8,12},{9,13},{12,14},{13,15},{14,10},{15,... | collective-permute-start | bytes 393224 | tf_op jit(solution)/shard_map/ppermute | solution.py:51
  38.2 3.6 %collective-permute-done.9.refs_11_.refs_4_ = bf16[64,1024]{1,0:T(8,128)(2,1)S(1)} collective-permute-done((bf16[64,1024]{1,0:T(8,128)(2,1)S(1)}, bf16[64,1024]{1,0:T(8,128)(2,1)S(1)}, u32[]{:S(2)}, u32[]{:S(2)}) %collective-permute-start.9) | collective-permute-done | bytes 131104 | tf_op jit(solution)/shard_map/ppermute | solution.py:51
  41.8 1.5 %collective-permute-done.10.refs_12_.refs_5_ = bf16[64,1024]{1,0:T(8,128)(2,1)S(1)} collective-permute-done((bf16[64,1024]{1,0:T(8,128)(2,1)S(1)}, bf16[64,1024]{1,0:T(8,128)(2,1)S(1)}, u32[]{:S(2)}, u32[]{:S(2)}) %collective-permute-start.10) | collective-permute-done | bytes 131104 | tf_op jit(solution)/shard_map/ppermute | solution.py:51
  44.8 2.1 %forward_hidden.1 = (f32[512,1024]{1,0:T(8,128)S(1)}, bf16[512,1024]{1,0:T(8,128)(2,1)S(1)}, f32[8,1024]{1,0:T(8,128)S(1)}, f32[4,160,128]{2,1,0:T(8,128)S(1)}, f32[4,160,128]{2,1,0:T(8,128)S(1)}) custom-call(s32[18]{0:T(128)S(1)} %dynamic-slice_bitcast_fusion.1.refs_2_.refs_0_, f32[512,1024]{1,0:T(8,128)S(1)} %get-tuple-element.103.refs_1_, ...), custom_call_target="tpu_custom_call" | custom-call | flops 1000000000 | bytes 4000000 | tf_op jit(solution)/shard_map/forward_hidden/pallas_call | solution.py:65
  49.6 5.8 %collective-permute-done.14.refs_2_ = f32[2,160,128]{2,1,0:T(8,128)S(1)} collective-permute-done((f32[2,160,128]{2,1,0:T(8,128)S(1)}, f32[2,160,128]{2,1,0:T(8,128)S(1)}, u32[]{:S(2)}, u32[]{:S(2)}) %collective-permute-start.14) | collective-permute-done | bytes 163872 | tf_op jit(solution)/shard_map/ppermute | solution.py:51
  55.5 1.6 %collective-permute-start.15 = (f32[1,160,128]{2,1,0:T(8,128)S(1)}, f32[1,160,128]{2,1,0:T(8,128)S(1)}, u32[]{:S(2)}, u32[]{:S(2)}) collective-permute-start(f32[1,160,128]{2,1,0:T(8,128)S(1)} %get-tuple-element.114), channel_id=1, source_target_pairs={{0,4},{1,5},{2,6},{3,7},{4,0},{5,1},{6,2},{7,3},{8,12},{9,13},{10,... | collective-permute-start | bytes 245768 | tf_op jit(solution)/shard_map/ppermute | solution.py:51
  58.0 2.0 %collective-permute-done.15.refs_1_ = f32[1,160,128]{2,1,0:T(8,128)S(1)} collective-permute-done((f32[1,160,128]{2,1,0:T(8,128)S(1)}, f32[1,160,128]{2,1,0:T(8,128)S(1)}, u32[]{:S(2)}, u32[]{:S(2)}) %collective-permute-start.15) | collective-permute-done | bytes 81952 | tf_op jit(solution)/shard_map/ppermute | solution.py:51
  60.0 2.6 %collective-permute-start.16 = (f32[1,160,128]{2,1,0:T(8,128)S(1)}, f32[1,160,128]{2,1,0:T(8,128)S(1)}, u32[]{:S(2)}, u32[]{:S(2)}) collective-permute-start(f32[1,160,128]{2,1,0:T(8,128)S(1)} %fold_z.1.refs_2_.refs_1_), channel_id=1, source_target_pairs={{0,8},{1,9},{2,10},{3,11},{4,12},{5,13},{6,14},{7,15},{8,0},{9,1},... | collective-permute-start | bytes 245768 | tf_op jit(solution)/shard_map/ppermute | solution.py:51
  63.3 2.2 %collective-permute-done.16.refs_2_ = f32[1,160,128]{2,1,0:T(8,128)S(1)} collective-permute-done((f32[1,160,128]{2,1,0:T(8,128)S(1)}, f32[1,160,128]{2,1,0:T(8,128)S(1)}, u32[]{:S(2)}, u32[]{:S(2)}) %collective-permute-start.16) | collective-permute-done | bytes 81952 | tf_op jit(solution)/shard_map/ppermute | solution.py:51
  65.5 1.6 %collective-permute-start.18 = (bf16[1,160,128]{2,1,0:T(8,128)(2,1)S(1)}, bf16[1,160,128]{2,1,0:T(8,128)(2,1)S(1)}, u32[]{:S(2)}, u32[]{:S(2)}) collective-permute-start(bf16[1,160,128]{2,1,0:T(8,128)(2,1)S(1)} %class_grad.1.refs_1_), channel_id=1, source_target_pairs={{0,4},{1,5},{2,6},{3,7},{4,0},{5,1},{6,2},{7,3},{8,12},{9,13},{10,... | collective-permute-start | bytes 122888 | tf_op jit(solution)/shard_map/ppermute | solution.py:51
  67.7 1.9 %collective-permute-done.18.refs_2_ = bf16[1,160,128]{2,1,0:T(8,128)(2,1)S(1)} collective-permute-done((bf16[1,160,128]{2,1,0:T(8,128)(2,1)S(1)}, bf16[1,160,128]{2,1,0:T(8,128)(2,1)S(1)}, u32[]{:S(2)}, u32[]{:S(2)}) %collective-permute-start.18) | collective-permute-done | bytes 40992 | tf_op jit(solution)/shard_map/ppermute | solution.py:51
  70.1 4.0 %collective-permute-done.19.refs_2_ = bf16[2,160,128]{2,1,0:T(8,128)(2,1)S(1)} collective-permute-done((bf16[2,160,128]{2,1,0:T(8,128)(2,1)S(1)}, bf16[2,160,128]{2,1,0:T(8,128)(2,1)S(1)}, u32[]{:S(2)}, u32[]{:S(2)}) %collective-permute-start.19) | collective-permute-done | bytes 81952 | tf_op jit(solution)/shard_map/ppermute | solution.py:51
  77.2 2.0 %class_products.1 = (bf16[512,160]{1,0:T(8,128)(2,1)S(1)}, f32[176,1024]{1,0:T(8,128)S(1)}, bf16[176,1024]{1,0:T(8,128)(2,1)S(1)}) custom-call(s32[18]{0:T(128)S(1)} %dynamic-slice_bitcast_fusion.1.refs_2_.refs_0_, bf16[512,1024]{1,0:T(8,128)(2,1)S(1)} %get-tuple-element.118.refs_1_, bf16[160,1024]{1,0:T(8,128)(2,1)S(1)} %get-tuple-element.119.refs_2_.refs_3_, ...), custom_call_target="tpu_custom_call" | custom-call | flops 800000000 | bytes 4000000 | tf_op jit(solution)/shard_map/class_products/pallas_call | solution.py:65
  81.4 1.6 %collective-permute-start.23 = (bf16[80,1024]{1,0:T(8,128)(2,1)S(1)}, bf16[80,1024]{1,0:T(8,128)(2,1)S(1)}, u32[]{:S(2)}, u32[]{:S(2)}) collective-permute-start(bf16[80,1024]{1,0:T(8,128)(2,1)S(1)} %get-tuple-element.129), channel_id=1, source_target_pairs={{0,4},{1,5},{4,8},{5,9},{8,12},{9,13},{12,14},{13,15},{14,10},{15,... | collective-permute-start | bytes 491528 | tf_op jit(solution)/shard_map/ppermute | solution.py:51
  84.2 4.7 %collective-permute-done.24.refs_3_ = bf16[72,1024]{1,0:T(8,128)(2,1)S(1)} collective-permute-done((bf16[72,1024]{1,0:T(8,128)(2,1)S(1)}, bf16[72,1024]{1,0:T(8,128)(2,1)S(1)}, u32[]{:S(2)}, u32[]{:S(2)}) %collective-permute-start.24) | collective-permute-done | bytes 147488 | tf_op jit(solution)/shard_map/ppermute | solution.py:51
  89.0 1.8 %collective-permute-start.25 = (bf16[152,1024]{1,0:T(8,128)(2,1)S(1)}, bf16[152,1024]{1,0:T(8,128)(2,1)S(1)}, u32[]{:S(2)}, u32[]{:S(2)}) collective-permute-start(bf16[152,1024]{1,0:T(8,128)(2,1)S(1)} %get-tuple-element.131), channel_id=1, source_target_pairs={{0,4},{1,5},{4,8},{5,9},{8,12},{9,13},{12,14},{13,15},{14,10},{15,... | collective-permute-start | bytes 933896 | tf_op jit(solution)/shard_map/ppermute | solution.py:51
  93.2 2.3 %d_w_out.1 = (f32[512,2048]{1,0:T(8,128)}, f32[8,128]{1,0:T(8,128)S(1)}) custom-call(bf16[512,160]{1,0:T(8,128)(2,1)S(1)} %get-tuple-element.133.refs_0_, bf16[160,2048]{1,0:T(8,128)(2,1)S(1)} %get-tuple-element.108.refs_7_.refs_1_.refs_2_.refs_10_, f32[1,2048]{1,0:T(1,128)S(1)} %bitcast.16, bf16[80,1024]{1,0:T(8,128)(2,1)S(1)} %collective-permute-done.23.refs_2_.refs_3_.refs_4_), custom_call_target="tpu_custom_call" | custom-call | flops 1000000000 | bytes 8000000 | tf_op jit(solution)/shard_map/d_w_out/pallas_call | solution.py:65
  95.5 2.1 %collective-permute-done.25.refs_2_ = bf16[152,1024]{1,0:T(8,128)(2,1)S(1)} collective-permute-done((bf16[152,1024]{1,0:T(8,128)(2,1)S(1)}, bf16[152,1024]{1,0:T(8,128)(2,1)S(1)}, u32[]{:S(2)}, u32[]{:S(2)}) %collective-permute-start.25) | collective-permute-done | bytes 311328 | tf_op jit(solution)/shard_map/ppermute | solution.py:51
  99.6 1.7 %collective-permute-start.27 = (bf16[152,1024]{1,0:T(8,128)(2,1)S(1)}, bf16[152,1024]{1,0:T(8,128)(2,1)S(1)}, u32[]{:S(2)}, u32[]{:S(2)}) collective-permute-start(bf16[152,1024]{1,0:T(8,128)(2,1)S(1)} %get-tuple-element.136.refs_6_), channel_id=1, source_target_pairs={{0,4},{1,5},{4,8},{5,9},{8,12},{9,13},{12,14},{13,15},{14,10},{15,... | collective-permute-start | bytes 933896 | tf_op jit(solution)/shard_map/ppermute | solution.py:51
  102.0 4.3 %d_w_in.1 = (f32[512,2048]{1,0:T(8,128)}, f32[8,128]{1,0:T(8,128)S(1)}) custom-call(s32[18]{0:T(128)S(1)} %dynamic-slice_bitcast_fusion.1.refs_2_.refs_0_, f32[1,2048]{1,0:T(1,128)S(1)} %bitcast.19, bf16[512,1024]{1,0:T(8,128)(2,1)S(1)} %get-tuple-element.117.refs_1_.refs_2_, f32[8,1024]{1,0:T(8,128)S(1)} %get-tuple-element.116.refs_1_.refs_3_.refs_5_, ...), custom_call_target="tpu_custom_call" | custom-call | flops 2000000000 | bytes 8000000 | tf_op jit(solution)/shard_map/d_w_in/pallas_call | solution.py:65
  107.1 1.6 %collective-permute-start.29 = (bf16[152,1024]{1,0:T(8,128)(2,1)S(1)}, bf16[152,1024]{1,0:T(8,128)(2,1)S(1)}, u32[]{:S(2)}, u32[]{:S(2)}) collective-permute-start(bf16[152,1024]{1,0:T(8,128)(2,1)S(1)} %get-tuple-element.139), channel_id=1, source_target_pairs={{0,4},{1,5},{4,8},{5,9},{8,12},{9,13},{12,14},{13,15},{14,10},{15,... | collective-permute-start | bytes 933896 | tf_op jit(solution)/shard_map/ppermute | solution.py:51
  109.6 4.4 %collective-permute-done.29.refs_2_ = bf16[152,1024]{1,0:T(8,128)(2,1)S(1)} collective-permute-done((bf16[152,1024]{1,0:T(8,128)(2,1)S(1)}, bf16[152,1024]{1,0:T(8,128)(2,1)S(1)}, u32[]{:S(2)}, u32[]{:S(2)}) %collective-permute-start.29) | collective-permute-done | bytes 311328 | tf_op jit(solution)/shard_map/ppermute | solution.py:51
  114.0 1.5 %collective-permute-done.30.refs_3_ = bf16[152,1024]{1,0:T(8,128)(2,1)S(1)} collective-permute-done((bf16[152,1024]{1,0:T(8,128)(2,1)S(1)}, bf16[152,1024]{1,0:T(8,128)(2,1)S(1)}, u32[]{:S(2)}, u32[]{:S(2)}) %collective-permute-start.30) | collective-permute-done | bytes 311328 | tf_op jit(solution)/shard_map/ppermute | solution.py:51
  115.6 6.8 %conv_backward.1 = (f32[128,1024]{1,0:T(8,128)}, f32[49,128]{1,0:T(8,128)}, f32[1,128]{1,0:T(1,128)}, f32[150,128]{1,0:T(8,128)}) custom-call(s32[18]{0:T(128)S(1)} %dynamic-slice_bitcast_fusion.1.refs_2_.refs_0_, f32[152,1024]{1,0:T(8,128)S(1)} %messages.5.refs_1_, bf16[152,1024]{1,0:T(8,128)(2,1)S(1)} %collective-permute-done.29.refs_2_, ...), custom_call_target="tpu_custom_call" | custom-call | tf_op jit(solution)/shard_map/conv_backward/pallas_call | solution.py:65
  (88 shorter events, 33.9 us)
Async XLA Ops:
  6.3 9.4 %collective-permute-start.1 = (bf16[128,1024]{1,0:T(8,128)(2,1)S(1)}, bf16[128,1024]{1,0:T(8,128)(2,1)S(1)}, u32[]{:S(2)}, u32[]{:S(2)}) collective-permute-start(bf16[128,1024]{1,0:T(8,128)(2,1)S(1)} %conv_forward.1.refs_3_.refs_2_.refs_0_.refs_4_), channel_id=1, source_target_pairs={{0,2},{1,3},{4,0},{5,1},{8,4},{9,5},{12,8},{13,9},{14,12},{15,13},... | collective-permute-start | bytes 786440 | tf_op jit(solution)/shard_map/ppermute | solution.py:51
  9.4 7.8 %collective-permute-start = (bf16[128,1024]{1,0:T(8,128)(2,1)S(1)}, bf16[128,1024]{1,0:T(8,128)(2,1)S(1)}, u32[]{:S(2)}, u32[]{:S(2)}) collective-permute-start(bf16[128,1024]{1,0:T(8,128)(2,1)S(1)} %conv_forward.1.refs_3_.refs_2_.refs_0_.refs_4_), channel_id=1, source_target_pairs={{0,4},{1,5},{4,8},{5,9},{8,12},{9,13},{12,14},{13,15},{14,10},{15,... | collective-permute-start | bytes 786440 | tf_op jit(solution)/shard_map/ppermute | solution.py:51
  17.1 2.7 %collective-permute-start.2 = (bf16[512,1024]{1,0:T(8,128)(2,1)S(1)}, bf16[512,1024]{1,0:T(8,128)(2,1)S(1)}, u32[]{:S(2)}, u32[]{:S(2)}) collective-permute-start(bf16[512,1024]{1,0:T(8,128)(2,1)S(1)} %get-tuple-element.82.refs_10_), channel_id=1, source_target_pairs={{0,1},{1,0},{2,3},{3,2},{4,5},{5,4},{6,7},{7,6},{8,9},{9,8},{10,11... | collective-permute-start | bytes 3145736 | tf_op jit(solution)/shard_map/ppermute | solution.py:51
  17.1 8.7 %collective-permute-start.3 = (bf16[128,1024]{1,0:T(8,128)(2,1)S(1)}, bf16[128,1024]{1,0:T(8,128)(2,1)S(1)}, u32[]{:S(2)}, u32[]{:S(2)}) collective-permute-start(bf16[128,1024]{1,0:T(8,128)(2,1)S(1)} %collective-permute-done.refs_4_.refs_8_), channel_id=1, source_target_pairs={{0,4},{1,5},{4,8},{5,9},{8,12},{9,13},{12,14},{13,15},{14,10},{15,... | collective-permute-start | bytes 786440 | tf_op jit(solution)/shard_map/ppermute | solution.py:51
  17.5 8.4 %collective-permute-start.4 = (bf16[128,1024]{1,0:T(8,128)(2,1)S(1)}, bf16[128,1024]{1,0:T(8,128)(2,1)S(1)}, u32[]{:S(2)}, u32[]{:S(2)}) collective-permute-start(bf16[128,1024]{1,0:T(8,128)(2,1)S(1)} %collective-permute-done.1.refs_3_.refs_1_), channel_id=1, source_target_pairs={{0,2},{1,3},{4,0},{5,1},{8,4},{9,5},{12,8},{13,9},{14,12},{15,13},... | collective-permute-start | bytes 786440 | tf_op jit(solution)/shard_map/ppermute | solution.py:51
  26.0 7.9 %collective-permute-start.5 = (bf16[128,1024]{1,0:T(8,128)(2,1)S(1)}, bf16[128,1024]{1,0:T(8,128)(2,1)S(1)}, u32[]{:S(2)}, u32[]{:S(2)}) collective-permute-start(bf16[128,1024]{1,0:T(8,128)(2,1)S(1)} %collective-permute-done.3.refs_6_.refs_7_), channel_id=1, source_target_pairs={{0,4},{1,5},{4,8},{5,9},{8,12},{9,13},{12,14},{13,15},{14,10},{15,... | collective-permute-start | bytes 786440 | tf_op jit(solution)/shard_map/ppermute | solution.py:51
  27.7 7.3 %collective-permute-start.6 = (bf16[128,1024]{1,0:T(8,128)(2,1)S(1)}, bf16[128,1024]{1,0:T(8,128)(2,1)S(1)}, u32[]{:S(2)}, u32[]{:S(2)}) collective-permute-start(bf16[128,1024]{1,0:T(8,128)(2,1)S(1)} %collective-permute-done.4.refs_5_.refs_2_), channel_id=1, source_target_pairs={{0,2},{1,3},{4,0},{5,1},{8,4},{9,5},{12,8},{13,9},{14,12},{15,13},... | collective-permute-start | bytes 786440 | tf_op jit(solution)/shard_map/ppermute | solution.py:51
  35.0 9.8 %copy-start.1 = (bf16[128,1024]{1,0:T(8,128)(2,1)S(1)}, bf16[128,1024]{1,0:T(8,128)(2,1)}, u32[]{:S(2)}) copy-start(bf16[128,1024]{1,0:T(8,128)(2,1)} %refs_1_.3) | copy-start | bytes 786436
  35.8 9.0 %collective-permute-start.7 = (bf16[512,1024]{1,0:T(8,128)(2,1)S(1)}, bf16[512,1024]{1,0:T(8,128)(2,1)S(1)}, u32[]{:S(2)}, u32[]{:S(2)}) collective-permute-start(bf16[512,1024]{1,0:T(8,128)(2,1)S(1)} %get-tuple-element.104), channel_id=1, source_target_pairs={{0,1},{1,0},{2,3},{3,2},{4,5},{5,4},{6,7},{7,6},{8,9},{9,8},{10,11... | collective-permute-start | bytes 3145736 | tf_op jit(solution)/shard_map/ppermute | solution.py:51
  35.9 5.9 %collective-permute-start.9 = (bf16[64,1024]{1,0:T(8,128)(2,1)S(1)}, bf16[64,1024]{1,0:T(8,128)(2,1)S(1)}, u32[]{:S(2)}, u32[]{:S(2)}) collective-permute-start(bf16[64,1024]{1,0:T(8,128)(2,1)S(1)} %slice.6), channel_id=1, source_target_pairs={{0,4},{1,5},{4,8},{5,9},{8,12},{9,13},{12,14},{13,15},{14,10},{15,... | collective-permute-start | bytes 393224 | tf_op jit(solution)/shard_map/ppermute | solution.py:51
  37.5 5.8 %collective-permute-start.10 = (bf16[64,1024]{1,0:T(8,128)(2,1)S(1)}, bf16[64,1024]{1,0:T(8,128)(2,1)S(1)}, u32[]{:S(2)}, u32[]{:S(2)}) collective-permute-start(bf16[64,1024]{1,0:T(8,128)(2,1)S(1)} %slice.7), channel_id=1, source_target_pairs={{0,2},{1,3},{4,0},{5,1},{8,4},{9,5},{12,8},{13,9},{14,12},{15,13},... | collective-permute-start | bytes 393224 | tf_op jit(solution)/shard_map/ppermute | solution.py:51
  41.8 2.9 %collective-permute-start.11 = (bf16[64,1024]{1,0:T(8,128)(2,1)S(1)}, bf16[64,1024]{1,0:T(8,128)(2,1)S(1)}, u32[]{:S(2)}, u32[]{:S(2)}) collective-permute-start(bf16[64,1024]{1,0:T(8,128)(2,1)S(1)} %collective-permute-done.9.refs_11_.refs_4_), channel_id=1, source_target_pairs={{0,1},{1,0},{2,3},{3,2},{4,5},{5,4},{6,7},{7,6},{8,9},{9,8},{10,11... | collective-permute-start | bytes 393224 | tf_op jit(solution)/shard_map/ppermute | solution.py:51
  43.4 1.4 %collective-permute-start.12 = (bf16[64,1024]{1,0:T(8,128)(2,1)S(1)}, bf16[64,1024]{1,0:T(8,128)(2,1)S(1)}, u32[]{:S(2)}, u32[]{:S(2)}) collective-permute-start(bf16[64,1024]{1,0:T(8,128)(2,1)S(1)} %collective-permute-done.10.refs_12_.refs_5_), channel_id=1, source_target_pairs={{0,1},{1,0},{2,3},{3,2},{4,5},{5,4},{6,7},{7,6},{8,9},{9,8},{10,11... | collective-permute-start | bytes 393224 | tf_op jit(solution)/shard_map/ppermute | solution.py:51
  43.4 1.4 %collective-permute-start.8 = (f32[8,1024]{1,0:T(8,128)S(1)}, f32[8,1024]{1,0:T(8,128)S(1)}, u32[]{:S(2)}, u32[]{:S(2)}) collective-permute-start(f32[8,1024]{1,0:T(8,128)S(1)} %get-tuple-element.105.refs_3_), channel_id=1, source_target_pairs={{0,1},{1,0},{2,3},{3,2},{4,5},{5,4},{6,7},{7,6},{8,9},{9,8},{10,11... | collective-permute-start | bytes 98312 | tf_op jit(solution)/shard_map/ppermute | solution.py:51
  46.9 1.7 %collective-permute-start.13 = (f32[4,160,128]{2,1,0:T(8,128)S(1)}, f32[4,160,128]{2,1,0:T(8,128)S(1)}, u32[]{:S(2)}, u32[]{:S(2)}) collective-permute-start(f32[4,160,128]{2,1,0:T(8,128)S(1)} %get-tuple-element.110), channel_id=1, source_target_pairs={{0,1},{1,0},{2,3},{3,2},{4,5},{5,4},{6,7},{7,6},{8,9},{9,8},{10,11... | collective-permute-start | bytes 983048 | tf_op jit(solution)/shard_map/ppermute | solution.py:51
  48.8 16.7 %collective-permute-start.17 = (bf16[1024,1024]{1,0:T(8,128)(2,1)S(1)}, bf16[1024,1024]{1,0:T(8,128)(2,1)S(1)}, u32[]{:S(2)}, u32[]{:S(2)}) collective-permute-start(bf16[1024,1024]{1,0:T(8,128)(2,1)S(1)} %pack_blocks.1.refs_3_.refs_4_), channel_id=1, source_target_pairs={{0,1},{1,0},{2,3},{3,2},{4,5},{5,4},{6,7},{7,6},{8,9},{9,8},{10,11... | collective-permute-start | bytes 6291464 | tf_op jit(solution)/shard_map/ppermute | solution.py:51
  49.2 6.3 %collective-permute-start.14 = (f32[2,160,128]{2,1,0:T(8,128)S(1)}, f32[2,160,128]{2,1,0:T(8,128)S(1)}, u32[]{:S(2)}, u32[]{:S(2)}) collective-permute-start(f32[2,160,128]{2,1,0:T(8,128)S(1)} %get-tuple-element.112), channel_id=1, source_target_pairs={{0,2},{1,3},{2,0},{3,1},{4,6},{5,7},{6,4},{7,5},{8,10},{9,11},{10,... | collective-permute-start | bytes 491528 | tf_op jit(solution)/shard_map/ppermute | solution.py:51
  55.5 4.5 %collective-permute-start.15 = (f32[1,160,128]{2,1,0:T(8,128)S(1)}, f32[1,160,128]{2,1,0:T(8,128)S(1)}, u32[]{:S(2)}, u32[]{:S(2)}) collective-permute-start(f32[1,160,128]{2,1,0:T(8,128)S(1)} %get-tuple-element.114), channel_id=1, source_target_pairs={{0,4},{1,5},{2,6},{3,7},{4,0},{5,1},{6,2},{7,3},{8,12},{9,13},{10,... | collective-permute-start | bytes 245768 | tf_op jit(solution)/shard_map/ppermute | solution.py:51
  60.0 5.4 %collective-permute-start.16 = (f32[1,160,128]{2,1,0:T(8,128)S(1)}, f32[1,160,128]{2,1,0:T(8,128)S(1)}, u32[]{:S(2)}, u32[]{:S(2)}) collective-permute-start(f32[1,160,128]{2,1,0:T(8,128)S(1)} %fold_z.1.refs_2_.refs_1_), channel_id=1, source_target_pairs={{0,8},{1,9},{2,10},{3,11},{4,12},{5,13},{6,14},{7,15},{8,0},{9,1},... | collective-permute-start | bytes 245768 | tf_op jit(solution)/shard_map/ppermute | solution.py:51
  65.5 4.1 %collective-permute-start.18 = (bf16[1,160,128]{2,1,0:T(8,128)(2,1)S(1)}, bf16[1,160,128]{2,1,0:T(8,128)(2,1)S(1)}, u32[]{:S(2)}, u32[]{:S(2)}) collective-permute-start(bf16[1,160,128]{2,1,0:T(8,128)(2,1)S(1)} %class_grad.1.refs_1_), channel_id=1, source_target_pairs={{0,4},{1,5},{2,6},{3,7},{4,0},{5,1},{6,2},{7,3},{8,12},{9,13},{10,... | collective-permute-start | bytes 122888 | tf_op jit(solution)/shard_map/ppermute | solution.py:51
  69.6 4.5 %collective-permute-start.19 = (bf16[2,160,128]{2,1,0:T(8,128)(2,1)S(1)}, bf16[2,160,128]{2,1,0:T(8,128)(2,1)S(1)}, u32[]{:S(2)}, u32[]{:S(2)}) collective-permute-start(bf16[2,160,128]{2,1,0:T(8,128)(2,1)S(1)} %join_z.1.refs_1_), channel_id=1, source_target_pairs={{0,2},{1,3},{2,0},{3,1},{4,6},{5,7},{6,4},{7,5},{8,10},{9,11},{10,... | collective-permute-start | bytes 245768 | tf_op jit(solution)/shard_map/ppermute | solution.py:51
  74.2 1.5 %collective-permute-start.20 = (bf16[4,160,128]{2,1,0:T(8,128)(2,1)S(1)}, bf16[4,160,128]{2,1,0:T(8,128)(2,1)S(1)}, u32[]{:S(2)}, u32[]{:S(2)}) collective-permute-start(bf16[4,160,128]{2,1,0:T(8,128)(2,1)S(1)} %join_y.1.refs_1_), channel_id=1, source_target_pairs={{0,1},{1,0},{2,3},{3,2},{4,5},{5,4},{6,7},{7,6},{8,9},{9,8},{10,11... | collective-permute-start | bytes 491528 | tf_op jit(solution)/shard_map/ppermute | solution.py:51
  77.0 4.0 %collective-permute-start.21 = (bf16[512,1024]{1,0:T(8,128)(2,1)S(1)}, bf16[512,1024]{1,0:T(8,128)(2,1)S(1)}, u32[]{:S(2)}, u32[]{:S(2)}) collective-permute-start(bf16[512,1024]{1,0:T(8,128)(2,1)S(1)} %get-tuple-element.117.refs_1_.refs_2_), channel_id=1, source_target_pairs={{0,1},{1,0},{2,3},{3,2},{4,5},{5,4},{6,7},{7,6},{8,9},{9,8},{10,11... | collective-permute-start | bytes 3145736 | tf_op jit(solution)/shard_map/ppermute | solution.py:51
  79.2 1.7 %collective-permute-start.22 = (bf16[176,1024]{1,0:T(8,128)(2,1)S(1)}, bf16[176,1024]{1,0:T(8,128)(2,1)S(1)}, u32[]{:S(2)}, u32[]{:S(2)}) collective-permute-start(bf16[176,1024]{1,0:T(8,128)(2,1)S(1)} %get-tuple-element.122), channel_id=1, source_target_pairs={{0,1},{1,0},{2,3},{3,2},{4,5},{5,4},{6,7},{7,6},{8,9},{9,8},{10,11... | collective-permute-start | bytes 1081352 | tf_op jit(solution)/shard_map/ppermute | solution.py:51
  81.4 7.5 %collective-permute-start.23 = (bf16[80,1024]{1,0:T(8,128)(2,1)S(1)}, bf16[80,1024]{1,0:T(8,128)(2,1)S(1)}, u32[]{:S(2)}, u32[]{:S(2)}) collective-permute-start(bf16[80,1024]{1,0:T(8,128)(2,1)S(1)} %get-tuple-element.129), channel_id=1, source_target_pairs={{0,4},{1,5},{4,8},{5,9},{8,12},{9,13},{12,14},{13,15},{14,10},{15,... | collective-permute-start | bytes 491528 | tf_op jit(solution)/shard_map/ppermute | solution.py:51
  83.0 5.9 %collective-permute-start.24 = (bf16[72,1024]{1,0:T(8,128)(2,1)S(1)}, bf16[72,1024]{1,0:T(8,128)(2,1)S(1)}, u32[]{:S(2)}, u32[]{:S(2)}) collective-permute-start(bf16[72,1024]{1,0:T(8,128)(2,1)S(1)} %get-tuple-element.130), channel_id=1, source_target_pairs={{0,2},{1,3},{4,0},{5,1},{8,4},{9,5},{12,8},{13,9},{14,12},{15,13},... | collective-permute-start | bytes 442376 | tf_op jit(solution)/shard_map/ppermute | solution.py:51
  89.0 8.6 %collective-permute-start.25 = (bf16[152,1024]{1,0:T(8,128)(2,1)S(1)}, bf16[152,1024]{1,0:T(8,128)(2,1)S(1)}, u32[]{:S(2)}, u32[]{:S(2)}) collective-permute-start(bf16[152,1024]{1,0:T(8,128)(2,1)S(1)} %get-tuple-element.131), channel_id=1, source_target_pairs={{0,4},{1,5},{4,8},{5,9},{8,12},{9,13},{12,14},{13,15},{14,10},{15,... | collective-permute-start | bytes 933896 | tf_op jit(solution)/shard_map/ppermute | solution.py:51
  90.8 8.2 %collective-permute-start.26 = (bf16[152,1024]{1,0:T(8,128)(2,1)S(1)}, bf16[152,1024]{1,0:T(8,128)(2,1)S(1)}, u32[]{:S(2)}, u32[]{:S(2)}) collective-permute-start(bf16[152,1024]{1,0:T(8,128)(2,1)S(1)} %get-tuple-element.132), channel_id=1, source_target_pairs={{0,2},{1,3},{4,0},{5,1},{8,4},{9,5},{12,8},{13,9},{14,12},{15,13},... | collective-permute-start | bytes 933896 | tf_op jit(solution)/shard_map/ppermute | solution.py:51
  99.2 7.3 %collective-permute-start.28 = (bf16[152,1024]{1,0:T(8,128)(2,1)S(1)}, bf16[152,1024]{1,0:T(8,128)(2,1)S(1)}, u32[]{:S(2)}, u32[]{:S(2)}) collective-permute-start(bf16[152,1024]{1,0:T(8,128)(2,1)S(1)} %get-tuple-element.137), channel_id=1, source_target_pairs={{0,2},{1,3},{4,0},{5,1},{8,4},{9,5},{12,8},{13,9},{14,12},{15,13},... | collective-permute-start | bytes 933896 | tf_op jit(solution)/shard_map/ppermute | solution.py:51
  99.6 7.3 %collective-permute-start.27 = (bf16[152,1024]{1,0:T(8,128)(2,1)S(1)}, bf16[152,1024]{1,0:T(8,128)(2,1)S(1)}, u32[]{:S(2)}, u32[]{:S(2)}) collective-permute-start(bf16[152,1024]{1,0:T(8,128)(2,1)S(1)} %get-tuple-element.136.refs_6_), channel_id=1, source_target_pairs={{0,4},{1,5},{4,8},{5,9},{8,12},{9,13},{12,14},{13,15},{14,10},{15,... | collective-permute-start | bytes 933896 | tf_op jit(solution)/shard_map/ppermute | solution.py:51
  107.1 7.0 %collective-permute-start.29 = (bf16[152,1024]{1,0:T(8,128)(2,1)S(1)}, bf16[152,1024]{1,0:T(8,128)(2,1)S(1)}, u32[]{:S(2)}, u32[]{:S(2)}) collective-permute-start(bf16[152,1024]{1,0:T(8,128)(2,1)S(1)} %get-tuple-element.139), channel_id=1, source_target_pairs={{0,4},{1,5},{4,8},{5,9},{8,12},{9,13},{12,14},{13,15},{14,10},{15,... | collective-permute-start | bytes 933896 | tf_op jit(solution)/shard_map/ppermute | solution.py:51
  108.7 6.9 %collective-permute-start.30 = (bf16[152,1024]{1,0:T(8,128)(2,1)S(1)}, bf16[152,1024]{1,0:T(8,128)(2,1)S(1)}, u32[]{:S(2)}, u32[]{:S(2)}) collective-permute-start(bf16[152,1024]{1,0:T(8,128)(2,1)S(1)} %get-tuple-element.140), channel_id=1, source_target_pairs={{0,2},{1,3},{4,0},{5,1},{8,4},{9,5},{12,8},{13,9},{14,12},{15,13},... | collective-permute-start | bytes 933896 | tf_op jit(solution)/shard_map/ppermute | solution.py:51
  (10 other events, 27.2 us)

commit v3 on v2

--- a/solution.py
+++ b/solution.py
@@ -54,6 +54,7 @@
 FORTH, BACK, SIBLING = walk_perm(1), walk_perm(-1), flip_perm(1)
 VMEM = pl.BlockSpec(memory_space=pltpu.VMEM)
 SMEM = pl.BlockSpec(memory_space=pltpu.SMEM)
+HBM = pl.BlockSpec(memory_space=pltpu.HBM)
 
 
 def call(kernel, outs, ins, scratch=(), flops=0, moved=0, limit=40, name=None, after=(), out_spaces=None):
@@ -102,8 +103,13 @@
     return acc
 
 
-def conv_kernel(x_ref, taps, out_ref, grid_pad, copies):
+def conv_kernel(x_hbm, taps_hbm, out_ref, x_ref, taps, grid_pad, copies, sems):
+    fetches = [pltpu.make_async_copy(x_hbm, x_ref, sems.at[0]), pltpu.make_async_copy(taps_hbm, taps, sems.at[1])]
+    for fetch in fetches:
+        fetch.start()
     clear_border(grid_pad)
+    for fetch in fetches:
+        fetch.wait()
     for g in range(8):
         put_rows(grid_pad, 4 * g, x_ref[:, g * LANE : (g + 1) * LANE].astype(F32))
     shifted_copies(grid_pad, copies)
@@ -135,7 +141,10 @@
     gain_sum_ref[...] = jnp.sum(total, axis=1, keepdims=True)
 
 
-def mix_kernel(w_out_ref, scale_ref, head_ref, head_pad_ref, mix_ref):
+def mix_kernel(places_ref, w_out_ref, scale_ref, head_ref, head_pad_ref, mix_ref, walk_ref):
+    for d in range(CHIPS):
+        for side in range(2):
+            walk_ref[:, (side * CHIPS + d) * LANE : (side * CHIPS + d + 1) * LANE] = w_out_ref[:, columns(places_ref, 2 * d + side)]
     head_pad_ref[...] = jnp.zeros_like(head_pad_ref)
     head_pad_ref[0 : head_ref.shape[0], :] = head_ref[...]
     head = head_pad_ref[...]
@@ -179,11 +188,23 @@
     sums_ref[...] = jnp.concatenate([shift, first, second, jnp.zeros((5, shift.shape[1]), F32)], axis=0)
 
 
+def pairs_kernel(ids, own_ref, sib_ref, acc_in_ref, shift_ref, *refs):
+    blocks, (acc_ref, sums_ref) = refs[:-2], refs[-2:]
+    held = jnp.concatenate([b[...] for b in blocks], axis=0)
+    pick = [ref[:, d * LANE : (d + 1) * LANE] for ref in (own_ref, sib_ref) for d in ids]
+    acc_ref[...] = acc_in_ref[...] + dot(jnp.concatenate(pick, axis=1), held, ((1,), (0,)))
+    shift = shift_ref[0:1, :]
+    away = held.astype(F32) - shift
+    first = jnp.sum(away, axis=0, keepdims=True)
+    second = jnp.sum(away * away, axis=0, keepdims=True)
+    sums_ref[...] = jnp.concatenate([shift, first, second, jnp.zeros((5, shift.shape[1]), F32)], axis=0)
+
+
 def pack_kernel(*refs):
     refs[-1][...] = jnp.concatenate([ref[...] for ref in refs[:-1]], axis=0)
 
 
-def forward_kernel(places_ref, acc_ref, got_ref, sums_ref, sib_sums_ref, gain_sum_ref, mix_ref, head_ref, x_ref, own_ref, sib_ref, *refs):
+def forward_kernel(places_ref, acc_ref, got_ref, sums_ref, sib_sums_ref, pair_sums_ref, gain_sum_ref, mix_ref, head_ref, x_ref, own_ref, sib_ref, *refs):
     blocks, (pre_ref, hidden_ref, stats_ref, keep_ref, give_ref, scratch) = refs[:-6], refs[-6:]
     held = jnp.concatenate([b[...] for b in blocks], axis=0)
     at = slice(CHIPS // 2 * LANE, (CHIPS // 2 + 1) * LANE)
@@ -191,7 +212,7 @@
     shift = sums_ref[0:1, :]
     away = held.astype(F32) - shift
     sets = [(held.shape[0], shift, jnp.sum(away, axis=0, keepdims=True), jnp.sum(away * away, axis=0, keepdims=True))]
-    sets += [((CHIPS - 1) * LANE, ref[0:1, :], ref[1:2, :], ref[2:3, :]) for ref in (sums_ref, sib_sums_ref)]
+    sets += [(count * LANE, ref[0:1, :], ref[1:2, :], ref[2:3, :]) for count, ref in ((5, sums_ref), (5, sib_sums_ref), (4, pair_sums_ref))]
     means = [base + first / count for count, base, first, _ in sets]
     channels = 2 * CHIPS * LANE
     tok_mean = sum(s[0] * mean for s, mean in zip(sets, means)) / channels
@@ -219,21 +240,25 @@
     slope_ref[...] = (cum_prob + pre_act * density) * stats_ref[1:2, :]
 
 
-def fold_kernel(row, marks_ref, keep_ref, got_ref, kept_ref, give_ref):
-    bit = jnp.broadcast_to(marks_ref[row : row + 1, :], kept_ref.shape[-2:]) == 1
-    half = keep_ref.shape[0] // 2
-    for g in range(half):
-        low, high = keep_ref[g] + got_ref[g], keep_ref[half + g] + got_ref[half + g]
-        kept_ref[g] = jnp.where(bit, high, low)
-        give_ref[g] = jnp.where(bit, low, high)
-
-
-def add_kernel(a_ref, b_ref, out_ref):
-    out_ref[...] = a_ref[...] + b_ref[...]
+def pick(marks_ref, y, z, chunks):
+    size = chunks[0].shape
+    bit_y = jnp.broadcast_to(marks_ref[1:2, :], size) != y
+    bit_z = jnp.broadcast_to(marks_ref[2:3, :], size) != z
+    return jnp.where(bit_y, jnp.where(bit_z, chunks[3], chunks[2]), jnp.where(bit_z, chunks[1], chunks[0]))
+
+
+def fold_kernel(marks_ref, keep_ref, got_ref, *outs):
+    chunks = [keep_ref[g] + got_ref[g] for g in range(4)]
+    for out, (y, z) in zip(outs, ((0, 0), (1, 0), (0, 1), (1, 1))):
+        out[...] = pick(marks_ref, y, z, chunks)
+
+
+def add_kernel(*refs):
+    refs[-1][...] = sum(ref[...] for ref in refs[:-1])
 
 
 def softmax_kernel(classes, marks_ref, kept_ref, got_ref, labels_ref, grad_ref):
-    kept = kept_ref[0] + got_ref[0]
+    kept = kept_ref[...] + got_ref[...]
     chunk = 4 * marks_ref[0:1, :] + 2 * marks_ref[1:2, :] + marks_ref[2:3, :]
     labels = labels_ref[:, :LANE]
     for g in range(1, labels_ref.shape[1] // LANE):
@@ -249,39 +274,35 @@
     loss_high = loss.astype(BF).astype(F32)
     grad = exp_terms / exp_total - onehot.astype(F32)
     grad = jnp.where(class_id == classes, loss_high, jnp.where(class_id == classes + 1, loss - loss_high, grad))
-    grad_ref[0] = grad.astype(BF)
-
-
-def join_kernel(row, marks_ref, own_ref, other_ref, out_ref):
-    bit = jnp.broadcast_to(marks_ref[row : row + 1, :], own_ref.shape[1:]) == 1
-    half = own_ref.shape[0]
-    for g in range(half):
-        own, other = own_ref[g].astype(F32), other_ref[g].astype(F32)
-        out_ref[g] = jnp.where(bit, other, own).astype(BF)
-        out_ref[half + g] = jnp.where(bit, own, other).astype(BF)
-
-
-def grad_kernel(places_ref, own_ref, sib_ref, mix_ref, slope_ref, pre_ref, gain_sum_ref, grad_ref, scaled_ref, means_ref):
+    grad_ref[...] = grad.astype(BF)
+
+
+def join_kernel(marks_ref, own_ref, y_ref, z_ref, both_ref, out_ref):
+    chunks = [ref[...].astype(F32) for ref in (own_ref, z_ref, y_ref, both_ref)]
+    for g in range(4):
+        out_ref[g] = pick(marks_ref, g // 2, g % 2, chunks).astype(BF)
+
+
+def grad_kernel(places_ref, own_ref, sib_ref, mix_ref, slope_ref, grad_ref, scaled_ref):
     core = places_ref[CORE]
     chunks = own_ref.shape[0]
     for g in range(chunks):
         grad_ref[:, pl.ds(pl.multiple_of((core * chunks + g) * LANE, LANE), LANE)] = own_ref[g]
         grad_ref[:, pl.ds(pl.multiple_of(((1 - core) * chunks + g) * LANE, LANE), LANE)] = sib_ref[g]
-    scaled = (dot(mix_ref[...], grad_ref[...], ((1,), (0,))) * slope_ref[...]).astype(BF)
-    scaled_ref[...] = scaled
-    wide = scaled.astype(F32)
+    scaled_ref[...] = (dot(mix_ref[...], grad_ref[...], ((1,), (0,))) * slope_ref[...]).astype(BF)
+
+
+def branch_kernel(hidden_ref, grad_ref, w_out_ref, scaled_ref, pre_ref, gain_sum_ref, mixed_ref, keep_ref, give_ref):
+    mixed = dot(hidden_ref[...], grad_ref[...], ((1,), (1,))).astype(BF)
+    mixed_ref[...] = mixed
+    branch = dot(mixed, w_out_ref[...], ((0,), (0,)))
+    wide = scaled_ref[...].astype(F32)
     mean_part = jnp.sum(wide * gain_sum_ref[...], axis=0, keepdims=True)
     proj_part = jnp.sum(wide * pre_ref[...], axis=0, keepdims=True)
-    means_ref[...] = jnp.concatenate([mean_part, proj_part, jnp.zeros((SUB_ROWS - 2, wide.shape[1]), F32)], axis=0)
-
-
-def branch_kernel(places_ref, hidden_ref, grad_ref, w_out_ref, means_ref, mixed_ref, keep_ref, give_ref):
-    mixed = dot(hidden_ref[...], grad_ref[...], ((1,), (1,))).astype(BF)
-    mixed_ref[...] = mixed
+    means = jnp.concatenate([mean_part, proj_part, jnp.zeros((SUB_ROWS - 2, wide.shape[1]), F32)], axis=0)
+    width = keep_ref.shape[1]
     for side, out in enumerate((keep_ref, give_ref)):
-        cols = jnp.concatenate([w_out_ref[:, columns(places_ref, 2 * d + side)] for d in range(CHIPS)], axis=1)
-        both = jnp.concatenate([dot(mixed, cols, ((0,), (0,))), means_ref[...]], axis=0)
-        out[...] = both.astype(out.dtype)
+        out[...] = jnp.concatenate([branch[:, side * width : (side + 1) * width], means], axis=0).astype(out.dtype)
 
 
 def message_of(d, turned_ref, own_ref, got_ref, keep_ref, sib_ref):
@@ -293,7 +314,7 @@
     means = jnp.concatenate(means + [jnp.zeros((EXTRA - 16, LANE), F32)], axis=0)
     branch = keep_ref[:CLASS_ROWS, at] + sib_ref[:CLASS_ROWS, at].astype(F32)
     branch = jnp.concatenate([branch, jnp.zeros((7 * EXTRA - CLASS_ROWS, LANE), F32)], axis=0)
-    extra = jnp.concatenate([branch[g * EXTRA : (g + 1) * EXTRA] for g in range(7)] + [means], axis=1)
+    extra = jnp.concatenate([means] + [branch[g * EXTRA : (g + 1) * EXTRA] for g in range(7)], axis=1)
     return jnp.concatenate([rows, extra], axis=0)
 
 
@@ -310,15 +331,14 @@
     lower[...] = total[cut:].astype(BF)
 
 
-def sum_kernel(ahead, behind, forth, back, ahead_out, behind_out):
-    ahead, behind = ahead[...], behind[...]
-    height, cut = ahead.shape[0], forth.shape[0]
-    if cut < height:
-        ahead_out[...] = jnp.concatenate([ahead[:cut] + forth[...].astype(F32), ahead[cut:]], axis=0).astype(BF)
-        behind_out[...] = jnp.concatenate([behind[:cut], behind[cut:] + back[...].astype(F32)], axis=0).astype(BF)
-    else:
-        ahead_out[...] = (ahead + forth[...].astype(F32)).astype(BF)
-        behind_out[...] = (behind + back[...].astype(F32)).astype(BF)
+def sum_kernel(begin, own_ref, got_ref, *outs):
+    own, got = own_ref[...], got_ref[...].astype(F32)
+    end = begin + got.shape[0]
+    pieces = [own[:begin]] * (begin > 0) + [own[begin:end] + got] + [own[end:]] * (end < own.shape[0])
+    total = jnp.concatenate(pieces, axis=0) if len(pieces) > 1 else pieces[0]
+    for n, out in enumerate(outs):
+        width = out.shape[1]
+        out[...] = total[:, n * width : (n + 1) * width].astype(BF)
 
 
 def d_w_out_kernel(mixed_ref, head_ref, scale_ref, out_ref, done_ref, held, sems):
@@ -360,35 +380,67 @@
     loss_ref[...] = (jnp.sum(grad[classes : classes + 2].astype(F32)) / grad.shape[1]).reshape(1, 1)
 
 
-def last_kernel(classes, places_ref, mine_ref, forth_ref, back_ref, conv_ref, stats_ref, taps, copies_x, out_grad_ref, head_grad_ref, head_ref, scale_ref,
-                d_x_ref, d_dw_ref, d_scale_ref, d_head_ref, grid_pad, copies, sums):
+def put_conv_grad(groups, got, means_rows, conv_ref, stats_ref, grid_pad):
     rows = conv_ref.shape[0]
     channels = rows * 2 * CHIPS
-    got = mine_ref[...] + forth_ref[...].astype(F32) + back_ref[...].astype(F32)
-    extra = got[rows:]
-    branch = jnp.concatenate([extra[:, g * LANE : (g + 1) * LANE] for g in range(7)], axis=0)[:CLASS_ROWS]
-    means = extra[:, 7 * LANE :]
-    clear_border(grid_pad)
-    for g in range(8):
+    for n, g in enumerate(groups):
         at = slice(g * LANE, (g + 1) * LANE)
         normed = (conv_ref[:, at].astype(F32) - stats_ref[0:1, at]) * stats_ref[1:2, at]
-        conv_grad = got[:rows, at] - (means[g : g + 1, :] + normed * means[8 + g : 9 + g, :]) * (1.0 / channels)
+        conv_grad = got[:rows, n * LANE : (n + 1) * LANE] - (means_rows[g : g + 1, :] + normed * means_rows[8 + g : 9 + g, :]) * (1.0 / channels)
         put_rows(grid_pad, 4 * g, conv_grad)
-    shifted_copies(grid_pad, copies)
-    for g in range(8):
-        at = slice(g * LANE, (g + 1) * LANE)
-        d_x_ref[:, at] = out_grad_ref[:, at] + conv_rows(copies, taps, 4 * g, True).reshape(LANE, LANE).T
-    for g in range(8):
+
+
+def add_taps(groups, copies, copies_x, sums):
+    for g in groups:
         conv_grad = copies[HALF, pl.ds(4 * g + HALF, 4)]
         for j in range(KS):
             for i in range(KS):
                 prod = (conv_grad * copies_x[j, pl.ds(4 * g + i, 4)]).reshape(16, 8, LANE)
+                index = i * KS + j
                 total = jnp.sum(prod, axis=0)
-                index = i * KS + j
                 if g == 0:
                     sums[index] = total
                 else:
                     sums[index] += total
+
+
+def copy_rows(begin, end, grid_pad, copies):
+    rows = pl.ds(begin, end - begin)
+    for j in range(KS):
+        copies[j, rows] = grid_pad[rows, pl.ds(8 + j - HALF, WIN_W), :]
+
+
+def upper_kernel(mine_ref, forth_ref, back_ref, conv_ref, stats_ref, taps, copies_x, out_grad_ref,
+                 d_x_ref, sums, grid_pad, extra_ref, copies):
+    rows = conv_ref.shape[0]
+    width = forth_ref.shape[1]
+    got = mine_ref[:, :width] + forth_ref[...].astype(F32) + back_ref[...].astype(F32)
+    extra_ref[...] = got[rows:]
+    clear_border(grid_pad)
+    put_conv_grad(range(4), got, got[rows:, :LANE], conv_ref, stats_ref, grid_pad)
+    copy_rows(0, 16 + HALF, grid_pad, copies)
+    for g in range(3):
+        at = slice(g * LANE, (g + 1) * LANE)
+        d_x_ref[:, at] = out_grad_ref[:, at] + conv_rows(copies, taps, 4 * g, True).reshape(LANE, LANE).T
+    add_taps(range(4), copies, copies_x, sums)
+
+
+def lower_kernel(classes, places_ref, mine_ref, forth_ref, back_ref, conv_ref, stats_ref, taps, copies_x, out_grad_ref, head_grad_ref, head_ref, scale_ref,
+                 d_upper_ref, sums_ref, grid_ref, extra_ref, d_x_ref, d_dw_ref, d_scale_ref, d_head_ref, grid_pad, copies, sums):
+    rows = conv_ref.shape[0]
+    width = forth_ref.shape[1]
+    got = mine_ref[:, width:] + forth_ref[...].astype(F32) + back_ref[...].astype(F32)
+    extra = jnp.concatenate([extra_ref[...], got[rows:]], axis=1)
+    branch = jnp.concatenate([extra[:, g * LANE : (g + 1) * LANE] for g in range(1, 8)], axis=0)[:CLASS_ROWS]
+    sums[...] = sums_ref[...]
+    grid_pad[...] = grid_ref[...]
+    put_conv_grad(range(4, 8), got, extra[:, :LANE], conv_ref, stats_ref, grid_pad)
+    copy_rows(12, WIN_H + 2 * HALF, grid_pad, copies)
+    d_x_ref[:, : 3 * LANE] = d_upper_ref[...]
+    for g in range(3, 8):
+        at = slice(g * LANE, (g + 1) * LANE)
+        d_x_ref[:, at] = out_grad_ref[:, at] + conv_rows(copies, taps, 4 * g, True).reshape(LANE, LANE).T
+    add_taps(range(4, 8), copies, copies_x, sums)
     d_dw_ref[...] = jnp.sum(sums[...], axis=1)
     at = columns(places_ref, MINE)
     d_scale_ref[...] = jnp.sum(head_ref[:, at].astype(F32) * branch, axis=0, keepdims=True)
@@ -405,7 +457,7 @@
 
 
 def hold(walk, step, *others):
-    spots = [((-step) % CHIPS), step]
+    spots = [(-step) % CHIPS, step]
     held = lax.optimization_barrier((walk[spots[0]][0], walk[spots[1]][0], *others))
     walk[spots[0]], walk[spots[1]] = (held[0],), (held[1],)
     return held[2:]
@@ -427,16 +479,17 @@
     spot, mark = [(places, SMEM)], vm(marks)
     f32s, bf16s, sums_size = ((units, tokens), F32), ((units, tokens), BF), ((8, tokens), F32)
 
-    (conv_out,) = call(
-        conv_kernel, [((rows, tokens), BF)], vm(features, taps), [grid_shape, pltpu.VMEM(copies_size, F32)], limit=12, name="conv_forward",
-        after=[places, marks],
+    conv_out, features, taps = call(
+        conv_kernel, [((rows, tokens), BF), ((rows, tokens), BF), ((KS * KS, rows), F32)], [(features, HBM), (taps, HBM)],
+        [grid_shape, pltpu.VMEM(copies_size, F32), pltpu.SemaphoreType.DMA((2,))],
+        limit=12, name="conv_forward",
     )
     walk = {0: (conv_out,)}
     walk_step(walk, 1)
     w_own, w_give, gain_sum = call(
         weights_kernel,
         [((units, half_channels), BF), ((units, half_channels), BF), ((units, 1), F32)],
-        spot + vm(w_in, gain_row), flops=4e8, moved=4e6, limit=12, name="weights_ready", after=[conv_out],
+        spot + vm(w_in, gain_row), flops=4e8, moved=4e6, limit=12, name="weights_ready", after=[conv_out, marks],
     )
     w_own, w_give, gain_sum = hold(walk, 1, w_own, w_give, gain_sum)
     w_sib = send(w_give, SIBLING)
@@ -447,56 +500,63 @@
     )
     so_far = hold(walk, 2, *so_far)
     walk_step(walk, 3)
-    head_pad, mix = call(
+    head_pad, mix, w_out_walk = call(
         mix_kernel,
-        [((CLASS_ROWS, channels), BF), ((units, CLASS_ROWS), BF)],
-        vm(w_out, scale_row, w_head.T), flops=1e9, moved=4e6, limit=12, name="mix_ready", after=[so_far[2]],
+        [((CLASS_ROWS, channels), BF), ((units, CLASS_ROWS), BF), ((units, channels), BF)],
+        spot + vm(w_out, scale_row, w_head.T), flops=1e9, moved=4e6, limit=12, name="mix_ready", after=[so_far[2]],
     )
     so_far = call(
-        functools.partial(next_kernel, (2, 6)), [f32s, f32s, sums_size],
+        functools.partial(next_kernel, (2, 6)), [f32s, bf16s, sums_size],
         vm(w_own, w_sib, *so_far, *walk[2], *walk[6]), flops=6e8, moved=4e6, limit=16, name="forward_next",
     )
-    *so_far, head_pad, mix = hold(walk, 3, *so_far, head_pad, mix)
+    *so_far, head_pad, mix, w_out_walk = hold(walk, 3, *so_far, head_pad, mix, w_out_walk)
+    acc, give, sums = so_far
+    got, sib_sums = send(give, SIBLING), send(sums, SIBLING)
     walk_step(walk, 4)
-    acc, give, sums = call(
-        functools.partial(next_kernel, (3, 5)), [f32s, bf16s, sums_size],
-        vm(w_own, w_sib, *so_far, *walk[3], *walk[5]), flops=6e8, moved=4e6, limit=16, name="forward_next",
-    )
-    got, sib_sums = send(give, SIBLING), send(sums, SIBLING)
+    acc, pair_sums = call(
+        functools.partial(pairs_kernel, (3, 5)), [f32s, sums_size],
+        vm(w_own, w_give, acc, sums, *walk[3], *walk[5], send(walk[3][0], SIBLING), send(walk[5][0], SIBLING)),
+        flops=1e9, moved=4e6, limit=16, name="forward_pairs",
+    )
+    upper, acc, pair_sums = lax.optimization_barrier((walk[4][0], acc, pair_sums))
+    walk[4] = (upper, walk[4][1])
     far = [*walk[4], *[send(b, SIBLING) for b in walk[4]]]
     chunks = tokens // LANE // 2
     chunk = lambda count, kind=F32: ((count, CLASS_ROWS, LANE), kind)
     pre_act, hidden, stats, keep, give = call(
         forward_kernel, [f32s, bf16s, sums_size, chunk(chunks), chunk(chunks)],
-        spot + vm(acc, got, sums, sib_sums, gain_sum, mix, head_pad, features, w_own, w_give, *far),
+        spot + vm(acc, got, sums, sib_sums, pair_sums, gain_sum, mix, head_pad, features, w_own, w_give, *far),
         [pltpu.VMEM((2 * chunks, CLASS_ROWS, LANE), F32)], flops=1e9, moved=4e6, limit=16, name="forward_hidden",
     )
 
-    kept, give = call(functools.partial(fold_kernel, 1), [chunk(2), chunk(2)], mark + vm(keep, send(give, SIBLING)), limit=4, name="fold_core")
+    own_chunk = ((CLASS_ROWS, LANE), F32)
+    others = (2, 4, 6)
+    kept, *gives = call(fold_kernel, [own_chunk] * 4, mark + vm(keep, send(give, SIBLING)), limit=4, name="fold_core")
     (packed,) = call(
         pack_kernel, [((half_channels, tokens), BF)], vm(*[b for d in range(CHIPS) for b in walk[d]]), flops=4e8, moved=4e6, limit=10, name="pack_blocks", after=[kept],
     )
     sib_packed = send(packed, SIBLING)
-    kept, give = call(functools.partial(fold_kernel, 2), [chunk(1), chunk(1)], mark + vm(kept, send(give, flip_perm(2))), limit=4, name="fold_y", after=[packed])
-    (slope,) = call(slope_kernel, [f32s], vm(pre_act, stats), flops=5e8, moved=4e6, limit=8, name="gelu_slope", after=[kept])
-    (kept,) = call(add_kernel, [chunk(1)], vm(kept, send(give, flip_perm(4))), limit=4, name="fold_z", after=[slope])
+    (slope,) = call(slope_kernel, [f32s], vm(pre_act, stats), flops=5e8, moved=4e6, limit=8, name="gelu_slope", after=[packed])
+    (kept,) = call(
+        add_kernel, [own_chunk], vm(kept, *[send(part, flip_perm(bits)) for part, bits in zip(gives, others)]), limit=4, name="fold_chips", after=[slope],
+    )
     (turned,) = call(turn_kernel, [((half_channels, 2 * units), BF)], vm(w_own, w_sib), flops=4e8, moved=4e6, limit=10, name="weights_turned", after=[kept])
     (grad,) = call(
-        functools.partial(softmax_kernel, classes), [chunk(1, BF)], mark + vm(kept, send(kept, flip_perm(8)), labels_row), limit=4, name="class_grad", after=[turned, sib_packed],
+        functools.partial(softmax_kernel, classes), [((CLASS_ROWS, LANE), BF)], mark + vm(kept, send(kept, flip_perm(8)), labels_row), limit=4, name="class_grad", after=[turned, sib_packed],
     )
     (copies_x,) = call(copies_kernel, [(copies_size, F32)], vm(features), [grid_shape], flops=4e8, moved=4e6, limit=12, name="window_copies", after=[grad])
-    (grad,) = call(functools.partial(join_kernel, 2), [chunk(2, BF)], mark + vm(grad, send(grad, flip_perm(4))), limit=4, name="join_z", after=[copies_x])
-    (grad,) = call(functools.partial(join_kernel, 1), [chunk(4, BF)], mark + vm(grad, send(grad, flip_perm(2))), limit=4, name="join_y")
-
-    grad, scaled, means = call(
-        grad_kernel, [((CLASS_ROWS, tokens), BF), bf16s, ((SUB_ROWS, tokens), F32)],
-        spot + vm(grad, send(grad, SIBLING), mix, slope, pre_act, gain_sum), flops=6e8, moved=4e6, limit=12, name="hidden_grad",
+    (grad,) = call(
+        join_kernel, [((chunks, CLASS_ROWS, LANE), BF)], mark + vm(grad, *[send(grad, flip_perm(bits)) for bits in others]), limit=4, name="join_chips", after=[copies_x],
+    )
+
+    grad, scaled = call(
+        grad_kernel, [((CLASS_ROWS, tokens), BF), bf16s], spot + vm(grad, send(grad, SIBLING), mix, slope), flops=6e8, moved=4e6, limit=12, name="hidden_grad",
     )
     got = send(scaled, SIBLING)
     extra_rows = CLASS_ROWS + SUB_ROWS
     mixed, keep, give = call(
         branch_kernel, [((units, CLASS_ROWS), BF), ((extra_rows, half_channels), F32), ((extra_rows, half_channels), BF)],
-        spot + vm(hidden, grad, w_out, means), flops=8e8, moved=4e6, limit=12, name="class_products",
+        vm(hidden, grad, w_out_walk, scaled, pre_act, gain_sum), flops=8e8, moved=4e6, limit=12, name="class_products",
     )
     sources = vm(turned, scaled, got, keep, send(give, SIBLING))
     height = rows + EXTRA
@@ -518,21 +578,36 @@
             functools.partial(message_kernel, (step, CHIPS - step)), [((height, tokens), F32)] * 2, sources,
             flops=6e8, moved=2e6, limit=8, name="messages",
         )
-        forth, back = call(sum_kernel, [((height, tokens), BF)] * 2, vm(ahead, behind, forth, back), limit=6, name="walk_sum", after=beside[step])
+        first = step == CHIPS // 2 - 1
+        parts = 2 if step == 1 else 1
+        add = lambda begin, own, got, waits: call(
+            functools.partial(sum_kernel, begin), [((height, tokens // parts), BF)] * parts, vm(own, got), limit=6, name="walk_sum", after=waits,
+        )
+        forth, back = add(0, ahead, forth, []), add(cut if first else 0, behind, back, beside[step])
+        if step == 1:
+            continue
+        (forth,), (back,) = forth, back
         if step == 2:
             d_w_in, d_w_in_done = call(
                 d_w_in_kernel, [((units, channels), F32), ((8, LANE), F32)], spot + vm(gain_row, scaled, stats, packed, sib_packed),
                 [pltpu.VMEM((2 * CHIPS, units, LANE), F32), pltpu.SemaphoreType.DMA((2 * CHIPS,))],
-                flops=2e9, moved=8e6, limit=12, name="d_w_in", out_spaces=(pl.ANY, pltpu.VMEM), after=[forth],
+                flops=2e9, moved=8e6, limit=12, name="d_w_in", out_spaces=(pl.ANY, pltpu.VMEM), after=[forth, back],
             )
             beside[1] = [d_w_in_done]
         forth, back = send(forth, FORTH), send(back, BACK)
     (mine,) = call(functools.partial(message_kernel, (0,)), [((height, tokens), F32)], sources, flops=3e8, moved=2e6, limit=8, name="messages", after=[ahead])
+    ends = [(send(forth[n], FORTH), send(back[n], BACK)) for n in range(2)]
+    upper = call(
+        upper_kernel,
+        [((rows, 3 * LANE), F32), ((KS * KS, 8, LANE), F32), (grid_shape.shape, F32), ((EXTRA, tokens // 2), F32)],
+        vm(mine, *ends[0], conv_out, stats, taps, copies_x, out_grad), [pltpu.VMEM(copies_size, F32)],
+        flops=4e8, moved=2e6, limit=16, name="conv_backward_upper",
+    )
     d_features, d_dw, d_scale, d_head = call(
-        functools.partial(last_kernel, classes),
+        functools.partial(lower_kernel, classes),
         [((rows, tokens), F32), ((KS * KS, rows), F32), ((1, rows), F32), ((classes, rows), F32)],
-        spot + vm(mine, forth, back, conv_out, stats, taps, copies_x, out_grad, head_grad, head_pad, scale_row),
-        [grid_shape, pltpu.VMEM(copies_size, F32), pltpu.VMEM((KS * KS, 8, LANE), F32)], limit=16, name="conv_backward",
+        spot + vm(mine, *ends[1], conv_out, stats, taps, copies_x, out_grad, head_grad, head_pad, scale_row, *upper),
+        [grid_shape, pltpu.VMEM(copies_size, F32), pltpu.VMEM((KS * KS, 8, LANE), F32)], limit=16, name="conv_backward_lower",
     )
     return (d_features, d_dw.T, d_scale[0], d_w_in, d_w_out, d_head.T, mean_loss[0])
 

time: 123 us -> 111 us (0.902)
  waiting for transfers between devices: 55.7 us -> 38.6 us
  starting transfers between devices: 26.7 us -> 32.1 us
    ppermute x31 -> x37, waiting for transfers between devices: 55.7 us -> 38.6 us  [send(): return lax.ppermute(value, 'ch', perm)]
    ppermute x31 -> x37, starting transfers between devices: 26.7 us -> 32.1 us  [send(): return lax.ppermute(value, 'ch', perm)]
    pallas_call x31 -> x33, Pallas kernels: 33.5 us -> 33.7 us  [call(): pl.pallas_call(body, out_shape=[jax.ShapeDtypeStruct(s, d) for s, d in ou...]
    unnamed x22 -> x18, local copies, waits for them, and re-layouts: 4.01 us -> 4 us
  transfers between devices with their start and end apart: 31 -> 37, of which waited for: 25 -> 23; matrix products, arithmetic and copies ran while one was open for 0% -> 1% of each run, Pallas kernels for 15% -> 21%
where the time goes in v3:
time: 111 us
  waiting for transfers between devices  38.6 us (35%)
  Pallas kernels  33.7 us (30%)
  starting transfers between devices  32.1 us (29%)
  local copies, waits for them, and re-layouts  5.47 us (5%)
    ppermute x37, waiting for transfers between devices, send(): return lax.ppermute(value, 'ch', perm)  38.6 us
    pallas_call x33, Pallas kernels, call(): pl.pallas_call(body, out_shape=[jax.ShapeDtypeStruct(s, d) for s, d in ou...  33.7 us
    ppermute x37, starting transfers between devices, send(): return lax.ppermute(value, 'ch', perm)  32.1 us
    unnamed x18, local copies, waits for them, and re-layouts  4 us
  transfers between devices with their start and end apart: 37, of which 23 were waited for; matrix products, arithmetic and copies ran while one was open for 1% of the time, Pallas kernels for 21%

profile of v3, /device:TPU:0, one launch (start us, length us, event | category | flops | bytes accessed | tf_op | source)
XLA Modules:
  0.0 110.8 jit_solution(1427671808424852323)
XLA Ops:
  2.3 2.6 %conv_forward.1 = (bf16[128,1024]{1,0:T(8,128)(2,1)S(1)}, bf16[128,1024]{1,0:T(8,128)(2,1)S(1)}, f32[49,128]{1,0:T(8,128)S(1)}) custom-call(bf16[128,1024]{1,0:T(8,128)(2,1)S(1)} %copy-done.1, f32[49,128]{1,0:T(8,128)S(1)} %bitcast.13), custom_call_target="tpu_custom_call" | custom-call | tf_op jit(solution)/shard_map/conv_forward/pallas_call | solution.py:66
  5.0 3.0 %collective-permute-start.1 = (bf16[128,1024]{1,0:T(8,128)(2,1)S(1)}, bf16[128,1024]{1,0:T(8,128)(2,1)S(1)}, u32[]{:S(2)}, u32[]{:S(2)}) collective-permute-start(bf16[128,1024]{1,0:T(8,128)(2,1)S(1)} %get-tuple-element.86.refs_3_.refs_2_.refs_0_.refs_4_), channel_id=1, source_target_pairs={{0,2},{1,3},{4,0},{5,1},{8,4},{9,5},{12,8},{13,9},{14,12},{15,13},... | collective-permute-start | bytes 786440 | tf_op jit(solution)/shard_map/ppermute | solution.py:51
  9.6 1.6 %copy-done = bf16[512,2048]{1,0:T(8,128)(2,1)S(1)} copy-done((bf16[512,2048]{1,0:T(8,128)(2,1)S(1)}, bf16[512,2048]{1,0:T(8,128)(2,1)}, u32[]{:S(2)}) %copy-start) | copy-done | bytes 2097176
  11.9 1.4 %weights_ready.1 = (bf16[512,1024]{1,0:T(8,128)(2,1)S(1)}, bf16[512,1024]{1,0:T(8,128)(2,1)S(1)}, f32[512,1]{1,0:T(8,128)S(1)}) custom-call(s32[18]{0:T(128)S(1)} %dynamic-slice_bitcast_fusion.1.refs_0_, bf16[512,2048]{1,0:T(8,128)(2,1)S(1)} %copy-done, f32[1,2048]{1,0:T(1,128)S(1)} %bitcast.14, ...), custom_call_target="tpu_custom_call" | custom-call | flops 400000000 | bytes 4000000 | tf_op jit(solution)/shard_map/weights_ready/pallas_call | solution.py:66
  14.3 1.4 %collective-permute-done.refs_4_.refs_8_ = bf16[128,1024]{1,0:T(8,128)(2,1)S(1)} collective-permute-done((bf16[128,1024]{1,0:T(8,128)(2,1)S(1)}, bf16[128,1024]{1,0:T(8,128)(2,1)S(1)}, u32[]{:S(2)}, u32[]{:S(2)}) %collective-permute-start) | collective-permute-done | bytes 262176 | tf_op jit(solution)/shard_map/ppermute | solution.py:51
  16.2 1.6 %collective-permute-start.4 = (bf16[128,1024]{1,0:T(8,128)(2,1)S(1)}, bf16[128,1024]{1,0:T(8,128)(2,1)S(1)}, u32[]{:S(2)}, u32[]{:S(2)}) collective-permute-start(bf16[128,1024]{1,0:T(8,128)(2,1)S(1)} %collective-permute-done.1.refs_3_.refs_1_), channel_id=1, source_target_pairs={{0,2},{1,3},{4,0},{5,1},{8,4},{9,5},{12,8},{13,9},{14,12},{15,13},... | collective-permute-start | bytes 786440 | tf_op jit(solution)/shard_map/ppermute | solution.py:51
  18.4 1.4 %forward_first.1 = (f32[512,1024]{1,0:T(8,128)S(1)}, f32[512,1024]{1,0:T(8,128)S(1)}, f32[8,1024]{1,0:T(8,128)S(1)}) custom-call(bf16[512,1024]{1,0:T(8,128)(2,1)S(1)} %get-tuple-element.90.refs_0_.refs_10_, bf16[512,1024]{1,0:T(8,128)(2,1)S(1)} %collective-permute-done.2.refs_1_, bf16[128,1024]{1,0:T(8,128)(2,1)S(1)} %get-tuple-element.86.refs_3_.refs_2_.refs_0_.refs_4_, ...), custom_call_target="tpu_custom_call" | custom-call | flops 1000000000 | bytes 4000000 | tf_op jit(solution)/shard_map/forward_first/pallas_call | solution.py:66
  19.8 4.7 %collective-permute-done.3.refs_6_.refs_7_ = bf16[128,1024]{1,0:T(8,128)(2,1)S(1)} collective-permute-done((bf16[128,1024]{1,0:T(8,128)(2,1)S(1)}, bf16[128,1024]{1,0:T(8,128)(2,1)S(1)}, u32[]{:S(2)}, u32[]{:S(2)}) %collective-permute-start.3) | collective-permute-done | bytes 262176 | tf_op jit(solution)/shard_map/ppermute | solution.py:51
  24.6 1.7 %collective-permute-start.5 = (bf16[128,1024]{1,0:T(8,128)(2,1)S(1)}, bf16[128,1024]{1,0:T(8,128)(2,1)S(1)}, u32[]{:S(2)}, u32[]{:S(2)}) collective-permute-start(bf16[128,1024]{1,0:T(8,128)(2,1)S(1)} %collective-permute-done.3.refs_6_.refs_7_), channel_id=1, source_target_pairs={{0,4},{1,5},{4,8},{5,9},{8,12},{9,13},{12,14},{13,15},{14,10},{15,... | collective-permute-start | bytes 786440 | tf_op jit(solution)/shard_map/ppermute | solution.py:51
  27.5 1.8 %mix_ready.1 = (bf16[160,2048]{1,0:T(8,128)(2,1)S(1)}, bf16[512,160]{1,0:T(8,128)(2,1)S(1)}, bf16[512,2048]{1,0:T(8,128)(2,1)S(1)}) custom-call(s32[18]{0:T(128)S(1)} %dynamic-slice_bitcast_fusion.1.refs_0_, bf16[512,2048]{1,0:T(8,128)(2,1)S(1)} %copy-done.7, f32[1,2048]{1,0:T(1,128)S(1)} %bitcast.16, bf16[150,2048]{1,0:T(8,128)(2,1)S(1)} %bitcast.20, ...), custom_call_target="tpu_custom_call" | custom-call | flops 1000000000 | bytes 4000000 | tf_op jit(solution)/shard_map/mix_ready/pallas_call | solution.py:66
  29.3 3.2 %collective-permute-done.5.refs_5_.refs_6_ = bf16[128,1024]{1,0:T(8,128)(2,1)S(1)} collective-permute-done((bf16[128,1024]{1,0:T(8,128)(2,1)S(1)}, bf16[128,1024]{1,0:T(8,128)(2,1)S(1)}, u32[]{:S(2)}, u32[]{:S(2)}) %collective-permute-start.5) | collective-permute-done | bytes 262176 | tf_op jit(solution)/shard_map/ppermute | solution.py:51
  34.8 1.7 %collective-permute-start.7 = (bf16[64,1024]{1,0:T(8,128)(2,1)S(1)}, bf16[64,1024]{1,0:T(8,128)(2,1)S(1)}, u32[]{:S(2)}, u32[]{:S(2)}) collective-permute-start(bf16[64,1024]{1,0:T(8,128)(2,1)S(1)} %slice.6), channel_id=1, source_target_pairs={{0,4},{1,5},{4,8},{5,9},{8,12},{9,13},{12,14},{13,15},{14,10},{15,... | collective-permute-start | bytes 393224 | tf_op jit(solution)/shard_map/ppermute | solution.py:51
  36.5 3.6 %collective-permute-done.12.refs_13_.refs_5_ = bf16[64,1024]{1,0:T(8,128)(2,1)S(1)} collective-permute-done((bf16[64,1024]{1,0:T(8,128)(2,1)S(1)}, bf16[64,1024]{1,0:T(8,128)(2,1)S(1)}, u32[]{:S(2)}, u32[]{:S(2)}) %collective-permute-start.12) | collective-permute-done | bytes 131104 | tf_op jit(solution)/shard_map/ppermute | solution.py:51
  42.7 2.1 %forward_hidden.1 = (f32[512,1024]{1,0:T(8,128)S(1)}, bf16[512,1024]{1,0:T(8,128)(2,1)S(1)}, f32[8,1024]{1,0:T(8,128)S(1)}, f32[4,160,128]{2,1,0:T(8,128)S(1)}, f32[4,160,128]{2,1,0:T(8,128)S(1)}) custom-call(s32[18]{0:T(128)S(1)} %dynamic-slice_bitcast_fusion.1.refs_0_, f32[512,1024]{1,0:T(8,128)S(1)} %get-tuple-element.114.refs_1_, ...), custom_call_target="tpu_custom_call" | custom-call | flops 1000000000 | bytes 4000000 | tf_op jit(solution)/shard_map/forward_hidden/pallas_call | solution.py:66
  45.1 1.5 %collective-permute-done.15.refs_2_ = f32[4,160,128]{2,1,0:T(8,128)S(1)} collective-permute-done((f32[4,160,128]{2,1,0:T(8,128)S(1)}, f32[4,160,128]{2,1,0:T(8,128)S(1)}, u32[]{:S(2)}, u32[]{:S(2)}) %collective-permute-start.15) | collective-permute-done | bytes 327712 | tf_op jit(solution)/shard_map/ppermute | solution.py:51
  48.1 1.6 %collective-permute-start.17 = (f32[160,128]{1,0:T(8,128)S(1)}, f32[160,128]{1,0:T(8,128)S(1)}, u32[]{:S(2)}, u32[]{:S(2)}) collective-permute-start(f32[160,128]{1,0:T(8,128)S(1)} %get-tuple-element.126), channel_id=1, source_target_pairs={{0,4},{1,5},{2,6},{3,7},{4,0},{5,1},{6,2},{7,3},{8,12},{9,13},{10,... | collective-permute-start | bytes 245768 | tf_op jit(solution)/shard_map/ppermute | solution.py:51
  52.7 2.3 %collective-permute-done.18.refs_3_ = f32[160,128]{1,0:T(8,128)S(1)} collective-permute-done((f32[160,128]{1,0:T(8,128)S(1)}, f32[160,128]{1,0:T(8,128)S(1)}, u32[]{:S(2)}, u32[]{:S(2)}) %collective-permute-start.18) | collective-permute-done | bytes 81952 | tf_op jit(solution)/shard_map/ppermute | solution.py:51
  55.0 2.4 %collective-permute-start.19 = (f32[160,128]{1,0:T(8,128)S(1)}, f32[160,128]{1,0:T(8,128)S(1)}, u32[]{:S(2)}, u32[]{:S(2)}) collective-permute-start(f32[160,128]{1,0:T(8,128)S(1)} %fold_chips.1.refs_2_.refs_1_), channel_id=1, source_target_pairs={{0,8},{1,9},{2,10},{3,11},{4,12},{5,13},{6,14},{7,15},{8,0},{9,1},... | collective-permute-start | bytes 245768 | tf_op jit(solution)/shard_map/ppermute | solution.py:51
  58.1 3.2 %collective-permute-done.19.refs_2_ = f32[160,128]{1,0:T(8,128)S(1)} collective-permute-done((f32[160,128]{1,0:T(8,128)S(1)}, f32[160,128]{1,0:T(8,128)S(1)}, u32[]{:S(2)}, u32[]{:S(2)}) %collective-permute-start.19) | collective-permute-done | bytes 81952 | tf_op jit(solution)/shard_map/ppermute | solution.py:51
  62.2 1.7 %collective-permute-start.22 = (bf16[160,128]{1,0:T(8,128)(2,1)S(1)}, bf16[160,128]{1,0:T(8,128)(2,1)S(1)}, u32[]{:S(2)}, u32[]{:S(2)}) collective-permute-start(bf16[160,128]{1,0:T(8,128)(2,1)S(1)} %class_grad.1.refs_1_), channel_id=1, source_target_pairs={{0,4},{1,5},{2,6},{3,7},{4,0},{5,1},{6,2},{7,3},{8,12},{9,13},{10,... | collective-permute-start | bytes 122888 | tf_op jit(solution)/shard_map/ppermute | solution.py:51
  66.4 1.6 %collective-permute-done.21.refs_2_ = bf16[160,128]{1,0:T(8,128)(2,1)S(1)} collective-permute-done((bf16[160,128]{1,0:T(8,128)(2,1)S(1)}, bf16[160,128]{1,0:T(8,128)(2,1)S(1)}, u32[]{:S(2)}, u32[]{:S(2)}) %collective-permute-start.21) | collective-permute-done | bytes 40992 | tf_op jit(solution)/shard_map/ppermute | solution.py:51
  68.1 1.4 %collective-permute-done.24.refs_2_ = bf16[4,160,128]{2,1,0:T(8,128)(2,1)S(1)} collective-permute-done((bf16[4,160,128]{2,1,0:T(8,128)(2,1)S(1)}, bf16[4,160,128]{2,1,0:T(8,128)(2,1)S(1)}, u32[]{:S(2)}, u32[]{:S(2)}) %collective-permute-start.24) | collective-permute-done | bytes 163872 | tf_op jit(solution)/shard_map/ppermute | solution.py:51
  70.8 1.6 %class_products.1 = (bf16[512,160]{1,0:T(8,128)(2,1)S(1)}, f32[176,1024]{1,0:T(8,128)S(1)}, bf16[176,1024]{1,0:T(8,128)(2,1)S(1)}) custom-call(bf16[512,1024]{1,0:T(8,128)(2,1)S(1)} %get-tuple-element.131.refs_0_, bf16[160,1024]{1,0:T(8,128)(2,1)S(1)} %get-tuple-element.132.refs_1_.refs_3_, bf16[512,2048]{1,0:T(8,128)(2,1)S(1)} %get-tuple-element.133.refs_2_, ...), custom_call_target="tpu_custom_call" | custom-call | flops 800000000 | bytes 4000000 | tf_op jit(solution)/shard_map/class_products/pallas_call | solution.py:66
  75.0 1.7 %collective-permute-start.31 = (bf16[72,1024]{1,0:T(8,128)(2,1)S(1)}, bf16[72,1024]{1,0:T(8,128)(2,1)S(1)}, u32[]{:S(2)}, u32[]{:S(2)}) collective-permute-start(bf16[72,1024]{1,0:T(8,128)(2,1)S(1)} %get-tuple-element.144), channel_id=1, source_target_pairs={{0,2},{1,3},{4,0},{5,1},{8,4},{9,5},{12,8},{13,9},{14,12},{15,13},... | collective-permute-start | bytes 442376 | tf_op jit(solution)/shard_map/ppermute | solution.py:51
  77.4 3.6 %collective-permute-done.31.refs_1_ = bf16[72,1024]{1,0:T(8,128)(2,1)S(1)} collective-permute-done((bf16[72,1024]{1,0:T(8,128)(2,1)S(1)}, bf16[72,1024]{1,0:T(8,128)(2,1)S(1)}, u32[]{:S(2)}, u32[]{:S(2)}) %collective-permute-start.31) | collective-permute-done | bytes 147488 | tf_op jit(solution)/shard_map/ppermute | solution.py:51
  81.0 1.6 %collective-permute-start.32 = (bf16[152,1024]{1,0:T(8,128)(2,1)S(1)}, bf16[152,1024]{1,0:T(8,128)(2,1)S(1)}, u32[]{:S(2)}, u32[]{:S(2)}) collective-permute-start(bf16[152,1024]{1,0:T(8,128)(2,1)S(1)} %walk_sum.9), channel_id=1, source_target_pairs={{0,2},{1,3},{4,0},{5,1},{8,4},{9,5},{12,8},{13,9},{14,12},{15,13},... | collective-permute-start | bytes 933896 | tf_op jit(solution)/shard_map/ppermute | solution.py:51
  85.3 2.3 %d_w_out.1 = (f32[512,2048]{1,0:T(8,128)}, f32[8,128]{1,0:T(8,128)S(1)}) custom-call(bf16[512,160]{1,0:T(8,128)(2,1)S(1)} %get-tuple-element.145.refs_0_, bf16[160,2048]{1,0:T(8,128)(2,1)S(1)} %get-tuple-element.119.refs_8_.refs_1_.refs_2_.refs_10_, f32[1,2048]{1,0:T(1,128)S(1)} %bitcast.17, bf16[80,1024]{1,0:T(8,128)(2,1)S(1)} %collective-permute-done.27.refs_1_.refs_3_.refs_4_), custom_call_target="tpu_custom_call" | custom-call | flops 1000000000 | bytes 8000000 | tf_op jit(solution)/shard_map/d_w_out/pallas_call | solution.py:66
  87.6 2.2 %collective-permute-done.32.refs_1_ = bf16[152,1024]{1,0:T(8,128)(2,1)S(1)} collective-permute-done((bf16[152,1024]{1,0:T(8,128)(2,1)S(1)}, bf16[152,1024]{1,0:T(8,128)(2,1)S(1)}, u32[]{:S(2)}, u32[]{:S(2)}) %collective-permute-start.32) | collective-permute-done | bytes 311328 | tf_op jit(solution)/shard_map/ppermute | solution.py:51
  89.8 1.4 %collective-permute-start.33 = (bf16[152,1024]{1,0:T(8,128)(2,1)S(1)}, bf16[152,1024]{1,0:T(8,128)(2,1)S(1)}, u32[]{:S(2)}, u32[]{:S(2)}) collective-permute-start(bf16[152,1024]{1,0:T(8,128)(2,1)S(1)} %walk_sum.10.refs_7_), channel_id=1, source_target_pairs={{0,2},{1,3},{4,0},{5,1},{8,4},{9,5},{12,8},{13,9},{14,12},{15,13},... | collective-permute-start | bytes 933896 | tf_op jit(solution)/shard_map/ppermute | solution.py:51
  93.0 4.3 %d_w_in.1 = (f32[512,2048]{1,0:T(8,128)}, f32[8,128]{1,0:T(8,128)S(1)}) custom-call(s32[18]{0:T(128)S(1)} %dynamic-slice_bitcast_fusion.1.refs_0_, f32[1,2048]{1,0:T(1,128)S(1)} %bitcast.15, bf16[512,1024]{1,0:T(8,128)(2,1)S(1)} %get-tuple-element.130.refs_3_.refs_1_.refs_2_, f32[8,1024]{1,0:T(8,128)S(1)} %get-tuple-element.129.refs_1_.refs_3_.refs_4_.refs_5_, ...), custom_call_target="tpu_custom_call" | custom-call | flops 2000000000 | bytes 8000000 | tf_op jit(solution)/shard_map/d_w_in/pallas_call | solution.py:66
  104.3 2.1 %conv_backward_upper.1 = (f32[128,384]{1,0:T(8,128)S(1)}, f32[49,8,128]{2,1,0:T(8,128)S(1)}, f32[38,48,128]{2,1,0:T(8,128)S(1)}, f32[24,512]{1,0:T(8,128)S(1)}) custom-call(f32[152,1024]{1,0:T(8,128)S(1)} %messages.5.refs_0_.refs_1_, bf16[152,512]{1,0:T(8,128)(2,1)S(1)} %collective-permute-done.35.refs_1_, ...), custom_call_target="tpu_custom_call" | custom-call | flops 400000000 | bytes 2000000 | tf_op jit(solution)/shard_map/conv_backward_upper/pallas_call | solution.py:66
  106.4 4.4 %conv_backward_lower.1 = (f32[128,1024]{1,0:T(8,128)}, f32[49,128]{1,0:T(8,128)}, f32[1,128]{1,0:T(1,128)}, f32[150,128]{1,0:T(8,128)}) custom-call(s32[18]{0:T(128)S(1)} %dynamic-slice_bitcast_fusion.1.refs_0_, f32[152,1024]{1,0:T(8,128)S(1)} %messages.5.refs_0_.refs_1_, bf16[152,512]{1,0:T(8,128)(2,1)S(1)} %collective-permute-done.30.refs_2_, ...), custom_call_target="tpu_custom_call" | custom-call | tf_op jit(solution)/shard_map/conv_backward_lower/pallas_call | solution.py:66
  (98 shorter events, 37.3 us)
Async XLA Ops:
  5.0 9.4 %collective-permute-start.1 = (bf16[128,1024]{1,0:T(8,128)(2,1)S(1)}, bf16[128,1024]{1,0:T(8,128)(2,1)S(1)}, u32[]{:S(2)}, u32[]{:S(2)}) collective-permute-start(bf16[128,1024]{1,0:T(8,128)(2,1)S(1)} %get-tuple-element.86.refs_3_.refs_2_.refs_0_.refs_4_), channel_id=1, source_target_pairs={{0,2},{1,3},{4,0},{5,1},{8,4},{9,5},{12,8},{13,9},{14,12},{15,13},... | collective-permute-start | bytes 786440 | tf_op jit(solution)/shard_map/ppermute | solution.py:51
  8.0 7.8 %collective-permute-start = (bf16[128,1024]{1,0:T(8,128)(2,1)S(1)}, bf16[128,1024]{1,0:T(8,128)(2,1)S(1)}, u32[]{:S(2)}, u32[]{:S(2)}) collective-permute-start(bf16[128,1024]{1,0:T(8,128)(2,1)S(1)} %get-tuple-element.86.refs_3_.refs_2_.refs_0_.refs_4_), channel_id=1, source_target_pairs={{0,4},{1,5},{4,8},{5,9},{8,12},{9,13},{12,14},{13,15},{14,10},{15,... | collective-permute-start | bytes 786440 | tf_op jit(solution)/shard_map/ppermute | solution.py:51
  15.8 2.7 %collective-permute-start.2 = (bf16[512,1024]{1,0:T(8,128)(2,1)S(1)}, bf16[512,1024]{1,0:T(8,128)(2,1)S(1)}, u32[]{:S(2)}, u32[]{:S(2)}) collective-permute-start(bf16[512,1024]{1,0:T(8,128)(2,1)S(1)} %get-tuple-element.91.refs_1_.refs_11_), channel_id=1, source_target_pairs={{0,1},{1,0},{2,3},{3,2},{4,5},{5,4},{6,7},{7,6},{8,9},{9,8},{10,11... | collective-permute-start | bytes 3145736 | tf_op jit(solution)/shard_map/ppermute | solution.py:51
  15.8 8.7 %collective-permute-start.3 = (bf16[128,1024]{1,0:T(8,128)(2,1)S(1)}, bf16[128,1024]{1,0:T(8,128)(2,1)S(1)}, u32[]{:S(2)}, u32[]{:S(2)}) collective-permute-start(bf16[128,1024]{1,0:T(8,128)(2,1)S(1)} %collective-permute-done.refs_4_.refs_8_), channel_id=1, source_target_pairs={{0,4},{1,5},{4,8},{5,9},{8,12},{9,13},{12,14},{13,15},{14,10},{15,... | collective-permute-start | bytes 786440 | tf_op jit(solution)/shard_map/ppermute | solution.py:51
  16.2 8.4 %collective-permute-start.4 = (bf16[128,1024]{1,0:T(8,128)(2,1)S(1)}, bf16[128,1024]{1,0:T(8,128)(2,1)S(1)}, u32[]{:S(2)}, u32[]{:S(2)}) collective-permute-start(bf16[128,1024]{1,0:T(8,128)(2,1)S(1)} %collective-permute-done.1.refs_3_.refs_1_), channel_id=1, source_target_pairs={{0,2},{1,3},{4,0},{5,1},{8,4},{9,5},{12,8},{13,9},{14,12},{15,13},... | collective-permute-start | bytes 786440 | tf_op jit(solution)/shard_map/ppermute | solution.py:51
  24.6 7.9 %collective-permute-start.5 = (bf16[128,1024]{1,0:T(8,128)(2,1)S(1)}, bf16[128,1024]{1,0:T(8,128)(2,1)S(1)}, u32[]{:S(2)}, u32[]{:S(2)}) collective-permute-start(bf16[128,1024]{1,0:T(8,128)(2,1)S(1)} %collective-permute-done.3.refs_6_.refs_7_), channel_id=1, source_target_pairs={{0,4},{1,5},{4,8},{5,9},{8,12},{9,13},{12,14},{13,15},{14,10},{15,... | collective-permute-start | bytes 786440 | tf_op jit(solution)/shard_map/ppermute | solution.py:51
  26.3 7.3 %collective-permute-start.6 = (bf16[128,1024]{1,0:T(8,128)(2,1)S(1)}, bf16[128,1024]{1,0:T(8,128)(2,1)S(1)}, u32[]{:S(2)}, u32[]{:S(2)}) collective-permute-start(bf16[128,1024]{1,0:T(8,128)(2,1)S(1)} %collective-permute-done.4.refs_5_.refs_2_), channel_id=1, source_target_pairs={{0,2},{1,3},{4,0},{5,1},{8,4},{9,5},{12,8},{13,9},{14,12},{15,13},... | collective-permute-start | bytes 786440 | tf_op jit(solution)/shard_map/ppermute | solution.py:51
  33.6 9.1 %collective-permute-start.10 = (bf16[512,1024]{1,0:T(8,128)(2,1)S(1)}, bf16[512,1024]{1,0:T(8,128)(2,1)S(1)}, u32[]{:S(2)}, u32[]{:S(2)}) collective-permute-start(bf16[512,1024]{1,0:T(8,128)(2,1)S(1)} %get-tuple-element.115), channel_id=1, source_target_pairs={{0,1},{1,0},{2,3},{3,2},{4,5},{5,4},{6,7},{7,6},{8,9},{9,8},{10,11... | collective-permute-start | bytes 3145736 | tf_op jit(solution)/shard_map/ppermute | solution.py:51
  33.6 6.5 %collective-permute-start.9 = (bf16[128,1024]{1,0:T(8,128)(2,1)S(1)}, bf16[128,1024]{1,0:T(8,128)(2,1)S(1)}, u32[]{:S(2)}, u32[]{:S(2)}) collective-permute-start(bf16[128,1024]{1,0:T(8,128)(2,1)S(1)} %collective-permute-done.5.refs_5_.refs_6_), channel_id=1, source_target_pairs={{0,1},{1,0},{2,3},{3,2},{4,5},{5,4},{6,7},{7,6},{8,9},{9,8},{10,11... | collective-permute-start | bytes 786440 | tf_op jit(solution)/shard_map/ppermute | solution.py:51
  34.1 6.0 %collective-permute-start.8 = (bf16[128,1024]{1,0:T(8,128)(2,1)S(1)}, bf16[128,1024]{1,0:T(8,128)(2,1)S(1)}, u32[]{:S(2)}, u32[]{:S(2)}) collective-permute-start(bf16[128,1024]{1,0:T(8,128)(2,1)S(1)} %collective-permute-done.6.refs_4_.refs_3_), channel_id=1, source_target_pairs={{0,1},{1,0},{2,3},{3,2},{4,5},{5,4},{6,7},{7,6},{8,9},{9,8},{10,11... | collective-permute-start | bytes 786440 | tf_op jit(solution)/shard_map/ppermute | solution.py:51
  34.2 6.0 %collective-permute-start.12 = (bf16[64,1024]{1,0:T(8,128)(2,1)S(1)}, bf16[64,1024]{1,0:T(8,128)(2,1)S(1)}, u32[]{:S(2)}, u32[]{:S(2)}) collective-permute-start(bf16[64,1024]{1,0:T(8,128)(2,1)S(1)} %slice.7), channel_id=1, source_target_pairs={{0,2},{1,3},{4,0},{5,1},{8,4},{9,5},{12,8},{13,9},{14,12},{15,13},... | collective-permute-start | bytes 393224 | tf_op jit(solution)/shard_map/ppermute | solution.py:51
  34.8 6.1 %collective-permute-start.7 = (bf16[64,1024]{1,0:T(8,128)(2,1)S(1)}, bf16[64,1024]{1,0:T(8,128)(2,1)S(1)}, u32[]{:S(2)}, u32[]{:S(2)}) collective-permute-start(bf16[64,1024]{1,0:T(8,128)(2,1)S(1)} %slice.6), channel_id=1, source_target_pairs={{0,4},{1,5},{4,8},{5,9},{8,12},{9,13},{12,14},{13,15},{14,10},{15,... | collective-permute-start | bytes 393224 | tf_op jit(solution)/shard_map/ppermute | solution.py:51
  40.1 2.6 %collective-permute-start.14 = (bf16[64,1024]{1,0:T(8,128)(2,1)S(1)}, bf16[64,1024]{1,0:T(8,128)(2,1)S(1)}, u32[]{:S(2)}, u32[]{:S(2)}) collective-permute-start(bf16[64,1024]{1,0:T(8,128)(2,1)S(1)} %collective-permute-done.12.refs_13_.refs_5_), channel_id=1, source_target_pairs={{0,1},{1,0},{2,3},{3,2},{4,5},{5,4},{6,7},{7,6},{8,9},{9,8},{10,11... | collective-permute-start | bytes 393224 | tf_op jit(solution)/shard_map/ppermute | solution.py:51
  46.7 14.6 %collective-permute-start.20 = (bf16[1024,1024]{1,0:T(8,128)(2,1)S(1)}, bf16[1024,1024]{1,0:T(8,128)(2,1)S(1)}, u32[]{:S(2)}, u32[]{:S(2)}) collective-permute-start(bf16[1024,1024]{1,0:T(8,128)(2,1)S(1)} %pack_blocks.1.refs_2_.refs_4_), channel_id=1, source_target_pairs={{0,1},{1,0},{2,3},{3,2},{4,5},{5,4},{6,7},{7,6},{8,9},{9,8},{10,11... | collective-permute-start | bytes 6291464 | tf_op jit(solution)/shard_map/ppermute | solution.py:51
  47.0 4.7 %collective-permute-start.16 = (f32[160,128]{1,0:T(8,128)S(1)}, f32[160,128]{1,0:T(8,128)S(1)}, u32[]{:S(2)}, u32[]{:S(2)}) collective-permute-start(f32[160,128]{1,0:T(8,128)S(1)} %get-tuple-element.125), channel_id=1, source_target_pairs={{0,2},{1,3},{2,0},{3,1},{4,6},{5,7},{6,4},{7,5},{8,10},{9,11},{10,... | collective-permute-start | bytes 245768 | tf_op jit(solution)/shard_map/ppermute | solution.py:51
  48.1 4.6 %collective-permute-start.17 = (f32[160,128]{1,0:T(8,128)S(1)}, f32[160,128]{1,0:T(8,128)S(1)}, u32[]{:S(2)}, u32[]{:S(2)}) collective-permute-start(f32[160,128]{1,0:T(8,128)S(1)} %get-tuple-element.126), channel_id=1, source_target_pairs={{0,4},{1,5},{2,6},{3,7},{4,0},{5,1},{6,2},{7,3},{8,12},{9,13},{10,... | collective-permute-start | bytes 245768 | tf_op jit(solution)/shard_map/ppermute | solution.py:51
  49.6 5.3 %collective-permute-start.18 = (f32[160,128]{1,0:T(8,128)S(1)}, f32[160,128]{1,0:T(8,128)S(1)}, u32[]{:S(2)}, u32[]{:S(2)}) collective-permute-start(f32[160,128]{1,0:T(8,128)S(1)} %get-tuple-element.127), channel_id=1, source_target_pairs={{0,6},{1,7},{2,4},{3,5},{4,2},{5,3},{6,0},{7,1},{8,14},{9,15},{10,... | collective-permute-start | bytes 245768 | tf_op jit(solution)/shard_map/ppermute | solution.py:51
  55.0 6.3 %collective-permute-start.19 = (f32[160,128]{1,0:T(8,128)S(1)}, f32[160,128]{1,0:T(8,128)S(1)}, u32[]{:S(2)}, u32[]{:S(2)}) collective-permute-start(f32[160,128]{1,0:T(8,128)S(1)} %fold_chips.1.refs_2_.refs_1_), channel_id=1, source_target_pairs={{0,8},{1,9},{2,10},{3,11},{4,12},{5,13},{6,14},{7,15},{8,0},{9,1},... | collective-permute-start | bytes 245768 | tf_op jit(solution)/shard_map/ppermute | solution.py:51
  61.4 5.0 %collective-permute-start.23 = (bf16[160,128]{1,0:T(8,128)(2,1)S(1)}, bf16[160,128]{1,0:T(8,128)(2,1)S(1)}, u32[]{:S(2)}, u32[]{:S(2)}) collective-permute-start(bf16[160,128]{1,0:T(8,128)(2,1)S(1)} %class_grad.1.refs_1_), channel_id=1, source_target_pairs={{0,6},{1,7},{2,4},{3,5},{4,2},{5,3},{6,0},{7,1},{8,14},{9,15},{10,... | collective-permute-start | bytes 122888 | tf_op jit(solution)/shard_map/ppermute | solution.py:51
  62.2 4.1 %collective-permute-start.22 = (bf16[160,128]{1,0:T(8,128)(2,1)S(1)}, bf16[160,128]{1,0:T(8,128)(2,1)S(1)}, u32[]{:S(2)}, u32[]{:S(2)}) collective-permute-start(bf16[160,128]{1,0:T(8,128)(2,1)S(1)} %class_grad.1.refs_1_), channel_id=1, source_target_pairs={{0,4},{1,5},{2,6},{3,7},{4,0},{5,1},{6,2},{7,3},{8,12},{9,13},{10,... | collective-permute-start | bytes 122888 | tf_op jit(solution)/shard_map/ppermute | solution.py:51
  64.0 4.0 %collective-permute-start.21 = (bf16[160,128]{1,0:T(8,128)(2,1)S(1)}, bf16[160,128]{1,0:T(8,128)(2,1)S(1)}, u32[]{:S(2)}, u32[]{:S(2)}) collective-permute-start(bf16[160,128]{1,0:T(8,128)(2,1)S(1)} %class_grad.1.refs_1_), channel_id=1, source_target_pairs={{0,2},{1,3},{2,0},{3,1},{4,6},{5,7},{6,4},{7,5},{8,10},{9,11},{10,... | collective-permute-start | bytes 122888 | tf_op jit(solution)/shard_map/ppermute | solution.py:51
  70.5 3.6 %collective-permute-start.25 = (bf16[512,1024]{1,0:T(8,128)(2,1)S(1)}, bf16[512,1024]{1,0:T(8,128)(2,1)S(1)}, u32[]{:S(2)}, u32[]{:S(2)}) collective-permute-start(bf16[512,1024]{1,0:T(8,128)(2,1)S(1)} %get-tuple-element.130.refs_3_.refs_1_.refs_2_), channel_id=1, source_target_pairs={{0,1},{1,0},{2,3},{3,2},{4,5},{5,4},{6,7},{7,6},{8,9},{9,8},{10,11... | collective-permute-start | bytes 3145736 | tf_op jit(solution)/shard_map/ppermute | solution.py:51
  74.6 8.0 %collective-permute-start.27 = (bf16[80,1024]{1,0:T(8,128)(2,1)S(1)}, bf16[80,1024]{1,0:T(8,128)(2,1)S(1)}, u32[]{:S(2)}, u32[]{:S(2)}) collective-permute-start(bf16[80,1024]{1,0:T(8,128)(2,1)S(1)} %get-tuple-element.139), channel_id=1, source_target_pairs={{0,4},{1,5},{4,8},{5,9},{8,12},{9,13},{12,14},{13,15},{14,10},{15,... | collective-permute-start | bytes 491528 | tf_op jit(solution)/shard_map/ppermute | solution.py:51
  75.0 6.0 %collective-permute-start.31 = (bf16[72,1024]{1,0:T(8,128)(2,1)S(1)}, bf16[72,1024]{1,0:T(8,128)(2,1)S(1)}, u32[]{:S(2)}, u32[]{:S(2)}) collective-permute-start(bf16[72,1024]{1,0:T(8,128)(2,1)S(1)} %get-tuple-element.144), channel_id=1, source_target_pairs={{0,2},{1,3},{4,0},{5,1},{8,4},{9,5},{12,8},{13,9},{14,12},{15,13},... | collective-permute-start | bytes 442376 | tf_op jit(solution)/shard_map/ppermute | solution.py:51
  81.0 8.8 %collective-permute-start.32 = (bf16[152,1024]{1,0:T(8,128)(2,1)S(1)}, bf16[152,1024]{1,0:T(8,128)(2,1)S(1)}, u32[]{:S(2)}, u32[]{:S(2)}) collective-permute-start(bf16[152,1024]{1,0:T(8,128)(2,1)S(1)} %walk_sum.9), channel_id=1, source_target_pairs={{0,2},{1,3},{4,0},{5,1},{8,4},{9,5},{12,8},{13,9},{14,12},{15,13},... | collective-permute-start | bytes 933896 | tf_op jit(solution)/shard_map/ppermute | solution.py:51
  82.7 8.6 %collective-permute-start.28 = (bf16[152,1024]{1,0:T(8,128)(2,1)S(1)}, bf16[152,1024]{1,0:T(8,128)(2,1)S(1)}, u32[]{:S(2)}, u32[]{:S(2)}) collective-permute-start(bf16[152,1024]{1,0:T(8,128)(2,1)S(1)} %walk_sum.6), channel_id=1, source_target_pairs={{0,4},{1,5},{4,8},{5,9},{8,12},{9,13},{12,14},{13,15},{14,10},{15,... | collective-permute-start | bytes 933896 | tf_op jit(solution)/shard_map/ppermute | solution.py:51
  89.8 7.8 %collective-permute-start.33 = (bf16[152,1024]{1,0:T(8,128)(2,1)S(1)}, bf16[152,1024]{1,0:T(8,128)(2,1)S(1)}, u32[]{:S(2)}, u32[]{:S(2)}) collective-permute-start(bf16[152,1024]{1,0:T(8,128)(2,1)S(1)} %walk_sum.10.refs_7_), channel_id=1, source_target_pairs={{0,2},{1,3},{4,0},{5,1},{8,4},{9,5},{12,8},{13,9},{14,12},{15,13},... | collective-permute-start | bytes 933896 | tf_op jit(solution)/shard_map/ppermute | solution.py:51
  91.3 7.6 %collective-permute-start.29 = (bf16[152,1024]{1,0:T(8,128)(2,1)S(1)}, bf16[152,1024]{1,0:T(8,128)(2,1)S(1)}, u32[]{:S(2)}, u32[]{:S(2)}) collective-permute-start(bf16[152,1024]{1,0:T(8,128)(2,1)S(1)} %walk_sum.7.refs_6_), channel_id=1, source_target_pairs={{0,4},{1,5},{4,8},{5,9},{8,12},{9,13},{12,14},{13,15},{14,10},{15,... | collective-permute-start | bytes 933896 | tf_op jit(solution)/shard_map/ppermute | solution.py:51
  97.7 5.3 %collective-permute-start.36 = (bf16[152,512]{1,0:T(8,128)(2,1)S(1)}, bf16[152,512]{1,0:T(8,128)(2,1)S(1)}, u32[]{:S(2)}, u32[]{:S(2)}) collective-permute-start(bf16[152,512]{1,0:T(8,128)(2,1)S(1)} %get-tuple-element.153), channel_id=1, source_target_pairs={{0,2},{1,3},{4,0},{5,1},{8,4},{9,5},{12,8},{13,9},{14,12},{15,13},... | collective-permute-start | bytes 466952 | tf_op jit(solution)/shard_map/ppermute | solution.py:51
  99.0 5.3 %collective-permute-start.35 = (bf16[152,512]{1,0:T(8,128)(2,1)S(1)}, bf16[152,512]{1,0:T(8,128)(2,1)S(1)}, u32[]{:S(2)}, u32[]{:S(2)}) collective-permute-start(bf16[152,512]{1,0:T(8,128)(2,1)S(1)} %get-tuple-element.152), channel_id=1, source_target_pairs={{0,4},{1,5},{4,8},{5,9},{8,12},{9,13},{12,14},{13,15},{14,10},{15,... | collective-permute-start | bytes 466952 | tf_op jit(solution)/shard_map/ppermute | solution.py:51
  99.9 6.4 %collective-permute-start.34 = (bf16[152,512]{1,0:T(8,128)(2,1)S(1)}, bf16[152,512]{1,0:T(8,128)(2,1)S(1)}, u32[]{:S(2)}, u32[]{:S(2)}) collective-permute-start(bf16[152,512]{1,0:T(8,128)(2,1)S(1)} %get-tuple-element.149), channel_id=1, source_target_pairs={{0,2},{1,3},{4,0},{5,1},{8,4},{9,5},{12,8},{13,9},{14,12},{15,13},... | collective-permute-start | bytes 466952 | tf_op jit(solution)/shard_map/ppermute | solution.py:51
  101.1 5.3 %collective-permute-start.30 = (bf16[152,512]{1,0:T(8,128)(2,1)S(1)}, bf16[152,512]{1,0:T(8,128)(2,1)S(1)}, u32[]{:S(2)}, u32[]{:S(2)}) collective-permute-start(bf16[152,512]{1,0:T(8,128)(2,1)S(1)} %get-tuple-element.140), channel_id=1, source_target_pairs={{0,4},{1,5},{4,8},{5,9},{8,12},{9,13},{12,14},{13,15},{14,10},{15,... | collective-permute-start | bytes 466952 | tf_op jit(solution)/shard_map/ppermute | solution.py:51
  (14 other events, 28.4 us)

commit v4 on v3

--- a/solution.py
+++ b/solution.py
@@ -141,7 +141,7 @@
     gain_sum_ref[...] = jnp.sum(total, axis=1, keepdims=True)
 
 
-def mix_kernel(places_ref, w_out_ref, scale_ref, head_ref, head_pad_ref, mix_ref, walk_ref):
+def mix_kernel(places_ref, w_out_ref, scale_ref, head_ref, head_pad_ref, mix_ref, walk_ref, my_head_ref, my_scale_ref):
     for d in range(CHIPS):
         for side in range(2):
             walk_ref[:, (side * CHIPS + d) * LANE : (side * CHIPS + d + 1) * LANE] = w_out_ref[:, columns(places_ref, 2 * d + side)]
@@ -150,6 +150,8 @@
     head = head_pad_ref[...]
     scaled = (head.astype(F32) * scale_ref[...]).astype(BF)
     mix_ref[...] = dot(w_out_ref[...], scaled, ((1,), (1,))).astype(BF)
+    my_head_ref[...] = head_pad_ref[:, columns(places_ref, MINE)]
+    my_scale_ref[...] = scale_ref[:, columns(places_ref, MINE)]
 
 
 def turn_kernel(own_ref, sib_ref, out_ref):
@@ -204,8 +206,8 @@
     refs[-1][...] = jnp.concatenate([ref[...] for ref in refs[:-1]], axis=0)
 
 
-def forward_kernel(places_ref, acc_ref, got_ref, sums_ref, sib_sums_ref, pair_sums_ref, gain_sum_ref, mix_ref, head_ref, x_ref, own_ref, sib_ref, *refs):
-    blocks, (pre_ref, hidden_ref, stats_ref, keep_ref, give_ref, scratch) = refs[:-6], refs[-6:]
+def forward_kernel(marks_ref, acc_ref, got_ref, sums_ref, sib_sums_ref, pair_sums_ref, gain_sum_ref, mix_ref, head_ref, x_ref, own_ref, sib_ref, *refs):
+    blocks, (pre_ref, hidden_ref, stats_ref, keep_ref, give_ref) = refs[:-5], refs[-5:]
     held = jnp.concatenate([b[...] for b in blocks], axis=0)
     at = slice(CHIPS // 2 * LANE, (CHIPS // 2 + 1) * LANE)
     acc = dot(jnp.concatenate([own_ref[:, at], sib_ref[:, at]], axis=1), held, ((1,), (0,)))
@@ -223,14 +225,13 @@
     pre_ref[...] = pre_act
     hidden = (pre_act * (0.5 * (1.0 + lax.erf(pre_act * 0.7071067811865476)))).astype(BF)
     hidden_ref[...] = hidden
-    my_head = head_ref[:, columns(places_ref, MINE)]
-    logits = dot(mix_ref[...], hidden, ((0,), (0,))) + dot(my_head, x_ref[...], ((1,), (0,)))
-    core = places_ref[CORE]
+    logits = dot(mix_ref[...], hidden, ((0,), (0,))) + dot(head_ref[...], x_ref[...], ((1,), (0,)))
     chunks = keep_ref.shape[0]
-    for g in range(2 * chunks):
-        scratch[g] = logits[:, g * LANE : (g + 1) * LANE]
-    keep_ref[...] = scratch[pl.ds(chunks * core, chunks)]
-    give_ref[...] = scratch[pl.ds(chunks - chunks * core, chunks)]
+    core = jnp.broadcast_to(marks_ref[0:1, :], keep_ref.shape[1:]) == 1
+    for g in range(chunks):
+        low, high = logits[:, g * LANE : (g + 1) * LANE], logits[:, (chunks + g) * LANE : (chunks + g + 1) * LANE]
+        keep_ref[g] = jnp.where(core, high, low)
+        give_ref[g] = jnp.where(core, low, high)
 
 
 def slope_kernel(pre_ref, stats_ref, slope_ref):
@@ -283,26 +284,31 @@
         out_ref[g] = pick(marks_ref, g // 2, g % 2, chunks).astype(BF)
 
 
-def grad_kernel(places_ref, own_ref, sib_ref, mix_ref, slope_ref, grad_ref, scaled_ref):
-    core = places_ref[CORE]
+def grad_kernel(marks_ref, own_ref, sib_ref, mix_ref, slope_ref, grad_ref, scaled_ref):
     chunks = own_ref.shape[0]
+    core = jnp.broadcast_to(marks_ref[0:1, :], own_ref.shape[1:]) == 1
     for g in range(chunks):
-        grad_ref[:, pl.ds(pl.multiple_of((core * chunks + g) * LANE, LANE), LANE)] = own_ref[g]
-        grad_ref[:, pl.ds(pl.multiple_of(((1 - core) * chunks + g) * LANE, LANE), LANE)] = sib_ref[g]
+        own, sib = own_ref[g].astype(F32), sib_ref[g].astype(F32)
+        grad_ref[:, g * LANE : (g + 1) * LANE] = jnp.where(core, sib, own).astype(BF)
+        grad_ref[:, (chunks + g) * LANE : (chunks + g + 1) * LANE] = jnp.where(core, own, sib).astype(BF)
     scaled_ref[...] = (dot(mix_ref[...], grad_ref[...], ((1,), (0,))) * slope_ref[...]).astype(BF)
 
 
-def branch_kernel(hidden_ref, grad_ref, w_out_ref, scaled_ref, pre_ref, gain_sum_ref, mixed_ref, keep_ref, give_ref):
+def branch_kernel(hidden_ref, grad_ref, w_out_ref, scaled_ref, pre_ref, gain_sum_ref, mixed_ref, give_ref, means_ref):
     mixed = dot(hidden_ref[...], grad_ref[...], ((1,), (1,))).astype(BF)
     mixed_ref[...] = mixed
-    branch = dot(mixed, w_out_ref[...], ((0,), (0,)))
+    width = give_ref.shape[1]
     wide = scaled_ref[...].astype(F32)
     mean_part = jnp.sum(wide * gain_sum_ref[...], axis=0, keepdims=True)
     proj_part = jnp.sum(wide * pre_ref[...], axis=0, keepdims=True)
     means = jnp.concatenate([mean_part, proj_part, jnp.zeros((SUB_ROWS - 2, wide.shape[1]), F32)], axis=0)
+    means_ref[...] = means
+    give_ref[...] = jnp.concatenate([dot(mixed, w_out_ref[:, width:], ((0,), (0,))), means], axis=0).astype(BF)
+
+
+def own_branch_kernel(mixed_ref, w_out_ref, means_ref, keep_ref):
     width = keep_ref.shape[1]
-    for side, out in enumerate((keep_ref, give_ref)):
-        out[...] = jnp.concatenate([branch[:, side * width : (side + 1) * width], means], axis=0).astype(out.dtype)
+    keep_ref[...] = jnp.concatenate([dot(mixed_ref[...], w_out_ref[:, :width], ((0,), (0,))), means_ref[...]], axis=0)
 
 
 def message_of(d, turned_ref, own_ref, got_ref, keep_ref, sib_ref):
@@ -372,10 +378,9 @@
         copy.wait()
 
 
-def head_kernel(classes, places_ref, x_ref, head_ref, grad_ref, out_grad_ref, d_head_ref, loss_ref):
-    my_head = head_ref[:, columns(places_ref, MINE)]
+def head_kernel(classes, x_ref, head_ref, grad_ref, out_grad_ref, d_head_ref, loss_ref):
     grad = grad_ref[...]
-    out_grad_ref[...] = dot(my_head, grad, ((0,), (0,)))
+    out_grad_ref[...] = dot(head_ref[...], grad, ((0,), (0,)))
     d_head_ref[...] = dot(grad, x_ref[...], ((1,), (1,)))
     loss_ref[...] = (jnp.sum(grad[classes : classes + 2].astype(F32)) / grad.shape[1]).reshape(1, 1)
 
@@ -425,7 +430,7 @@
     add_taps(range(4), copies, copies_x, sums)
 
 
-def lower_kernel(classes, places_ref, mine_ref, forth_ref, back_ref, conv_ref, stats_ref, taps, copies_x, out_grad_ref, head_grad_ref, head_ref, scale_ref,
+def lower_kernel(classes, mine_ref, forth_ref, back_ref, conv_ref, stats_ref, taps, copies_x, out_grad_ref, head_grad_ref, head_ref, scale_ref,
                  d_upper_ref, sums_ref, grid_ref, extra_ref, d_x_ref, d_dw_ref, d_scale_ref, d_head_ref, grid_pad, copies, sums):
     rows = conv_ref.shape[0]
     width = forth_ref.shape[1]
@@ -442,9 +447,8 @@
         d_x_ref[:, at] = out_grad_ref[:, at] + conv_rows(copies, taps, 4 * g, True).reshape(LANE, LANE).T
     add_taps(range(4, 8), copies, copies_x, sums)
     d_dw_ref[...] = jnp.sum(sums[...], axis=1)
-    at = columns(places_ref, MINE)
-    d_scale_ref[...] = jnp.sum(head_ref[:, at].astype(F32) * branch, axis=0, keepdims=True)
-    d_head_ref[...] = (head_grad_ref[...] + scale_ref[:, at] * branch)[:classes]
+    d_scale_ref[...] = jnp.sum(head_ref[...].astype(F32) * branch, axis=0, keepdims=True)
+    d_head_ref[...] = (head_grad_ref[...] + scale_ref[...] * branch)[:classes]
 
 
 def walk_step(walk, step):
@@ -500,16 +504,16 @@
     )
     so_far = hold(walk, 2, *so_far)
     walk_step(walk, 3)
-    head_pad, mix, w_out_walk = call(
+    made = call(
         mix_kernel,
-        [((CLASS_ROWS, channels), BF), ((units, CLASS_ROWS), BF), ((units, channels), BF)],
+        [((CLASS_ROWS, channels), BF), ((units, CLASS_ROWS), BF), ((units, channels), BF), ((CLASS_ROWS, rows), BF), ((1, rows), F32)],
         spot + vm(w_out, scale_row, w_head.T), flops=1e9, moved=4e6, limit=12, name="mix_ready", after=[so_far[2]],
     )
     so_far = call(
         functools.partial(next_kernel, (2, 6)), [f32s, bf16s, sums_size],
         vm(w_own, w_sib, *so_far, *walk[2], *walk[6]), flops=6e8, moved=4e6, limit=16, name="forward_next",
     )
-    *so_far, head_pad, mix, w_out_walk = hold(walk, 3, *so_far, head_pad, mix, w_out_walk)
+    *so_far, head_pad, mix, w_out_walk, my_head, my_scale = hold(walk, 3, *so_far, *made)
     acc, give, sums = so_far
     got, sib_sums = send(give, SIBLING), send(sums, SIBLING)
     walk_step(walk, 4)
@@ -525,8 +529,8 @@
     chunk = lambda count, kind=F32: ((count, CLASS_ROWS, LANE), kind)
     pre_act, hidden, stats, keep, give = call(
         forward_kernel, [f32s, bf16s, sums_size, chunk(chunks), chunk(chunks)],
-        spot + vm(acc, got, sums, sib_sums, pair_sums, gain_sum, mix, head_pad, features, w_own, w_give, *far),
-        [pltpu.VMEM((2 * chunks, CLASS_ROWS, LANE), F32)], flops=1e9, moved=4e6, limit=16, name="forward_hidden",
+        mark + vm(acc, got, sums, sib_sums, pair_sums, gain_sum, mix, my_head, features, w_own, w_give, *far),
+        flops=1e9, moved=4e6, limit=16, name="forward_hidden",
     )
 
     own_chunk = ((CLASS_ROWS, LANE), F32)
@@ -550,13 +554,16 @@
     )
 
     grad, scaled = call(
-        grad_kernel, [((CLASS_ROWS, tokens), BF), bf16s], spot + vm(grad, send(grad, SIBLING), mix, slope), flops=6e8, moved=4e6, limit=12, name="hidden_grad",
+        grad_kernel, [((CLASS_ROWS, tokens), BF), bf16s], mark + vm(grad, send(grad, SIBLING), mix, slope), flops=6e8, moved=4e6, limit=12, name="hidden_grad",
     )
     got = send(scaled, SIBLING)
     extra_rows = CLASS_ROWS + SUB_ROWS
-    mixed, keep, give = call(
-        branch_kernel, [((units, CLASS_ROWS), BF), ((extra_rows, half_channels), F32), ((extra_rows, half_channels), BF)],
+    mixed, give, means = call(
+        branch_kernel, [((units, CLASS_ROWS), BF), ((extra_rows, half_channels), BF), ((SUB_ROWS, tokens), F32)],
         vm(hidden, grad, w_out_walk, scaled, pre_act, gain_sum), flops=8e8, moved=4e6, limit=12, name="class_products",
+    )
+    (keep,) = call(
+        own_branch_kernel, [((extra_rows, half_channels), F32)], vm(mixed, w_out_walk, means), flops=4e8, moved=4e6, limit=8, name="class_products_own",
     )
     sources = vm(turned, scaled, got, keep, send(give, SIBLING))
     height = rows + EXTRA
@@ -570,7 +577,7 @@
     )
     out_grad, head_grad, mean_loss = call(
         functools.partial(head_kernel, classes), [((rows, tokens), F32), ((CLASS_ROWS, rows), F32), ((1, 1), F32)],
-        spot + vm(features, head_pad, grad), flops=4e8, moved=2e6, limit=8, name="class_head", after=[forth],
+        vm(features, my_head, grad), flops=4e8, moved=2e6, limit=8, name="class_head", after=[forth],
     )
     beside = {3: [], 2: [d_w_out_done, out_grad], 1: []}
     for step in range(CHIPS // 2 - 1, 0, -1):
@@ -606,7 +613,7 @@
     d_features, d_dw, d_scale, d_head = call(
         functools.partial(lower_kernel, classes),
         [((rows, tokens), F32), ((KS * KS, rows), F32), ((1, rows), F32), ((classes, rows), F32)],
-        spot + vm(mine, *ends[1], conv_out, stats, taps, copies_x, out_grad, head_grad, head_pad, scale_row, *upper),
+        vm(mine, *ends[1], conv_out, stats, taps, copies_x, out_grad, head_grad, my_head, my_scale, *upper),
         [grid_shape, pltpu.VMEM(copies_size, F32), pltpu.VMEM((KS * KS, 8, LANE), F32)], limit=16, name="conv_backward_lower",
     )
     return (d_features, d_dw.T, d_scale[0], d_w_in, d_w_out, d_head.T, mean_loss[0])

time: 111 us -> 109 us (0.982)
  Pallas kernels: 33.7 us -> 31.5 us
    pallas_call x33 -> x34, Pallas kernels: 33.7 us -> 31.5 us  [call(): pl.pallas_call(body, out_shape=[jax.ShapeDtypeStruct(s, d) for s, d in ou...]
  transfers between devices with their start and end apart: 37 -> 37, of which waited for: 23 -> 23; matrix products, arithmetic and copies ran while one was open for 1% -> 1% of each run, Pallas kernels for 21% -> 20%
where the time goes in v4:
time: 109 us
  waiting for transfers between devices  38.7 us (36%)
  starting transfers between devices  32.1 us (29%)
  Pallas kernels  31.5 us (29%)
  local copies, waits for them, and re-layouts  5.47 us (5%)
    ppermute x37, waiting for transfers between devices, send(): return lax.ppermute(value, 'ch', perm)  38.7 us
    ppermute x37, starting transfers between devices, send(): return lax.ppermute(value, 'ch', perm)  32.1 us
    pallas_call x34, Pallas kernels, call(): pl.pallas_call(body, out_shape=[jax.ShapeDtypeStruct(s, d) for s, d in ou...  31.5 us
    unnamed x18, local copies, waits for them, and re-layouts  4 us
  transfers between devices with their start and end apart: 37, of which 23 were waited for; matrix products, arithmetic and copies ran while one was open for 1% of the time, Pallas kernels for 20%

profile of v4, /device:TPU:0, one launch (start us, length us, event | category | flops | bytes accessed | tf_op | source)
XLA Modules:
  0.0 108.7 jit_solution(8565609700663612632)
XLA Ops:
  2.3 2.6 %conv_forward.1 = (bf16[128,1024]{1,0:T(8,128)(2,1)S(1)}, bf16[128,1024]{1,0:T(8,128)(2,1)S(1)}, f32[49,128]{1,0:T(8,128)S(1)}) custom-call(bf16[128,1024]{1,0:T(8,128)(2,1)S(1)} %copy-done.1, f32[49,128]{1,0:T(8,128)S(1)} %bitcast.13), custom_call_target="tpu_custom_call" | custom-call | tf_op jit(solution)/shard_map/conv_forward/pallas_call | solution.py:66
  5.0 3.0 %collective-permute-start.1 = (bf16[128,1024]{1,0:T(8,128)(2,1)S(1)}, bf16[128,1024]{1,0:T(8,128)(2,1)S(1)}, u32[]{:S(2)}, u32[]{:S(2)}) collective-permute-start(bf16[128,1024]{1,0:T(8,128)(2,1)S(1)} %get-tuple-element.90.refs_3_.refs_2_.refs_0_), channel_id=1, source_target_pairs={{0,2},{1,3},{4,0},{5,1},{8,4},{9,5},{12,8},{13,9},{14,12},{15,13},... | collective-permute-start | bytes 786440 | tf_op jit(solution)/shard_map/ppermute | solution.py:51
  9.6 1.6 %copy-done = bf16[512,2048]{1,0:T(8,128)(2,1)S(1)} copy-done((bf16[512,2048]{1,0:T(8,128)(2,1)S(1)}, bf16[512,2048]{1,0:T(8,128)(2,1)}, u32[]{:S(2)}) %copy-start) | copy-done | bytes 2097176
  11.9 1.4 %weights_ready.1 = (bf16[512,1024]{1,0:T(8,128)(2,1)S(1)}, bf16[512,1024]{1,0:T(8,128)(2,1)S(1)}, f32[512,1]{1,0:T(8,128)S(1)}) custom-call(s32[18]{0:T(128)S(1)} %dynamic-slice_bitcast_fusion.1.refs_0_, bf16[512,2048]{1,0:T(8,128)(2,1)S(1)} %copy-done, f32[1,2048]{1,0:T(1,128)S(1)} %bitcast.14, ...), custom_call_target="tpu_custom_call" | custom-call | flops 400000000 | bytes 4000000 | tf_op jit(solution)/shard_map/weights_ready/pallas_call | solution.py:66
  14.3 1.4 %collective-permute-done.refs_4_.refs_8_ = bf16[128,1024]{1,0:T(8,128)(2,1)S(1)} collective-permute-done((bf16[128,1024]{1,0:T(8,128)(2,1)S(1)}, bf16[128,1024]{1,0:T(8,128)(2,1)S(1)}, u32[]{:S(2)}, u32[]{:S(2)}) %collective-permute-start) | collective-permute-done | bytes 262176 | tf_op jit(solution)/shard_map/ppermute | solution.py:51
  16.2 1.6 %collective-permute-start.4 = (bf16[128,1024]{1,0:T(8,128)(2,1)S(1)}, bf16[128,1024]{1,0:T(8,128)(2,1)S(1)}, u32[]{:S(2)}, u32[]{:S(2)}) collective-permute-start(bf16[128,1024]{1,0:T(8,128)(2,1)S(1)} %collective-permute-done.1.refs_3_.refs_1_), channel_id=1, source_target_pairs={{0,2},{1,3},{4,0},{5,1},{8,4},{9,5},{12,8},{13,9},{14,12},{15,13},... | collective-permute-start | bytes 786440 | tf_op jit(solution)/shard_map/ppermute | solution.py:51
  18.4 1.4 %forward_first.1 = (f32[512,1024]{1,0:T(8,128)S(1)}, f32[512,1024]{1,0:T(8,128)S(1)}, f32[8,1024]{1,0:T(8,128)S(1)}) custom-call(bf16[512,1024]{1,0:T(8,128)(2,1)S(1)} %get-tuple-element.94.refs_0_.refs_10_, bf16[512,1024]{1,0:T(8,128)(2,1)S(1)} %collective-permute-done.2.refs_1_, bf16[128,1024]{1,0:T(8,128)(2,1)S(1)} %get-tuple-element.90.refs_3_.refs_2_.refs_0_, ...), custom_call_target="tpu_custom_call" | custom-call | flops 1000000000 | bytes 4000000 | tf_op jit(solution)/shard_map/forward_first/pallas_call | solution.py:66
  19.8 4.7 %collective-permute-done.3.refs_6_.refs_7_ = bf16[128,1024]{1,0:T(8,128)(2,1)S(1)} collective-permute-done((bf16[128,1024]{1,0:T(8,128)(2,1)S(1)}, bf16[128,1024]{1,0:T(8,128)(2,1)S(1)}, u32[]{:S(2)}, u32[]{:S(2)}) %collective-permute-start.3) | collective-permute-done | bytes 262176 | tf_op jit(solution)/shard_map/ppermute | solution.py:51
  24.6 1.7 %collective-permute-start.5 = (bf16[128,1024]{1,0:T(8,128)(2,1)S(1)}, bf16[128,1024]{1,0:T(8,128)(2,1)S(1)}, u32[]{:S(2)}, u32[]{:S(2)}) collective-permute-start(bf16[128,1024]{1,0:T(8,128)(2,1)S(1)} %collective-permute-done.3.refs_6_.refs_7_), channel_id=1, source_target_pairs={{0,4},{1,5},{4,8},{5,9},{8,12},{9,13},{12,14},{13,15},{14,10},{15,... | collective-permute-start | bytes 786440 | tf_op jit(solution)/shard_map/ppermute | solution.py:51
  27.5 1.9 %mix_ready.1 = (bf16[160,2048]{1,0:T(8,128)(2,1)S(1)}, bf16[512,160]{1,0:T(8,128)(2,1)S(1)}, bf16[512,2048]{1,0:T(8,128)(2,1)S(1)}, bf16[160,128]{1,0:T(8,128)(2,1)S(1)}, f32[1,128]{1,0:T(1,128)S(1)}) custom-call(s32[18]{0:T(128)S(1)} %dynamic-slice_bitcast_fusion.1.refs_0_, bf16[512,2048]{1,0:T(8,128)(2,1)S(1)} %copy-done.6, f32[1,2048]{1,0:T(1,128)S(1)} %bitcast.18, ...), custom_call_target="tpu_custom_call" | custom-call | flops 1000000000 | bytes 4000000 | tf_op jit(solution)/shard_map/mix_ready/pallas_call | solution.py:66
  29.3 3.2 %collective-permute-done.5.refs_5_.refs_6_ = bf16[128,1024]{1,0:T(8,128)(2,1)S(1)} collective-permute-done((bf16[128,1024]{1,0:T(8,128)(2,1)S(1)}, bf16[128,1024]{1,0:T(8,128)(2,1)S(1)}, u32[]{:S(2)}, u32[]{:S(2)}) %collective-permute-start.5) | collective-permute-done | bytes 262176 | tf_op jit(solution)/shard_map/ppermute | solution.py:51
  34.8 1.7 %collective-permute-start.7 = (bf16[64,1024]{1,0:T(8,128)(2,1)S(1)}, bf16[64,1024]{1,0:T(8,128)(2,1)S(1)}, u32[]{:S(2)}, u32[]{:S(2)}) collective-permute-start(bf16[64,1024]{1,0:T(8,128)(2,1)S(1)} %slice.6), channel_id=1, source_target_pairs={{0,4},{1,5},{4,8},{5,9},{8,12},{9,13},{12,14},{13,15},{14,10},{15,... | collective-permute-start | bytes 393224 | tf_op jit(solution)/shard_map/ppermute | solution.py:51
  36.5 3.6 %collective-permute-done.12.refs_13_.refs_5_ = bf16[64,1024]{1,0:T(8,128)(2,1)S(1)} collective-permute-done((bf16[64,1024]{1,0:T(8,128)(2,1)S(1)}, bf16[64,1024]{1,0:T(8,128)(2,1)S(1)}, u32[]{:S(2)}, u32[]{:S(2)}) %collective-permute-start.12) | collective-permute-done | bytes 131104 | tf_op jit(solution)/shard_map/ppermute | solution.py:51
  42.7 1.5 %forward_hidden.1 = (f32[512,1024]{1,0:T(8,128)S(1)}, bf16[512,1024]{1,0:T(8,128)(2,1)S(1)}, f32[8,1024]{1,0:T(8,128)S(1)}, f32[4,160,128]{2,1,0:T(8,128)S(1)}, f32[4,160,128]{2,1,0:T(8,128)S(1)}) custom-call(s32[8,128]{1,0:T(8,128)S(1)} %broadcast.2.refs_4_.refs_0_, f32[512,1024]{1,0:T(8,128)S(1)} %get-tuple-element.120.refs_1_, ...), custom_call_target="tpu_custom_call" | custom-call | flops 1000000000 | bytes 4000000 | tf_op jit(solution)/shard_map/forward_hidden/pallas_call | solution.py:66
  44.5 1.5 %collective-permute-done.15.refs_2_ = f32[4,160,128]{2,1,0:T(8,128)S(1)} collective-permute-done((f32[4,160,128]{2,1,0:T(8,128)S(1)}, f32[4,160,128]{2,1,0:T(8,128)S(1)}, u32[]{:S(2)}, u32[]{:S(2)}) %collective-permute-start.15) | collective-permute-done | bytes 327712 | tf_op jit(solution)/shard_map/ppermute | solution.py:51
  47.4 1.6 %collective-permute-start.17 = (f32[160,128]{1,0:T(8,128)S(1)}, f32[160,128]{1,0:T(8,128)S(1)}, u32[]{:S(2)}, u32[]{:S(2)}) collective-permute-start(f32[160,128]{1,0:T(8,128)S(1)} %get-tuple-element.132), channel_id=1, source_target_pairs={{0,4},{1,5},{2,6},{3,7},{4,0},{5,1},{6,2},{7,3},{8,12},{9,13},{10,... | collective-permute-start | bytes 245768 | tf_op jit(solution)/shard_map/ppermute | solution.py:51
  52.0 2.3 %collective-permute-done.18.refs_3_ = f32[160,128]{1,0:T(8,128)S(1)} collective-permute-done((f32[160,128]{1,0:T(8,128)S(1)}, f32[160,128]{1,0:T(8,128)S(1)}, u32[]{:S(2)}, u32[]{:S(2)}) %collective-permute-start.18) | collective-permute-done | bytes 81952 | tf_op jit(solution)/shard_map/ppermute | solution.py:51
  54.4 2.4 %collective-permute-start.19 = (f32[160,128]{1,0:T(8,128)S(1)}, f32[160,128]{1,0:T(8,128)S(1)}, u32[]{:S(2)}, u32[]{:S(2)}) collective-permute-start(f32[160,128]{1,0:T(8,128)S(1)} %fold_chips.1.refs_2_.refs_1_), channel_id=1, source_target_pairs={{0,8},{1,9},{2,10},{3,11},{4,12},{5,13},{6,14},{7,15},{8,0},{9,1},... | collective-permute-start | bytes 245768 | tf_op jit(solution)/shard_map/ppermute | solution.py:51
  57.5 3.2 %collective-permute-done.19.refs_2_ = f32[160,128]{1,0:T(8,128)S(1)} collective-permute-done((f32[160,128]{1,0:T(8,128)S(1)}, f32[160,128]{1,0:T(8,128)S(1)}, u32[]{:S(2)}, u32[]{:S(2)}) %collective-permute-start.19) | collective-permute-done | bytes 81952 | tf_op jit(solution)/shard_map/ppermute | solution.py:51
  61.6 1.7 %collective-permute-start.22 = (bf16[160,128]{1,0:T(8,128)(2,1)S(1)}, bf16[160,128]{1,0:T(8,128)(2,1)S(1)}, u32[]{:S(2)}, u32[]{:S(2)}) collective-permute-start(bf16[160,128]{1,0:T(8,128)(2,1)S(1)} %class_grad.1.refs_1_), channel_id=1, source_target_pairs={{0,4},{1,5},{2,6},{3,7},{4,0},{5,1},{6,2},{7,3},{8,12},{9,13},{10,... | collective-permute-start | bytes 122888 | tf_op jit(solution)/shard_map/ppermute | solution.py:51
  65.8 1.6 %collective-permute-done.21.refs_2_ = bf16[160,128]{1,0:T(8,128)(2,1)S(1)} collective-permute-done((bf16[160,128]{1,0:T(8,128)(2,1)S(1)}, bf16[160,128]{1,0:T(8,128)(2,1)S(1)}, u32[]{:S(2)}, u32[]{:S(2)}) %collective-permute-start.21) | collective-permute-done | bytes 40992 | tf_op jit(solution)/shard_map/ppermute | solution.py:51
  67.5 1.4 %collective-permute-done.24.refs_2_ = bf16[4,160,128]{2,1,0:T(8,128)(2,1)S(1)} collective-permute-done((bf16[4,160,128]{2,1,0:T(8,128)(2,1)S(1)}, bf16[4,160,128]{2,1,0:T(8,128)(2,1)S(1)}, u32[]{:S(2)}, u32[]{:S(2)}) %collective-permute-start.24) | collective-permute-done | bytes 163872 | tf_op jit(solution)/shard_map/ppermute | solution.py:51
  69.6 1.3 %class_products.1 = (bf16[512,160]{1,0:T(8,128)(2,1)S(1)}, bf16[176,1024]{1,0:T(8,128)(2,1)S(1)}, f32[16,1024]{1,0:T(8,128)S(1)}) custom-call(bf16[512,1024]{1,0:T(8,128)(2,1)S(1)} %get-tuple-element.137.refs_0_, bf16[160,1024]{1,0:T(8,128)(2,1)S(1)} %get-tuple-element.138.refs_1_.refs_2_, bf16[512,2048]{1,0:T(8,128)(2,1)S(1)} %get-tuple-element.139.refs_2_.refs_1_, ...), custom_call_target="tpu_custom_call" | custom-call | flops 800000000 | bytes 4000000 | tf_op jit(solution)/shard_map/class_products/pallas_call | solution.py:66
  73.5 1.7 %collective-permute-start.31 = (bf16[72,1024]{1,0:T(8,128)(2,1)S(1)}, bf16[72,1024]{1,0:T(8,128)(2,1)S(1)}, u32[]{:S(2)}, u32[]{:S(2)}) collective-permute-start(bf16[72,1024]{1,0:T(8,128)(2,1)S(1)} %get-tuple-element.151), channel_id=1, source_target_pairs={{0,2},{1,3},{4,0},{5,1},{8,4},{9,5},{12,8},{13,9},{14,12},{15,13},... | collective-permute-start | bytes 442376 | tf_op jit(solution)/shard_map/ppermute | solution.py:51
  75.9 3.5 %collective-permute-done.31.refs_1_ = bf16[72,1024]{1,0:T(8,128)(2,1)S(1)} collective-permute-done((bf16[72,1024]{1,0:T(8,128)(2,1)S(1)}, bf16[72,1024]{1,0:T(8,128)(2,1)S(1)}, u32[]{:S(2)}, u32[]{:S(2)}) %collective-permute-start.31) | collective-permute-done | bytes 147488 | tf_op jit(solution)/shard_map/ppermute | solution.py:51
  79.5 1.6 %collective-permute-start.32 = (bf16[152,1024]{1,0:T(8,128)(2,1)S(1)}, bf16[152,1024]{1,0:T(8,128)(2,1)S(1)}, u32[]{:S(2)}, u32[]{:S(2)}) collective-permute-start(bf16[152,1024]{1,0:T(8,128)(2,1)S(1)} %walk_sum.9), channel_id=1, source_target_pairs={{0,2},{1,3},{4,0},{5,1},{8,4},{9,5},{12,8},{13,9},{14,12},{15,13},... | collective-permute-start | bytes 933896 | tf_op jit(solution)/shard_map/ppermute | solution.py:51
  83.2 2.3 %d_w_out.1 = (f32[512,2048]{1,0:T(8,128)}, f32[8,128]{1,0:T(8,128)S(1)}) custom-call(bf16[512,160]{1,0:T(8,128)(2,1)S(1)} %get-tuple-element.140.refs_0_, bf16[160,2048]{1,0:T(8,128)(2,1)S(1)} %get-tuple-element.152.refs_1_, f32[1,2048]{1,0:T(1,128)S(1)} %bitcast.19, bf16[80,1024]{1,0:T(8,128)(2,1)S(1)} %collective-permute-done.27.refs_1_.refs_3_), custom_call_target="tpu_custom_call" | custom-call | flops 1000000000 | bytes 8000000 | tf_op jit(solution)/shard_map/d_w_out/pallas_call | solution.py:66
  85.6 2.7 %collective-permute-done.32.refs_1_ = bf16[152,1024]{1,0:T(8,128)(2,1)S(1)} collective-permute-done((bf16[152,1024]{1,0:T(8,128)(2,1)S(1)}, bf16[152,1024]{1,0:T(8,128)(2,1)S(1)}, u32[]{:S(2)}, u32[]{:S(2)}) %collective-permute-start.32) | collective-permute-done | bytes 311328 | tf_op jit(solution)/shard_map/ppermute | solution.py:51
  88.3 1.4 %collective-permute-start.33 = (bf16[152,1024]{1,0:T(8,128)(2,1)S(1)}, bf16[152,1024]{1,0:T(8,128)(2,1)S(1)}, u32[]{:S(2)}, u32[]{:S(2)}) collective-permute-start(bf16[152,1024]{1,0:T(8,128)(2,1)S(1)} %walk_sum.10.refs_7_), channel_id=1, source_target_pairs={{0,2},{1,3},{4,0},{5,1},{8,4},{9,5},{12,8},{13,9},{14,12},{15,13},... | collective-permute-start | bytes 933896 | tf_op jit(solution)/shard_map/ppermute | solution.py:51
  91.5 4.3 %d_w_in.1 = (f32[512,2048]{1,0:T(8,128)}, f32[8,128]{1,0:T(8,128)S(1)}) custom-call(s32[18]{0:T(128)S(1)} %dynamic-slice_bitcast_fusion.1.refs_0_, f32[1,2048]{1,0:T(1,128)S(1)} %bitcast.15, bf16[512,1024]{1,0:T(8,128)(2,1)S(1)} %get-tuple-element.136.refs_3_.refs_1_.refs_2_, f32[8,1024]{1,0:T(8,128)S(1)} %get-tuple-element.135.refs_1_.refs_3_.refs_4_, ...), custom_call_target="tpu_custom_call" | custom-call | flops 2000000000 | bytes 8000000 | tf_op jit(solution)/shard_map/d_w_in/pallas_call | solution.py:66
  102.8 2.1 %conv_backward_upper.1 = (f32[128,384]{1,0:T(8,128)S(1)}, f32[49,8,128]{2,1,0:T(8,128)S(1)}, f32[38,48,128]{2,1,0:T(8,128)S(1)}, f32[24,512]{1,0:T(8,128)S(1)}) custom-call(f32[152,1024]{1,0:T(8,128)S(1)} %messages.5.refs_0_, bf16[152,512]{1,0:T(8,128)(2,1)S(1)} %collective-permute-done.35.refs_1_, bf16[152,512]{1,0:T(8,128)(2,1)S(1)} %collective-permute-done.36.refs_2_, ...), custom_call_target="tpu_custom_call" | custom-call | flops 400000000 | bytes 2000000 | tf_op jit(solution)/shard_map/conv_backward_upper/pallas_call | solution.py:66
  104.9 3.9 %conv_backward_lower.1 = (f32[128,1024]{1,0:T(8,128)}, f32[49,128]{1,0:T(8,128)}, f32[1,128]{1,0:T(1,128)}, f32[150,128]{1,0:T(8,128)}) custom-call(f32[152,1024]{1,0:T(8,128)S(1)} %messages.5.refs_0_, bf16[152,512]{1,0:T(8,128)(2,1)S(1)} %collective-permute-done.30.refs_1_, bf16[152,512]{1,0:T(8,128)(2,1)S(1)} %collective-permute-done.34.refs_2_, ...), custom_call_target="tpu_custom_call" | custom-call | tf_op jit(solution)/shard_map/conv_backward_lower/pallas_call | solution.py:66
  (99 shorter events, 36.2 us)
Async XLA Ops:
  5.0 9.4 %collective-permute-start.1 = (bf16[128,1024]{1,0:T(8,128)(2,1)S(1)}, bf16[128,1024]{1,0:T(8,128)(2,1)S(1)}, u32[]{:S(2)}, u32[]{:S(2)}) collective-permute-start(bf16[128,1024]{1,0:T(8,128)(2,1)S(1)} %get-tuple-element.90.refs_3_.refs_2_.refs_0_), channel_id=1, source_target_pairs={{0,2},{1,3},{4,0},{5,1},{8,4},{9,5},{12,8},{13,9},{14,12},{15,13},... | collective-permute-start | bytes 786440 | tf_op jit(solution)/shard_map/ppermute | solution.py:51
  8.0 7.8 %collective-permute-start = (bf16[128,1024]{1,0:T(8,128)(2,1)S(1)}, bf16[128,1024]{1,0:T(8,128)(2,1)S(1)}, u32[]{:S(2)}, u32[]{:S(2)}) collective-permute-start(bf16[128,1024]{1,0:T(8,128)(2,1)S(1)} %get-tuple-element.90.refs_3_.refs_2_.refs_0_), channel_id=1, source_target_pairs={{0,4},{1,5},{4,8},{5,9},{8,12},{9,13},{12,14},{13,15},{14,10},{15,... | collective-permute-start | bytes 786440 | tf_op jit(solution)/shard_map/ppermute | solution.py:51
  15.8 2.7 %collective-permute-start.2 = (bf16[512,1024]{1,0:T(8,128)(2,1)S(1)}, bf16[512,1024]{1,0:T(8,128)(2,1)S(1)}, u32[]{:S(2)}, u32[]{:S(2)}) collective-permute-start(bf16[512,1024]{1,0:T(8,128)(2,1)S(1)} %get-tuple-element.95.refs_1_.refs_11_), channel_id=1, source_target_pairs={{0,1},{1,0},{2,3},{3,2},{4,5},{5,4},{6,7},{7,6},{8,9},{9,8},{10,11... | collective-permute-start | bytes 3145736 | tf_op jit(solution)/shard_map/ppermute | solution.py:51
  15.8 8.7 %collective-permute-start.3 = (bf16[128,1024]{1,0:T(8,128)(2,1)S(1)}, bf16[128,1024]{1,0:T(8,128)(2,1)S(1)}, u32[]{:S(2)}, u32[]{:S(2)}) collective-permute-start(bf16[128,1024]{1,0:T(8,128)(2,1)S(1)} %collective-permute-done.refs_4_.refs_8_), channel_id=1, source_target_pairs={{0,4},{1,5},{4,8},{5,9},{8,12},{9,13},{12,14},{13,15},{14,10},{15,... | collective-permute-start | bytes 786440 | tf_op jit(solution)/shard_map/ppermute | solution.py:51
  16.2 8.4 %collective-permute-start.4 = (bf16[128,1024]{1,0:T(8,128)(2,1)S(1)}, bf16[128,1024]{1,0:T(8,128)(2,1)S(1)}, u32[]{:S(2)}, u32[]{:S(2)}) collective-permute-start(bf16[128,1024]{1,0:T(8,128)(2,1)S(1)} %collective-permute-done.1.refs_3_.refs_1_), channel_id=1, source_target_pairs={{0,2},{1,3},{4,0},{5,1},{8,4},{9,5},{12,8},{13,9},{14,12},{15,13},... | collective-permute-start | bytes 786440 | tf_op jit(solution)/shard_map/ppermute | solution.py:51
  24.6 7.9 %collective-permute-start.5 = (bf16[128,1024]{1,0:T(8,128)(2,1)S(1)}, bf16[128,1024]{1,0:T(8,128)(2,1)S(1)}, u32[]{:S(2)}, u32[]{:S(2)}) collective-permute-start(bf16[128,1024]{1,0:T(8,128)(2,1)S(1)} %collective-permute-done.3.refs_6_.refs_7_), channel_id=1, source_target_pairs={{0,4},{1,5},{4,8},{5,9},{8,12},{9,13},{12,14},{13,15},{14,10},{15,... | collective-permute-start | bytes 786440 | tf_op jit(solution)/shard_map/ppermute | solution.py:51
  26.3 7.3 %collective-permute-start.6 = (bf16[128,1024]{1,0:T(8,128)(2,1)S(1)}, bf16[128,1024]{1,0:T(8,128)(2,1)S(1)}, u32[]{:S(2)}, u32[]{:S(2)}) collective-permute-start(bf16[128,1024]{1,0:T(8,128)(2,1)S(1)} %collective-permute-done.4.refs_5_.refs_2_), channel_id=1, source_target_pairs={{0,2},{1,3},{4,0},{5,1},{8,4},{9,5},{12,8},{13,9},{14,12},{15,13},... | collective-permute-start | bytes 786440 | tf_op jit(solution)/shard_map/ppermute | solution.py:51
  33.6 9.1 %collective-permute-start.10 = (bf16[512,1024]{1,0:T(8,128)(2,1)S(1)}, bf16[512,1024]{1,0:T(8,128)(2,1)S(1)}, u32[]{:S(2)}, u32[]{:S(2)}) collective-permute-start(bf16[512,1024]{1,0:T(8,128)(2,1)S(1)} %get-tuple-element.121), channel_id=1, source_target_pairs={{0,1},{1,0},{2,3},{3,2},{4,5},{5,4},{6,7},{7,6},{8,9},{9,8},{10,11... | collective-permute-start | bytes 3145736 | tf_op jit(solution)/shard_map/ppermute | solution.py:51
  33.6 6.5 %collective-permute-start.9 = (bf16[128,1024]{1,0:T(8,128)(2,1)S(1)}, bf16[128,1024]{1,0:T(8,128)(2,1)S(1)}, u32[]{:S(2)}, u32[]{:S(2)}) collective-permute-start(bf16[128,1024]{1,0:T(8,128)(2,1)S(1)} %collective-permute-done.5.refs_5_.refs_6_), channel_id=1, source_target_pairs={{0,1},{1,0},{2,3},{3,2},{4,5},{5,4},{6,7},{7,6},{8,9},{9,8},{10,11... | collective-permute-start | bytes 786440 | tf_op jit(solution)/shard_map/ppermute | solution.py:51
  34.1 6.0 %collective-permute-start.8 = (bf16[128,1024]{1,0:T(8,128)(2,1)S(1)}, bf16[128,1024]{1,0:T(8,128)(2,1)S(1)}, u32[]{:S(2)}, u32[]{:S(2)}) collective-permute-start(bf16[128,1024]{1,0:T(8,128)(2,1)S(1)} %collective-permute-done.6.refs_4_.refs_3_), channel_id=1, source_target_pairs={{0,1},{1,0},{2,3},{3,2},{4,5},{5,4},{6,7},{7,6},{8,9},{9,8},{10,11... | collective-permute-start | bytes 786440 | tf_op jit(solution)/shard_map/ppermute | solution.py:51
  34.2 6.0 %collective-permute-start.12 = (bf16[64,1024]{1,0:T(8,128)(2,1)S(1)}, bf16[64,1024]{1,0:T(8,128)(2,1)S(1)}, u32[]{:S(2)}, u32[]{:S(2)}) collective-permute-start(bf16[64,1024]{1,0:T(8,128)(2,1)S(1)} %slice.7), channel_id=1, source_target_pairs={{0,2},{1,3},{4,0},{5,1},{8,4},{9,5},{12,8},{13,9},{14,12},{15,13},... | collective-permute-start | bytes 393224 | tf_op jit(solution)/shard_map/ppermute | solution.py:51
  34.8 6.1 %collective-permute-start.7 = (bf16[64,1024]{1,0:T(8,128)(2,1)S(1)}, bf16[64,1024]{1,0:T(8,128)(2,1)S(1)}, u32[]{:S(2)}, u32[]{:S(2)}) collective-permute-start(bf16[64,1024]{1,0:T(8,128)(2,1)S(1)} %slice.6), channel_id=1, source_target_pairs={{0,4},{1,5},{4,8},{5,9},{8,12},{9,13},{12,14},{13,15},{14,10},{15,... | collective-permute-start | bytes 393224 | tf_op jit(solution)/shard_map/ppermute | solution.py:51
  40.1 2.6 %collective-permute-start.14 = (bf16[64,1024]{1,0:T(8,128)(2,1)S(1)}, bf16[64,1024]{1,0:T(8,128)(2,1)S(1)}, u32[]{:S(2)}, u32[]{:S(2)}) collective-permute-start(bf16[64,1024]{1,0:T(8,128)(2,1)S(1)} %collective-permute-done.12.refs_13_.refs_5_), channel_id=1, source_target_pairs={{0,1},{1,0},{2,3},{3,2},{4,5},{5,4},{6,7},{7,6},{8,9},{9,8},{10,11... | collective-permute-start | bytes 393224 | tf_op jit(solution)/shard_map/ppermute | solution.py:51
  46.1 14.6 %collective-permute-start.20 = (bf16[1024,1024]{1,0:T(8,128)(2,1)S(1)}, bf16[1024,1024]{1,0:T(8,128)(2,1)S(1)}, u32[]{:S(2)}, u32[]{:S(2)}) collective-permute-start(bf16[1024,1024]{1,0:T(8,128)(2,1)S(1)} %pack_blocks.1.refs_2_.refs_4_), channel_id=1, source_target_pairs={{0,1},{1,0},{2,3},{3,2},{4,5},{5,4},{6,7},{7,6},{8,9},{9,8},{10,11... | collective-permute-start | bytes 6291464 | tf_op jit(solution)/shard_map/ppermute | solution.py:51
  46.4 4.7 %collective-permute-start.16 = (f32[160,128]{1,0:T(8,128)S(1)}, f32[160,128]{1,0:T(8,128)S(1)}, u32[]{:S(2)}, u32[]{:S(2)}) collective-permute-start(f32[160,128]{1,0:T(8,128)S(1)} %get-tuple-element.131), channel_id=1, source_target_pairs={{0,2},{1,3},{2,0},{3,1},{4,6},{5,7},{6,4},{7,5},{8,10},{9,11},{10,... | collective-permute-start | bytes 245768 | tf_op jit(solution)/shard_map/ppermute | solution.py:51
  47.4 4.6 %collective-permute-start.17 = (f32[160,128]{1,0:T(8,128)S(1)}, f32[160,128]{1,0:T(8,128)S(1)}, u32[]{:S(2)}, u32[]{:S(2)}) collective-permute-start(f32[160,128]{1,0:T(8,128)S(1)} %get-tuple-element.132), channel_id=1, source_target_pairs={{0,4},{1,5},{2,6},{3,7},{4,0},{5,1},{6,2},{7,3},{8,12},{9,13},{10,... | collective-permute-start | bytes 245768 | tf_op jit(solution)/shard_map/ppermute | solution.py:51
  49.0 5.3 %collective-permute-start.18 = (f32[160,128]{1,0:T(8,128)S(1)}, f32[160,128]{1,0:T(8,128)S(1)}, u32[]{:S(2)}, u32[]{:S(2)}) collective-permute-start(f32[160,128]{1,0:T(8,128)S(1)} %get-tuple-element.133), channel_id=1, source_target_pairs={{0,6},{1,7},{2,4},{3,5},{4,2},{5,3},{6,0},{7,1},{8,14},{9,15},{10,... | collective-permute-start | bytes 245768 | tf_op jit(solution)/shard_map/ppermute | solution.py:51
  54.4 6.3 %collective-permute-start.19 = (f32[160,128]{1,0:T(8,128)S(1)}, f32[160,128]{1,0:T(8,128)S(1)}, u32[]{:S(2)}, u32[]{:S(2)}) collective-permute-start(f32[160,128]{1,0:T(8,128)S(1)} %fold_chips.1.refs_2_.refs_1_), channel_id=1, source_target_pairs={{0,8},{1,9},{2,10},{3,11},{4,12},{5,13},{6,14},{7,15},{8,0},{9,1},... | collective-permute-start | bytes 245768 | tf_op jit(solution)/shard_map/ppermute | solution.py:51
  60.8 5.0 %collective-permute-start.23 = (bf16[160,128]{1,0:T(8,128)(2,1)S(1)}, bf16[160,128]{1,0:T(8,128)(2,1)S(1)}, u32[]{:S(2)}, u32[]{:S(2)}) collective-permute-start(bf16[160,128]{1,0:T(8,128)(2,1)S(1)} %class_grad.1.refs_1_), channel_id=1, source_target_pairs={{0,6},{1,7},{2,4},{3,5},{4,2},{5,3},{6,0},{7,1},{8,14},{9,15},{10,... | collective-permute-start | bytes 122888 | tf_op jit(solution)/shard_map/ppermute | solution.py:51
  61.6 4.1 %collective-permute-start.22 = (bf16[160,128]{1,0:T(8,128)(2,1)S(1)}, bf16[160,128]{1,0:T(8,128)(2,1)S(1)}, u32[]{:S(2)}, u32[]{:S(2)}) collective-permute-start(bf16[160,128]{1,0:T(8,128)(2,1)S(1)} %class_grad.1.refs_1_), channel_id=1, source_target_pairs={{0,4},{1,5},{2,6},{3,7},{4,0},{5,1},{6,2},{7,3},{8,12},{9,13},{10,... | collective-permute-start | bytes 122888 | tf_op jit(solution)/shard_map/ppermute | solution.py:51
  63.3 4.0 %collective-permute-start.21 = (bf16[160,128]{1,0:T(8,128)(2,1)S(1)}, bf16[160,128]{1,0:T(8,128)(2,1)S(1)}, u32[]{:S(2)}, u32[]{:S(2)}) collective-permute-start(bf16[160,128]{1,0:T(8,128)(2,1)S(1)} %class_grad.1.refs_1_), channel_id=1, source_target_pairs={{0,2},{1,3},{2,0},{3,1},{4,6},{5,7},{6,4},{7,5},{8,10},{9,11},{10,... | collective-permute-start | bytes 122888 | tf_op jit(solution)/shard_map/ppermute | solution.py:51
  69.4 3.2 %collective-permute-start.25 = (bf16[512,1024]{1,0:T(8,128)(2,1)S(1)}, bf16[512,1024]{1,0:T(8,128)(2,1)S(1)}, u32[]{:S(2)}, u32[]{:S(2)}) collective-permute-start(bf16[512,1024]{1,0:T(8,128)(2,1)S(1)} %get-tuple-element.136.refs_3_.refs_1_.refs_2_), channel_id=1, source_target_pairs={{0,1},{1,0},{2,3},{3,2},{4,5},{5,4},{6,7},{7,6},{8,9},{9,8},{10,11... | collective-permute-start | bytes 3145736 | tf_op jit(solution)/shard_map/ppermute | solution.py:51
  73.1 8.0 %collective-permute-start.27 = (bf16[80,1024]{1,0:T(8,128)(2,1)S(1)}, bf16[80,1024]{1,0:T(8,128)(2,1)S(1)}, u32[]{:S(2)}, u32[]{:S(2)}) collective-permute-start(bf16[80,1024]{1,0:T(8,128)(2,1)S(1)} %get-tuple-element.146), channel_id=1, source_target_pairs={{0,4},{1,5},{4,8},{5,9},{8,12},{9,13},{12,14},{13,15},{14,10},{15,... | collective-permute-start | bytes 491528 | tf_op jit(solution)/shard_map/ppermute | solution.py:51
  73.5 6.0 %collective-permute-start.31 = (bf16[72,1024]{1,0:T(8,128)(2,1)S(1)}, bf16[72,1024]{1,0:T(8,128)(2,1)S(1)}, u32[]{:S(2)}, u32[]{:S(2)}) collective-permute-start(bf16[72,1024]{1,0:T(8,128)(2,1)S(1)} %get-tuple-element.151), channel_id=1, source_target_pairs={{0,2},{1,3},{4,0},{5,1},{8,4},{9,5},{12,8},{13,9},{14,12},{15,13},... | collective-permute-start | bytes 442376 | tf_op jit(solution)/shard_map/ppermute | solution.py:51
  79.5 8.8 %collective-permute-start.32 = (bf16[152,1024]{1,0:T(8,128)(2,1)S(1)}, bf16[152,1024]{1,0:T(8,128)(2,1)S(1)}, u32[]{:S(2)}, u32[]{:S(2)}) collective-permute-start(bf16[152,1024]{1,0:T(8,128)(2,1)S(1)} %walk_sum.9), channel_id=1, source_target_pairs={{0,2},{1,3},{4,0},{5,1},{8,4},{9,5},{12,8},{13,9},{14,12},{15,13},... | collective-permute-start | bytes 933896 | tf_op jit(solution)/shard_map/ppermute | solution.py:51
  81.2 8.5 %collective-permute-start.28 = (bf16[152,1024]{1,0:T(8,128)(2,1)S(1)}, bf16[152,1024]{1,0:T(8,128)(2,1)S(1)}, u32[]{:S(2)}, u32[]{:S(2)}) collective-permute-start(bf16[152,1024]{1,0:T(8,128)(2,1)S(1)} %walk_sum.6), channel_id=1, source_target_pairs={{0,4},{1,5},{4,8},{5,9},{8,12},{9,13},{12,14},{13,15},{14,10},{15,... | collective-permute-start | bytes 933896 | tf_op jit(solution)/shard_map/ppermute | solution.py:51
  88.3 7.8 %collective-permute-start.33 = (bf16[152,1024]{1,0:T(8,128)(2,1)S(1)}, bf16[152,1024]{1,0:T(8,128)(2,1)S(1)}, u32[]{:S(2)}, u32[]{:S(2)}) collective-permute-start(bf16[152,1024]{1,0:T(8,128)(2,1)S(1)} %walk_sum.10.refs_7_), channel_id=1, source_target_pairs={{0,2},{1,3},{4,0},{5,1},{8,4},{9,5},{12,8},{13,9},{14,12},{15,13},... | collective-permute-start | bytes 933896 | tf_op jit(solution)/shard_map/ppermute | solution.py:51
  89.8 7.6 %collective-permute-start.29 = (bf16[152,1024]{1,0:T(8,128)(2,1)S(1)}, bf16[152,1024]{1,0:T(8,128)(2,1)S(1)}, u32[]{:S(2)}, u32[]{:S(2)}) collective-permute-start(bf16[152,1024]{1,0:T(8,128)(2,1)S(1)} %walk_sum.7.refs_6_), channel_id=1, source_target_pairs={{0,4},{1,5},{4,8},{5,9},{8,12},{9,13},{12,14},{13,15},{14,10},{15,... | collective-permute-start | bytes 933896 | tf_op jit(solution)/shard_map/ppermute | solution.py:51
  96.2 5.3 %collective-permute-start.36 = (bf16[152,512]{1,0:T(8,128)(2,1)S(1)}, bf16[152,512]{1,0:T(8,128)(2,1)S(1)}, u32[]{:S(2)}, u32[]{:S(2)}) collective-permute-start(bf16[152,512]{1,0:T(8,128)(2,1)S(1)} %get-tuple-element.161), channel_id=1, source_target_pairs={{0,2},{1,3},{4,0},{5,1},{8,4},{9,5},{12,8},{13,9},{14,12},{15,13},... | collective-permute-start | bytes 466952 | tf_op jit(solution)/shard_map/ppermute | solution.py:51
  97.5 5.3 %collective-permute-start.35 = (bf16[152,512]{1,0:T(8,128)(2,1)S(1)}, bf16[152,512]{1,0:T(8,128)(2,1)S(1)}, u32[]{:S(2)}, u32[]{:S(2)}) collective-permute-start(bf16[152,512]{1,0:T(8,128)(2,1)S(1)} %get-tuple-element.160), channel_id=1, source_target_pairs={{0,4},{1,5},{4,8},{5,9},{8,12},{9,13},{12,14},{13,15},{14,10},{15,... | collective-permute-start | bytes 466952 | tf_op jit(solution)/shard_map/ppermute | solution.py:51
  98.4 6.4 %collective-permute-start.34 = (bf16[152,512]{1,0:T(8,128)(2,1)S(1)}, bf16[152,512]{1,0:T(8,128)(2,1)S(1)}, u32[]{:S(2)}, u32[]{:S(2)}) collective-permute-start(bf16[152,512]{1,0:T(8,128)(2,1)S(1)} %get-tuple-element.156), channel_id=1, source_target_pairs={{0,2},{1,3},{4,0},{5,1},{8,4},{9,5},{12,8},{13,9},{14,12},{15,13},... | collective-permute-start | bytes 466952 | tf_op jit(solution)/shard_map/ppermute | solution.py:51
  99.6 5.3 %collective-permute-start.30 = (bf16[152,512]{1,0:T(8,128)(2,1)S(1)}, bf16[152,512]{1,0:T(8,128)(2,1)S(1)}, u32[]{:S(2)}, u32[]{:S(2)}) collective-permute-start(bf16[152,512]{1,0:T(8,128)(2,1)S(1)} %get-tuple-element.147), channel_id=1, source_target_pairs={{0,4},{1,5},{4,8},{5,9},{8,12},{9,13},{12,14},{13,15},{14,10},{15,... | collective-permute-start | bytes 466952 | tf_op jit(solution)/shard_map/ppermute | solution.py:51
  (14 other events, 28.4 us)

commit v5 on v4

--- a/solution.py
+++ b/solution.py
@@ -93,29 +93,25 @@
     grid_pad[pl.ds(row + HALF, 4), pl.ds(8, WIN_W), :] = tile.T.reshape(4, WIN_W, tile.shape[0])
 
 
-def conv_rows(copies, taps, row, flip):
+def conv_rows(copies, taps, row, flip, count=4):
     acc = None
     for j in range(KS):
         for i in range(KS):
             index = (KS - 1 - i) * KS + KS - 1 - j if flip else i * KS + j
-            term = taps[index : index + 1, :][None] * copies[j, pl.ds(row + i, 4)]
+            term = taps[index : index + 1, :][None] * copies[j, pl.ds(row + i, count)]
             acc = term if acc is None else acc + term
     return acc
 
 
-def conv_kernel(x_hbm, taps_hbm, out_ref, x_ref, taps, grid_pad, copies, sems):
-    fetches = [pltpu.make_async_copy(x_hbm, x_ref, sems.at[0]), pltpu.make_async_copy(taps_hbm, taps, sems.at[1])]
-    for fetch in fetches:
-        fetch.start()
+def conv_kernel(x_ref, taps, out_ref, grid_pad, copies):
     clear_border(grid_pad)
-    for fetch in fetches:
-        fetch.wait()
     for g in range(8):
         put_rows(grid_pad, 4 * g, x_ref[:, g * LANE : (g + 1) * LANE].astype(F32))
     shifted_copies(grid_pad, copies)
-    for g in range(8):
-        acc = conv_rows(copies, taps, 4 * g, False)
-        out_ref[:, g * LANE : (g + 1) * LANE] = acc.reshape(LANE, LANE).T.astype(BF)
+    for g in range(0, 8, 2):
+        acc = conv_rows(copies, taps, 4 * g, False, 8).reshape(2 * LANE, LANE)
+        for k in range(2):
+            out_ref[:, (g + k) * LANE : (g + k + 1) * LANE] = acc[k * LANE : (k + 1) * LANE].T.astype(BF)
 
 
 def copies_kernel(x_ref, copies, grid_pad):
@@ -483,9 +479,8 @@
     spot, mark = [(places, SMEM)], vm(marks)
     f32s, bf16s, sums_size = ((units, tokens), F32), ((units, tokens), BF), ((8, tokens), F32)
 
-    conv_out, features, taps = call(
-        conv_kernel, [((rows, tokens), BF), ((rows, tokens), BF), ((KS * KS, rows), F32)], [(features, HBM), (taps, HBM)],
-        [grid_shape, pltpu.VMEM(copies_size, F32), pltpu.SemaphoreType.DMA((2,))],
+    (conv_out,) = call(
+        conv_kernel, [((rows, tokens), BF)], vm(features, taps), [grid_shape, pltpu.VMEM(copies_size, F32)],
         limit=12, name="conv_forward",
     )
     walk = {0: (conv_out,)}

time: 109 us -> 109 us (level)
    unnamed x18 -> x22, local copies, waits for them, and re-layouts: 4 us -> 4.01 us
  transfers between devices with their start and end apart: 37 -> 37, of which waited for: 23 -> 23; matrix products, arithmetic and copies ran while one was open for 1% -> 1% of each run, Pallas kernels for 20% -> 21%
where the time goes in v5:
time: 109 us
  waiting for transfers between devices  38.7 us (36%)
  starting transfers between devices  32.1 us (29%)
  Pallas kernels  31.5 us (29%)
  local copies, waits for them, and re-layouts  5.49 us (5%)
    ppermute x37, waiting for transfers between devices, send(): return lax.ppermute(value, 'ch', perm)  38.7 us
    ppermute x37, starting transfers between devices, send(): return lax.ppermute(value, 'ch', perm)  32.1 us
    pallas_call x34, Pallas kernels, call(): pl.pallas_call(body, out_shape=[jax.ShapeDtypeStruct(s, d) for s, d in ou...  31.5 us
    unnamed x22, local copies, waits for them, and re-layouts  4.01 us
  transfers between devices with their start and end apart: 37, of which 23 were waited for; matrix products, arithmetic and copies ran while one was open for 1% of the time, Pallas kernels for 21%

profile of v5, /device:TPU:0, one launch (start us, length us, event | category | flops | bytes accessed | tf_op | source)
XLA Modules:
  0.0 108.7 jit_solution(16397373550450692369)
XLA Ops:
  2.3 2.3 %conv_forward.1.refs_3_.refs_2_.refs_0_ = bf16[128,1024]{1,0:T(8,128)(2,1)S(1)} custom-call(bf16[128,1024]{1,0:T(8,128)(2,1)S(1)} %copy-done, f32[49,128]{1,0:T(8,128)S(1)} %bitcast.13), custom_call_target="tpu_custom_call" | custom-call | tf_op jit(solution)/shard_map/conv_forward/pallas_call | solution.py:66
  4.6 3.0 %collective-permute-start.1 = (bf16[128,1024]{1,0:T(8,128)(2,1)S(1)}, bf16[128,1024]{1,0:T(8,128)(2,1)S(1)}, u32[]{:S(2)}, u32[]{:S(2)}) collective-permute-start(bf16[128,1024]{1,0:T(8,128)(2,1)S(1)} %conv_forward.1.refs_3_.refs_2_.refs_0_), channel_id=1, source_target_pairs={{0,2},{1,3},{4,0},{5,1},{8,4},{9,5},{12,8},{13,9},{14,12},{15,13},... | collective-permute-start | bytes 786440 | tf_op jit(solution)/shard_map/ppermute | solution.py:51
  9.2 1.6 %copy-done.2 = bf16[512,2048]{1,0:T(8,128)(2,1)S(1)} copy-done((bf16[512,2048]{1,0:T(8,128)(2,1)S(1)}, bf16[512,2048]{1,0:T(8,128)(2,1)}, u32[]{:S(2)}) %copy-start.2) | copy-done | bytes 2097176
  11.5 1.4 %weights_ready.1 = (bf16[512,1024]{1,0:T(8,128)(2,1)S(1)}, bf16[512,1024]{1,0:T(8,128)(2,1)S(1)}, f32[512,1]{1,0:T(8,128)S(1)}) custom-call(s32[18]{0:T(128)S(1)} %dynamic-slice_bitcast_fusion.1.refs_0_, bf16[512,2048]{1,0:T(8,128)(2,1)S(1)} %copy-done.2, f32[1,2048]{1,0:T(1,128)S(1)} %bitcast.16, bf16[128,1024]{1,0:T(8,128)(2,1)S(1)} %conv_forward.1.refs_3_.refs_2_.refs_0_, ...), custom_call_target="tpu_custom_call" | custom-call | flops 400000000 | bytes 4000000 | tf_op jit(solution)/shard_map/weights_ready/pallas_call | solution.py:66
  14.0 1.4 %collective-permute-done.refs_4_.refs_8_ = bf16[128,1024]{1,0:T(8,128)(2,1)S(1)} collective-permute-done((bf16[128,1024]{1,0:T(8,128)(2,1)S(1)}, bf16[128,1024]{1,0:T(8,128)(2,1)S(1)}, u32[]{:S(2)}, u32[]{:S(2)}) %collective-permute-start) | collective-permute-done | bytes 262176 | tf_op jit(solution)/shard_map/ppermute | solution.py:51
  15.8 1.6 %collective-permute-start.4 = (bf16[128,1024]{1,0:T(8,128)(2,1)S(1)}, bf16[128,1024]{1,0:T(8,128)(2,1)S(1)}, u32[]{:S(2)}, u32[]{:S(2)}) collective-permute-start(bf16[128,1024]{1,0:T(8,128)(2,1)S(1)} %collective-permute-done.1.refs_3_.refs_1_), channel_id=1, source_target_pairs={{0,2},{1,3},{4,0},{5,1},{8,4},{9,5},{12,8},{13,9},{14,12},{15,13},... | collective-permute-start | bytes 786440 | tf_op jit(solution)/shard_map/ppermute | solution.py:51
  18.1 1.4 %forward_first.1 = (f32[512,1024]{1,0:T(8,128)S(1)}, f32[512,1024]{1,0:T(8,128)S(1)}, f32[8,1024]{1,0:T(8,128)S(1)}) custom-call(bf16[512,1024]{1,0:T(8,128)(2,1)S(1)} %get-tuple-element.90.refs_0_.refs_10_, bf16[512,1024]{1,0:T(8,128)(2,1)S(1)} %collective-permute-done.2.refs_1_, bf16[128,1024]{1,0:T(8,128)(2,1)S(1)} %conv_forward.1.refs_3_.refs_2_.refs_0_, ...), custom_call_target="tpu_custom_call" | custom-call | flops 1000000000 | bytes 4000000 | tf_op jit(solution)/shard_map/forward_first/pallas_call | solution.py:66
  19.5 4.7 %collective-permute-done.3.refs_6_.refs_7_ = bf16[128,1024]{1,0:T(8,128)(2,1)S(1)} collective-permute-done((bf16[128,1024]{1,0:T(8,128)(2,1)S(1)}, bf16[128,1024]{1,0:T(8,128)(2,1)S(1)}, u32[]{:S(2)}, u32[]{:S(2)}) %collective-permute-start.3) | collective-permute-done | bytes 262176 | tf_op jit(solution)/shard_map/ppermute | solution.py:51
  24.3 1.7 %collective-permute-start.5 = (bf16[128,1024]{1,0:T(8,128)(2,1)S(1)}, bf16[128,1024]{1,0:T(8,128)(2,1)S(1)}, u32[]{:S(2)}, u32[]{:S(2)}) collective-permute-start(bf16[128,1024]{1,0:T(8,128)(2,1)S(1)} %collective-permute-done.3.refs_6_.refs_7_), channel_id=1, source_target_pairs={{0,4},{1,5},{4,8},{5,9},{8,12},{9,13},{12,14},{13,15},{14,10},{15,... | collective-permute-start | bytes 786440 | tf_op jit(solution)/shard_map/ppermute | solution.py:51
  27.1 1.9 %mix_ready.1 = (bf16[160,2048]{1,0:T(8,128)(2,1)S(1)}, bf16[512,160]{1,0:T(8,128)(2,1)S(1)}, bf16[512,2048]{1,0:T(8,128)(2,1)S(1)}, bf16[160,128]{1,0:T(8,128)(2,1)S(1)}, f32[1,128]{1,0:T(1,128)S(1)}) custom-call(s32[18]{0:T(128)S(1)} %dynamic-slice_bitcast_fusion.1.refs_0_, bf16[512,2048]{1,0:T(8,128)(2,1)S(1)} %copy-done.8, f32[1,2048]{1,0:T(1,128)S(1)} %bitcast.20, ...), custom_call_target="tpu_custom_call" | custom-call | flops 1000000000 | bytes 4000000 | tf_op jit(solution)/shard_map/mix_ready/pallas_call | solution.py:66
  29.0 3.2 %collective-permute-done.5.refs_5_.refs_6_ = bf16[128,1024]{1,0:T(8,128)(2,1)S(1)} collective-permute-done((bf16[128,1024]{1,0:T(8,128)(2,1)S(1)}, bf16[128,1024]{1,0:T(8,128)(2,1)S(1)}, u32[]{:S(2)}, u32[]{:S(2)}) %collective-permute-start.5) | collective-permute-done | bytes 262176 | tf_op jit(solution)/shard_map/ppermute | solution.py:51
  34.5 1.7 %collective-permute-start.7 = (bf16[64,1024]{1,0:T(8,128)(2,1)S(1)}, bf16[64,1024]{1,0:T(8,128)(2,1)S(1)}, u32[]{:S(2)}, u32[]{:S(2)}) collective-permute-start(bf16[64,1024]{1,0:T(8,128)(2,1)S(1)} %slice.6), channel_id=1, source_target_pairs={{0,4},{1,5},{4,8},{5,9},{8,12},{9,13},{12,14},{13,15},{14,10},{15,... | collective-permute-start | bytes 393224 | tf_op jit(solution)/shard_map/ppermute | solution.py:51
  36.2 3.6 %collective-permute-done.12.refs_13_.refs_5_ = bf16[64,1024]{1,0:T(8,128)(2,1)S(1)} collective-permute-done((bf16[64,1024]{1,0:T(8,128)(2,1)S(1)}, bf16[64,1024]{1,0:T(8,128)(2,1)S(1)}, u32[]{:S(2)}, u32[]{:S(2)}) %collective-permute-start.12) | collective-permute-done | bytes 131104 | tf_op jit(solution)/shard_map/ppermute | solution.py:51
  42.4 1.5 %forward_hidden.1 = (f32[512,1024]{1,0:T(8,128)S(1)}, bf16[512,1024]{1,0:T(8,128)(2,1)S(1)}, f32[8,1024]{1,0:T(8,128)S(1)}, f32[4,160,128]{2,1,0:T(8,128)S(1)}, f32[4,160,128]{2,1,0:T(8,128)S(1)}) custom-call(s32[8,128]{1,0:T(8,128)S(1)} %broadcast.2.refs_4_.refs_0_, f32[512,1024]{1,0:T(8,128)S(1)} %get-tuple-element.116.refs_1_, ...), custom_call_target="tpu_custom_call" | custom-call | flops 1000000000 | bytes 4000000 | tf_op jit(solution)/shard_map/forward_hidden/pallas_call | solution.py:66
  44.1 1.4 %collective-permute-done.15.refs_2_ = f32[4,160,128]{2,1,0:T(8,128)S(1)} collective-permute-done((f32[4,160,128]{2,1,0:T(8,128)S(1)}, f32[4,160,128]{2,1,0:T(8,128)S(1)}, u32[]{:S(2)}, u32[]{:S(2)}) %collective-permute-start.15) | collective-permute-done | bytes 327712 | tf_op jit(solution)/shard_map/ppermute | solution.py:51
  47.1 1.6 %collective-permute-start.17 = (f32[160,128]{1,0:T(8,128)S(1)}, f32[160,128]{1,0:T(8,128)S(1)}, u32[]{:S(2)}, u32[]{:S(2)}) collective-permute-start(f32[160,128]{1,0:T(8,128)S(1)} %get-tuple-element.127), channel_id=1, source_target_pairs={{0,4},{1,5},{2,6},{3,7},{4,0},{5,1},{6,2},{7,3},{8,12},{9,13},{10,... | collective-permute-start | bytes 245768 | tf_op jit(solution)/shard_map/ppermute | solution.py:51
  51.8 2.3 %collective-permute-done.18.refs_3_ = f32[160,128]{1,0:T(8,128)S(1)} collective-permute-done((f32[160,128]{1,0:T(8,128)S(1)}, f32[160,128]{1,0:T(8,128)S(1)}, u32[]{:S(2)}, u32[]{:S(2)}) %collective-permute-start.18) | collective-permute-done | bytes 81952 | tf_op jit(solution)/shard_map/ppermute | solution.py:51
  54.1 2.4 %collective-permute-start.19 = (f32[160,128]{1,0:T(8,128)S(1)}, f32[160,128]{1,0:T(8,128)S(1)}, u32[]{:S(2)}, u32[]{:S(2)}) collective-permute-start(f32[160,128]{1,0:T(8,128)S(1)} %fold_chips.1.refs_2_.refs_1_), channel_id=1, source_target_pairs={{0,8},{1,9},{2,10},{3,11},{4,12},{5,13},{6,14},{7,15},{8,0},{9,1},... | collective-permute-start | bytes 245768 | tf_op jit(solution)/shard_map/ppermute | solution.py:51
  57.2 3.2 %collective-permute-done.19.refs_2_ = f32[160,128]{1,0:T(8,128)S(1)} collective-permute-done((f32[160,128]{1,0:T(8,128)S(1)}, f32[160,128]{1,0:T(8,128)S(1)}, u32[]{:S(2)}, u32[]{:S(2)}) %collective-permute-start.19) | collective-permute-done | bytes 81952 | tf_op jit(solution)/shard_map/ppermute | solution.py:51
  61.3 1.7 %collective-permute-start.22 = (bf16[160,128]{1,0:T(8,128)(2,1)S(1)}, bf16[160,128]{1,0:T(8,128)(2,1)S(1)}, u32[]{:S(2)}, u32[]{:S(2)}) collective-permute-start(bf16[160,128]{1,0:T(8,128)(2,1)S(1)} %class_grad.1.refs_1_), channel_id=1, source_target_pairs={{0,4},{1,5},{2,6},{3,7},{4,0},{5,1},{6,2},{7,3},{8,12},{9,13},{10,... | collective-permute-start | bytes 122888 | tf_op jit(solution)/shard_map/ppermute | solution.py:51
  65.4 1.6 %collective-permute-done.21.refs_2_ = bf16[160,128]{1,0:T(8,128)(2,1)S(1)} collective-permute-done((bf16[160,128]{1,0:T(8,128)(2,1)S(1)}, bf16[160,128]{1,0:T(8,128)(2,1)S(1)}, u32[]{:S(2)}, u32[]{:S(2)}) %collective-permute-start.21) | collective-permute-done | bytes 40992 | tf_op jit(solution)/shard_map/ppermute | solution.py:51
  67.1 1.4 %collective-permute-done.24.refs_2_ = bf16[4,160,128]{2,1,0:T(8,128)(2,1)S(1)} collective-permute-done((bf16[4,160,128]{2,1,0:T(8,128)(2,1)S(1)}, bf16[4,160,128]{2,1,0:T(8,128)(2,1)S(1)}, u32[]{:S(2)}, u32[]{:S(2)}) %collective-permute-start.24) | collective-permute-done | bytes 163872 | tf_op jit(solution)/shard_map/ppermute | solution.py:51
  73.2 1.7 %collective-permute-start.31 = (bf16[72,1024]{1,0:T(8,128)(2,1)S(1)}, bf16[72,1024]{1,0:T(8,128)(2,1)S(1)}, u32[]{:S(2)}, u32[]{:S(2)}) collective-permute-start(bf16[72,1024]{1,0:T(8,128)(2,1)S(1)} %get-tuple-element.146), channel_id=1, source_target_pairs={{0,2},{1,3},{4,0},{5,1},{8,4},{9,5},{12,8},{13,9},{14,12},{15,13},... | collective-permute-start | bytes 442376 | tf_op jit(solution)/shard_map/ppermute | solution.py:51
  75.6 3.5 %collective-permute-done.31.refs_1_ = bf16[72,1024]{1,0:T(8,128)(2,1)S(1)} collective-permute-done((bf16[72,1024]{1,0:T(8,128)(2,1)S(1)}, bf16[72,1024]{1,0:T(8,128)(2,1)S(1)}, u32[]{:S(2)}, u32[]{:S(2)}) %collective-permute-start.31) | collective-permute-done | bytes 147488 | tf_op jit(solution)/shard_map/ppermute | solution.py:51
  79.2 1.6 %collective-permute-start.32 = (bf16[152,1024]{1,0:T(8,128)(2,1)S(1)}, bf16[152,1024]{1,0:T(8,128)(2,1)S(1)}, u32[]{:S(2)}, u32[]{:S(2)}) collective-permute-start(bf16[152,1024]{1,0:T(8,128)(2,1)S(1)} %walk_sum.9), channel_id=1, source_target_pairs={{0,2},{1,3},{4,0},{5,1},{8,4},{9,5},{12,8},{13,9},{14,12},{15,13},... | collective-permute-start | bytes 933896 | tf_op jit(solution)/shard_map/ppermute | solution.py:51
  82.9 2.3 %d_w_out.1 = (f32[512,2048]{1,0:T(8,128)}, f32[8,128]{1,0:T(8,128)S(1)}) custom-call(bf16[512,160]{1,0:T(8,128)(2,1)S(1)} %get-tuple-element.135.refs_0_, bf16[160,2048]{1,0:T(8,128)(2,1)S(1)} %get-tuple-element.147.refs_1_, f32[1,2048]{1,0:T(1,128)S(1)} %bitcast.21, bf16[80,1024]{1,0:T(8,128)(2,1)S(1)} %collective-permute-done.27.refs_1_.refs_3_), custom_call_target="tpu_custom_call" | custom-call | flops 1000000000 | bytes 8000000 | tf_op jit(solution)/shard_map/d_w_out/pallas_call | solution.py:66
  85.2 2.7 %collective-permute-done.32.refs_1_ = bf16[152,1024]{1,0:T(8,128)(2,1)S(1)} collective-permute-done((bf16[152,1024]{1,0:T(8,128)(2,1)S(1)}, bf16[152,1024]{1,0:T(8,128)(2,1)S(1)}, u32[]{:S(2)}, u32[]{:S(2)}) %collective-permute-start.32) | collective-permute-done | bytes 311328 | tf_op jit(solution)/shard_map/ppermute | solution.py:51
  88.0 1.4 %collective-permute-start.33 = (bf16[152,1024]{1,0:T(8,128)(2,1)S(1)}, bf16[152,1024]{1,0:T(8,128)(2,1)S(1)}, u32[]{:S(2)}, u32[]{:S(2)}) collective-permute-start(bf16[152,1024]{1,0:T(8,128)(2,1)S(1)} %walk_sum.10.refs_7_), channel_id=1, source_target_pairs={{0,2},{1,3},{4,0},{5,1},{8,4},{9,5},{12,8},{13,9},{14,12},{15,13},... | collective-permute-start | bytes 933896 | tf_op jit(solution)/shard_map/ppermute | solution.py:51
  91.2 4.3 %d_w_in.1 = (f32[512,2048]{1,0:T(8,128)}, f32[8,128]{1,0:T(8,128)S(1)}) custom-call(s32[18]{0:T(128)S(1)} %dynamic-slice_bitcast_fusion.1.refs_0_, f32[1,2048]{1,0:T(1,128)S(1)} %bitcast.17, bf16[512,1024]{1,0:T(8,128)(2,1)S(1)} %get-tuple-element.131.refs_3_.refs_1_.refs_2_, f32[8,1024]{1,0:T(8,128)S(1)} %get-tuple-element.130.refs_1_.refs_3_.refs_4_, ...), custom_call_target="tpu_custom_call" | custom-call | flops 2000000000 | bytes 8000000 | tf_op jit(solution)/shard_map/d_w_in/pallas_call | solution.py:66
  101.1 1.3 %collective-permute-done.35.refs_1_ = bf16[152,512]{1,0:T(8,128)(2,1)S(1)} collective-permute-done((bf16[152,512]{1,0:T(8,128)(2,1)S(1)}, bf16[152,512]{1,0:T(8,128)(2,1)S(1)}, u32[]{:S(2)}, u32[]{:S(2)}) %collective-permute-start.35) | collective-permute-done | bytes 155680 | tf_op jit(solution)/shard_map/ppermute | solution.py:51
  102.4 2.2 %conv_backward_upper.1 = (f32[128,384]{1,0:T(8,128)S(1)}, f32[49,8,128]{2,1,0:T(8,128)S(1)}, f32[38,48,128]{2,1,0:T(8,128)S(1)}, f32[24,512]{1,0:T(8,128)S(1)}) custom-call(f32[152,1024]{1,0:T(8,128)S(1)} %messages.5.refs_0_, bf16[152,512]{1,0:T(8,128)(2,1)S(1)} %collective-permute-done.35.refs_1_, bf16[152,512]{1,0:T(8,128)(2,1)S(1)} %collective-permute-done.36.refs_2_, ...), custom_call_target="tpu_custom_call" | custom-call | flops 400000000 | bytes 2000000 | tf_op jit(solution)/shard_map/conv_backward_upper/pallas_call | solution.py:66
  104.7 4.0 %conv_backward_lower.1 = (f32[128,1024]{1,0:T(8,128)}, f32[49,128]{1,0:T(8,128)}, f32[1,128]{1,0:T(1,128)}, f32[150,128]{1,0:T(8,128)}) custom-call(f32[152,1024]{1,0:T(8,128)S(1)} %messages.5.refs_0_, bf16[152,512]{1,0:T(8,128)(2,1)S(1)} %collective-permute-done.30.refs_1_, bf16[152,512]{1,0:T(8,128)(2,1)S(1)} %collective-permute-done.34.refs_2_, ...), custom_call_target="tpu_custom_call" | custom-call | tf_op jit(solution)/shard_map/conv_backward_lower/pallas_call | solution.py:66
  (103 shorter events, 36.2 us)
Async XLA Ops:
  4.6 9.4 %collective-permute-start.1 = (bf16[128,1024]{1,0:T(8,128)(2,1)S(1)}, bf16[128,1024]{1,0:T(8,128)(2,1)S(1)}, u32[]{:S(2)}, u32[]{:S(2)}) collective-permute-start(bf16[128,1024]{1,0:T(8,128)(2,1)S(1)} %conv_forward.1.refs_3_.refs_2_.refs_0_), channel_id=1, source_target_pairs={{0,2},{1,3},{4,0},{5,1},{8,4},{9,5},{12,8},{13,9},{14,12},{15,13},... | collective-permute-start | bytes 786440 | tf_op jit(solution)/shard_map/ppermute | solution.py:51
  7.7 7.8 %collective-permute-start = (bf16[128,1024]{1,0:T(8,128)(2,1)S(1)}, bf16[128,1024]{1,0:T(8,128)(2,1)S(1)}, u32[]{:S(2)}, u32[]{:S(2)}) collective-permute-start(bf16[128,1024]{1,0:T(8,128)(2,1)S(1)} %conv_forward.1.refs_3_.refs_2_.refs_0_), channel_id=1, source_target_pairs={{0,4},{1,5},{4,8},{5,9},{8,12},{9,13},{12,14},{13,15},{14,10},{15,... | collective-permute-start | bytes 786440 | tf_op jit(solution)/shard_map/ppermute | solution.py:51
  15.4 2.7 %collective-permute-start.2 = (bf16[512,1024]{1,0:T(8,128)(2,1)S(1)}, bf16[512,1024]{1,0:T(8,128)(2,1)S(1)}, u32[]{:S(2)}, u32[]{:S(2)}) collective-permute-start(bf16[512,1024]{1,0:T(8,128)(2,1)S(1)} %get-tuple-element.91.refs_1_.refs_11_), channel_id=1, source_target_pairs={{0,1},{1,0},{2,3},{3,2},{4,5},{5,4},{6,7},{7,6},{8,9},{9,8},{10,11... | collective-permute-start | bytes 3145736 | tf_op jit(solution)/shard_map/ppermute | solution.py:51
  15.4 8.7 %collective-permute-start.3 = (bf16[128,1024]{1,0:T(8,128)(2,1)S(1)}, bf16[128,1024]{1,0:T(8,128)(2,1)S(1)}, u32[]{:S(2)}, u32[]{:S(2)}) collective-permute-start(bf16[128,1024]{1,0:T(8,128)(2,1)S(1)} %collective-permute-done.refs_4_.refs_8_), channel_id=1, source_target_pairs={{0,4},{1,5},{4,8},{5,9},{8,12},{9,13},{12,14},{13,15},{14,10},{15,... | collective-permute-start | bytes 786440 | tf_op jit(solution)/shard_map/ppermute | solution.py:51
  15.8 8.4 %collective-permute-start.4 = (bf16[128,1024]{1,0:T(8,128)(2,1)S(1)}, bf16[128,1024]{1,0:T(8,128)(2,1)S(1)}, u32[]{:S(2)}, u32[]{:S(2)}) collective-permute-start(bf16[128,1024]{1,0:T(8,128)(2,1)S(1)} %collective-permute-done.1.refs_3_.refs_1_), channel_id=1, source_target_pairs={{0,2},{1,3},{4,0},{5,1},{8,4},{9,5},{12,8},{13,9},{14,12},{15,13},... | collective-permute-start | bytes 786440 | tf_op jit(solution)/shard_map/ppermute | solution.py:51
  24.3 7.9 %collective-permute-start.5 = (bf16[128,1024]{1,0:T(8,128)(2,1)S(1)}, bf16[128,1024]{1,0:T(8,128)(2,1)S(1)}, u32[]{:S(2)}, u32[]{:S(2)}) collective-permute-start(bf16[128,1024]{1,0:T(8,128)(2,1)S(1)} %collective-permute-done.3.refs_6_.refs_7_), channel_id=1, source_target_pairs={{0,4},{1,5},{4,8},{5,9},{8,12},{9,13},{12,14},{13,15},{14,10},{15,... | collective-permute-start | bytes 786440 | tf_op jit(solution)/shard_map/ppermute | solution.py:51
  26.0 7.3 %collective-permute-start.6 = (bf16[128,1024]{1,0:T(8,128)(2,1)S(1)}, bf16[128,1024]{1,0:T(8,128)(2,1)S(1)}, u32[]{:S(2)}, u32[]{:S(2)}) collective-permute-start(bf16[128,1024]{1,0:T(8,128)(2,1)S(1)} %collective-permute-done.4.refs_5_.refs_2_), channel_id=1, source_target_pairs={{0,2},{1,3},{4,0},{5,1},{8,4},{9,5},{12,8},{13,9},{14,12},{15,13},... | collective-permute-start | bytes 786440 | tf_op jit(solution)/shard_map/ppermute | solution.py:51
  33.3 9.1 %collective-permute-start.10 = (bf16[512,1024]{1,0:T(8,128)(2,1)S(1)}, bf16[512,1024]{1,0:T(8,128)(2,1)S(1)}, u32[]{:S(2)}, u32[]{:S(2)}) collective-permute-start(bf16[512,1024]{1,0:T(8,128)(2,1)S(1)} %get-tuple-element.117), channel_id=1, source_target_pairs={{0,1},{1,0},{2,3},{3,2},{4,5},{5,4},{6,7},{7,6},{8,9},{9,8},{10,11... | collective-permute-start | bytes 3145736 | tf_op jit(solution)/shard_map/ppermute | solution.py:51
  33.3 6.5 %collective-permute-start.9 = (bf16[128,1024]{1,0:T(8,128)(2,1)S(1)}, bf16[128,1024]{1,0:T(8,128)(2,1)S(1)}, u32[]{:S(2)}, u32[]{:S(2)}) collective-permute-start(bf16[128,1024]{1,0:T(8,128)(2,1)S(1)} %collective-permute-done.5.refs_5_.refs_6_), channel_id=1, source_target_pairs={{0,1},{1,0},{2,3},{3,2},{4,5},{5,4},{6,7},{7,6},{8,9},{9,8},{10,11... | collective-permute-start | bytes 786440 | tf_op jit(solution)/shard_map/ppermute | solution.py:51
  33.8 6.0 %collective-permute-start.8 = (bf16[128,1024]{1,0:T(8,128)(2,1)S(1)}, bf16[128,1024]{1,0:T(8,128)(2,1)S(1)}, u32[]{:S(2)}, u32[]{:S(2)}) collective-permute-start(bf16[128,1024]{1,0:T(8,128)(2,1)S(1)} %collective-permute-done.6.refs_4_.refs_3_), channel_id=1, source_target_pairs={{0,1},{1,0},{2,3},{3,2},{4,5},{5,4},{6,7},{7,6},{8,9},{9,8},{10,11... | collective-permute-start | bytes 786440 | tf_op jit(solution)/shard_map/ppermute | solution.py:51
  33.8 6.0 %collective-permute-start.12 = (bf16[64,1024]{1,0:T(8,128)(2,1)S(1)}, bf16[64,1024]{1,0:T(8,128)(2,1)S(1)}, u32[]{:S(2)}, u32[]{:S(2)}) collective-permute-start(bf16[64,1024]{1,0:T(8,128)(2,1)S(1)} %slice.7), channel_id=1, source_target_pairs={{0,2},{1,3},{4,0},{5,1},{8,4},{9,5},{12,8},{13,9},{14,12},{15,13},... | collective-permute-start | bytes 393224 | tf_op jit(solution)/shard_map/ppermute | solution.py:51
  34.5 6.1 %collective-permute-start.7 = (bf16[64,1024]{1,0:T(8,128)(2,1)S(1)}, bf16[64,1024]{1,0:T(8,128)(2,1)S(1)}, u32[]{:S(2)}, u32[]{:S(2)}) collective-permute-start(bf16[64,1024]{1,0:T(8,128)(2,1)S(1)} %slice.6), channel_id=1, source_target_pairs={{0,4},{1,5},{4,8},{5,9},{8,12},{9,13},{12,14},{13,15},{14,10},{15,... | collective-permute-start | bytes 393224 | tf_op jit(solution)/shard_map/ppermute | solution.py:51
  39.8 2.6 %collective-permute-start.14 = (bf16[64,1024]{1,0:T(8,128)(2,1)S(1)}, bf16[64,1024]{1,0:T(8,128)(2,1)S(1)}, u32[]{:S(2)}, u32[]{:S(2)}) collective-permute-start(bf16[64,1024]{1,0:T(8,128)(2,1)S(1)} %collective-permute-done.12.refs_13_.refs_5_), channel_id=1, source_target_pairs={{0,1},{1,0},{2,3},{3,2},{4,5},{5,4},{6,7},{7,6},{8,9},{9,8},{10,11... | collective-permute-start | bytes 393224 | tf_op jit(solution)/shard_map/ppermute | solution.py:51
  45.8 14.6 %collective-permute-start.20 = (bf16[1024,1024]{1,0:T(8,128)(2,1)S(1)}, bf16[1024,1024]{1,0:T(8,128)(2,1)S(1)}, u32[]{:S(2)}, u32[]{:S(2)}) collective-permute-start(bf16[1024,1024]{1,0:T(8,128)(2,1)S(1)} %pack_blocks.1.refs_2_.refs_4_), channel_id=1, source_target_pairs={{0,1},{1,0},{2,3},{3,2},{4,5},{5,4},{6,7},{7,6},{8,9},{9,8},{10,11... | collective-permute-start | bytes 6291464 | tf_op jit(solution)/shard_map/ppermute | solution.py:51
  46.0 4.7 %collective-permute-start.16 = (f32[160,128]{1,0:T(8,128)S(1)}, f32[160,128]{1,0:T(8,128)S(1)}, u32[]{:S(2)}, u32[]{:S(2)}) collective-permute-start(f32[160,128]{1,0:T(8,128)S(1)} %get-tuple-element.126), channel_id=1, source_target_pairs={{0,2},{1,3},{2,0},{3,1},{4,6},{5,7},{6,4},{7,5},{8,10},{9,11},{10,... | collective-permute-start | bytes 245768 | tf_op jit(solution)/shard_map/ppermute | solution.py:51
  47.1 4.6 %collective-permute-start.17 = (f32[160,128]{1,0:T(8,128)S(1)}, f32[160,128]{1,0:T(8,128)S(1)}, u32[]{:S(2)}, u32[]{:S(2)}) collective-permute-start(f32[160,128]{1,0:T(8,128)S(1)} %get-tuple-element.127), channel_id=1, source_target_pairs={{0,4},{1,5},{2,6},{3,7},{4,0},{5,1},{6,2},{7,3},{8,12},{9,13},{10,... | collective-permute-start | bytes 245768 | tf_op jit(solution)/shard_map/ppermute | solution.py:51
  48.7 5.3 %collective-permute-start.18 = (f32[160,128]{1,0:T(8,128)S(1)}, f32[160,128]{1,0:T(8,128)S(1)}, u32[]{:S(2)}, u32[]{:S(2)}) collective-permute-start(f32[160,128]{1,0:T(8,128)S(1)} %get-tuple-element.128), channel_id=1, source_target_pairs={{0,6},{1,7},{2,4},{3,5},{4,2},{5,3},{6,0},{7,1},{8,14},{9,15},{10,... | collective-permute-start | bytes 245768 | tf_op jit(solution)/shard_map/ppermute | solution.py:51
  54.1 6.3 %collective-permute-start.19 = (f32[160,128]{1,0:T(8,128)S(1)}, f32[160,128]{1,0:T(8,128)S(1)}, u32[]{:S(2)}, u32[]{:S(2)}) collective-permute-start(f32[160,128]{1,0:T(8,128)S(1)} %fold_chips.1.refs_2_.refs_1_), channel_id=1, source_target_pairs={{0,8},{1,9},{2,10},{3,11},{4,12},{5,13},{6,14},{7,15},{8,0},{9,1},... | collective-permute-start | bytes 245768 | tf_op jit(solution)/shard_map/ppermute | solution.py:51
  60.5 5.0 %collective-permute-start.23 = (bf16[160,128]{1,0:T(8,128)(2,1)S(1)}, bf16[160,128]{1,0:T(8,128)(2,1)S(1)}, u32[]{:S(2)}, u32[]{:S(2)}) collective-permute-start(bf16[160,128]{1,0:T(8,128)(2,1)S(1)} %class_grad.1.refs_1_), channel_id=1, source_target_pairs={{0,6},{1,7},{2,4},{3,5},{4,2},{5,3},{6,0},{7,1},{8,14},{9,15},{10,... | collective-permute-start | bytes 122888 | tf_op jit(solution)/shard_map/ppermute | solution.py:51
  61.3 4.1 %collective-permute-start.22 = (bf16[160,128]{1,0:T(8,128)(2,1)S(1)}, bf16[160,128]{1,0:T(8,128)(2,1)S(1)}, u32[]{:S(2)}, u32[]{:S(2)}) collective-permute-start(bf16[160,128]{1,0:T(8,128)(2,1)S(1)} %class_grad.1.refs_1_), channel_id=1, source_target_pairs={{0,4},{1,5},{2,6},{3,7},{4,0},{5,1},{6,2},{7,3},{8,12},{9,13},{10,... | collective-permute-start | bytes 122888 | tf_op jit(solution)/shard_map/ppermute | solution.py:51
  63.0 4.0 %collective-permute-start.21 = (bf16[160,128]{1,0:T(8,128)(2,1)S(1)}, bf16[160,128]{1,0:T(8,128)(2,1)S(1)}, u32[]{:S(2)}, u32[]{:S(2)}) collective-permute-start(bf16[160,128]{1,0:T(8,128)(2,1)S(1)} %class_grad.1.refs_1_), channel_id=1, source_target_pairs={{0,2},{1,3},{2,0},{3,1},{4,6},{5,7},{6,4},{7,5},{8,10},{9,11},{10,... | collective-permute-start | bytes 122888 | tf_op jit(solution)/shard_map/ppermute | solution.py:51
  69.1 3.2 %collective-permute-start.25 = (bf16[512,1024]{1,0:T(8,128)(2,1)S(1)}, bf16[512,1024]{1,0:T(8,128)(2,1)S(1)}, u32[]{:S(2)}, u32[]{:S(2)}) collective-permute-start(bf16[512,1024]{1,0:T(8,128)(2,1)S(1)} %get-tuple-element.131.refs_3_.refs_1_.refs_2_), channel_id=1, source_target_pairs={{0,1},{1,0},{2,3},{3,2},{4,5},{5,4},{6,7},{7,6},{8,9},{9,8},{10,11... | collective-permute-start | bytes 3145736 | tf_op jit(solution)/shard_map/ppermute | solution.py:51
  72.8 8.0 %collective-permute-start.27 = (bf16[80,1024]{1,0:T(8,128)(2,1)S(1)}, bf16[80,1024]{1,0:T(8,128)(2,1)S(1)}, u32[]{:S(2)}, u32[]{:S(2)}) collective-permute-start(bf16[80,1024]{1,0:T(8,128)(2,1)S(1)} %get-tuple-element.141), channel_id=1, source_target_pairs={{0,4},{1,5},{4,8},{5,9},{8,12},{9,13},{12,14},{13,15},{14,10},{15,... | collective-permute-start | bytes 491528 | tf_op jit(solution)/shard_map/ppermute | solution.py:51
  73.2 6.0 %collective-permute-start.31 = (bf16[72,1024]{1,0:T(8,128)(2,1)S(1)}, bf16[72,1024]{1,0:T(8,128)(2,1)S(1)}, u32[]{:S(2)}, u32[]{:S(2)}) collective-permute-start(bf16[72,1024]{1,0:T(8,128)(2,1)S(1)} %get-tuple-element.146), channel_id=1, source_target_pairs={{0,2},{1,3},{4,0},{5,1},{8,4},{9,5},{12,8},{13,9},{14,12},{15,13},... | collective-permute-start | bytes 442376 | tf_op jit(solution)/shard_map/ppermute | solution.py:51
  79.2 8.7 %collective-permute-start.32 = (bf16[152,1024]{1,0:T(8,128)(2,1)S(1)}, bf16[152,1024]{1,0:T(8,128)(2,1)S(1)}, u32[]{:S(2)}, u32[]{:S(2)}) collective-permute-start(bf16[152,1024]{1,0:T(8,128)(2,1)S(1)} %walk_sum.9), channel_id=1, source_target_pairs={{0,2},{1,3},{4,0},{5,1},{8,4},{9,5},{12,8},{13,9},{14,12},{15,13},... | collective-permute-start | bytes 933896 | tf_op jit(solution)/shard_map/ppermute | solution.py:51
  80.8 8.5 %collective-permute-start.28 = (bf16[152,1024]{1,0:T(8,128)(2,1)S(1)}, bf16[152,1024]{1,0:T(8,128)(2,1)S(1)}, u32[]{:S(2)}, u32[]{:S(2)}) collective-permute-start(bf16[152,1024]{1,0:T(8,128)(2,1)S(1)} %walk_sum.6), channel_id=1, source_target_pairs={{0,4},{1,5},{4,8},{5,9},{8,12},{9,13},{12,14},{13,15},{14,10},{15,... | collective-permute-start | bytes 933896 | tf_op jit(solution)/shard_map/ppermute | solution.py:51
  88.0 7.8 %collective-permute-start.33 = (bf16[152,1024]{1,0:T(8,128)(2,1)S(1)}, bf16[152,1024]{1,0:T(8,128)(2,1)S(1)}, u32[]{:S(2)}, u32[]{:S(2)}) collective-permute-start(bf16[152,1024]{1,0:T(8,128)(2,1)S(1)} %walk_sum.10.refs_7_), channel_id=1, source_target_pairs={{0,2},{1,3},{4,0},{5,1},{8,4},{9,5},{12,8},{13,9},{14,12},{15,13},... | collective-permute-start | bytes 933896 | tf_op jit(solution)/shard_map/ppermute | solution.py:51
  89.5 7.6 %collective-permute-start.29 = (bf16[152,1024]{1,0:T(8,128)(2,1)S(1)}, bf16[152,1024]{1,0:T(8,128)(2,1)S(1)}, u32[]{:S(2)}, u32[]{:S(2)}) collective-permute-start(bf16[152,1024]{1,0:T(8,128)(2,1)S(1)} %walk_sum.7.refs_6_), channel_id=1, source_target_pairs={{0,4},{1,5},{4,8},{5,9},{8,12},{9,13},{12,14},{13,15},{14,10},{15,... | collective-permute-start | bytes 933896 | tf_op jit(solution)/shard_map/ppermute | solution.py:51
  95.8 5.3 %collective-permute-start.36 = (bf16[152,512]{1,0:T(8,128)(2,1)S(1)}, bf16[152,512]{1,0:T(8,128)(2,1)S(1)}, u32[]{:S(2)}, u32[]{:S(2)}) collective-permute-start(bf16[152,512]{1,0:T(8,128)(2,1)S(1)} %get-tuple-element.155), channel_id=1, source_target_pairs={{0,2},{1,3},{4,0},{5,1},{8,4},{9,5},{12,8},{13,9},{14,12},{15,13},... | collective-permute-start | bytes 466952 | tf_op jit(solution)/shard_map/ppermute | solution.py:51
  97.1 5.3 %collective-permute-start.35 = (bf16[152,512]{1,0:T(8,128)(2,1)S(1)}, bf16[152,512]{1,0:T(8,128)(2,1)S(1)}, u32[]{:S(2)}, u32[]{:S(2)}) collective-permute-start(bf16[152,512]{1,0:T(8,128)(2,1)S(1)} %get-tuple-element.154), channel_id=1, source_target_pairs={{0,4},{1,5},{4,8},{5,9},{8,12},{9,13},{12,14},{13,15},{14,10},{15,... | collective-permute-start | bytes 466952 | tf_op jit(solution)/shard_map/ppermute | solution.py:51
  98.1 6.6 %collective-permute-start.34 = (bf16[152,512]{1,0:T(8,128)(2,1)S(1)}, bf16[152,512]{1,0:T(8,128)(2,1)S(1)}, u32[]{:S(2)}, u32[]{:S(2)}) collective-permute-start(bf16[152,512]{1,0:T(8,128)(2,1)S(1)} %get-tuple-element.151), channel_id=1, source_target_pairs={{0,2},{1,3},{4,0},{5,1},{8,4},{9,5},{12,8},{13,9},{14,12},{15,13},... | collective-permute-start | bytes 466952 | tf_op jit(solution)/shard_map/ppermute | solution.py:51
  99.2 5.4 %collective-permute-start.30 = (bf16[152,512]{1,0:T(8,128)(2,1)S(1)}, bf16[152,512]{1,0:T(8,128)(2,1)S(1)}, u32[]{:S(2)}, u32[]{:S(2)}) collective-permute-start(bf16[152,512]{1,0:T(8,128)(2,1)S(1)} %get-tuple-element.142), channel_id=1, source_target_pairs={{0,4},{1,5},{4,8},{5,9},{8,12},{9,13},{12,14},{13,15},{14,10},{15,... | collective-permute-start | bytes 466952 | tf_op jit(solution)/shard_map/ppermute | solution.py:51
  (16 other events, 39.5 us)
